TPU v7x, 32 devices: a whole 2x2x4 slice. The times are simulated.
32 devices in a mesh: bf: 8 (over z, x), fr: 4 (over y, core).
Axes of the slice: x: 2, y: 2, z: 4, core: 2. Of those that a mesh axis runs over, the one named last changes fastest.
Arguments:
- top_source: bfloat16 [128, 4096], P('fr', 'bf'), may hold values from -6 to 6
- level_ordering: int32 [3, 8, 512], P(None, 'bf'), may hold values from 0 to 511, each once within a row
- butterfly_own: bfloat16 [3, 2048, 256], P(None, 'bf'), may hold values from -0.25 to 0.25
- butterfly_cross: bfloat16 [3, 2048, 256], P(None, 'bf'), may hold values from -0.25 to 0.25
- parent_rows: int32 [32, 256], P(('bf', 'fr')), may hold values from 0 to 511, as said below
- front_source: bfloat16 [128, 32768], P(None, ('bf', 'fr')), may hold values from -6 to 6
- panel_inverse: bfloat16 [32768, 1024], P(('bf', 'fr')), as said below
- coupling_read: bfloat16 [32768, 256], P(('bf', 'fr')), may hold values from -0.1875 to 0.1875
- coupling_write: bfloat16 [8192, 1024], P(('bf', 'fr')), may hold values from -0.25 to 0.25
Outputs:
- top_solution: bfloat16 [128, 4096], P('fr', 'bf')
- front_solution: bfloat16 [128, 32768], P(None, ('bf', 'fr'))
Inputs may be any that keep to these rules, and one draw needn't show every extreme that they name: `level_ordering`: for each level and group, a permutation of the group's 512 columns. `parent_rows`: each row holds 256 different column numbers. `panel_inverse`: each panel's block is lower triangular: zero above its diagonal.
All inputs are finite; a program needn't handle non-finite values.
Results may differ from a plain program's by a relative error of at most 0.0057.
Values may be sent and summed in bfloat16 or wider, within the bound.
No kernel may reach another device: no remote copies, remote signals or barrier semaphores. Data moves between devices by JAX's collectives and lax.ppermute only.
A program may use at most 64 MiB of HBM per device.

v0:
```python
import jax
import jax.numpy as jnp
from jax import lax
from jax.sharding import PartitionSpec as P


def swapped(value, axis, stride):
    mask = 2**stride
    pairs = [(source, source ^ mask) for source in range(lax.axis_size(axis))]
    return lax.ppermute(value, axis, pairs)


def passed_along(array, axis, by):
    devices = lax.axis_size(axis)
    pairs = [(i, i + by) for i in range(devices) if 0 <= i + by < devices]
    return lax.ppermute(array, axis, pairs)


def exact_dot(left, right):
    return jnp.dot(left, right, precision=lax.Precision.HIGHEST, preferred_element_type=jnp.float32)


def mix_level(shuffled, partner, own_factor, cross_factor):
    vector_rows = shuffled.shape[0]
    block_size = own_factor.shape[0]
    left_part = shuffled.reshape(vector_rows, -1, block_size)
    right_part = partner.reshape(vector_rows, -1, block_size)
    combined = jnp.einsum("vjr,rs->vjs", left_part, own_factor, preferred_element_type=jnp.float32)
    combined = combined + jnp.einsum(
        "vjr,rs->vjs", right_part, cross_factor, preferred_element_type=jnp.float32
    )
    return combined.astype(jnp.bfloat16).reshape(vector_rows, -1)


def solve_panel(projected, linked, source, write_float, inverse_float):
    link_rank = projected + linked.astype(jnp.float32)
    residue = source.astype(jnp.float32) - exact_dot(link_rank, write_float)
    return exact_dot(residue, inverse_float)


def body(
    top_source,
    level_ordering,
    butterfly_own,
    butterfly_cross,
    parent_rows,
    front_source,
    panel_inverse,
    coupling_read,
    coupling_write,
):
    level_count = level_ordering.shape[0]
    current = top_source
    for level_index in range(level_count):
        shuffled = jnp.take(current, level_ordering[level_index, 0], axis=1)
        partner = swapped(shuffled, "bf", level_index)
        current = mix_level(
            shuffled, partner, butterfly_own[level_index], butterfly_cross[level_index]
        )
    top_whole = lax.all_gather(current, "fr", axis=0, tiled=True)
    linked = jnp.take(top_whole, parent_rows[0], axis=1)
    my_index = lax.axis_index("fr")
    chain_length = lax.axis_size("fr")
    zero_panel = jnp.zeros(front_source.shape, jnp.float32)
    read_float = coupling_read.astype(jnp.float32)
    write_float = coupling_write.astype(jnp.float32)
    inverse_float = panel_inverse.astype(jnp.float32)

    def advance(turn_index, state_pair):
        incoming, solved = state_pair

        def compute(arriving):
            projected = exact_dot(arriving, read_float)
            return solve_panel(projected, linked, front_source, write_float, inverse_float)

        def unchanged(arriving):
            return solved

        solved = lax.cond(my_index == turn_index, compute, unchanged, incoming)
        incoming = passed_along(solved, "fr", 1)
        return (incoming, solved)

    incoming, solved = lax.fori_loop(0, chain_length - 1, advance, (zero_panel, zero_panel))

    def last_compute(arriving):
        projected = exact_dot(arriving, read_float)
        return solve_panel(projected, linked, front_source, write_float, inverse_float)

    def last_keep(arriving):
        return solved

    solved = lax.cond(my_index == chain_length - 1, last_compute, last_keep, incoming)
    return (current, solved.astype(jnp.bfloat16))


def solution(mesh):
    placed = (
        P("fr", "bf"),
        P(None, "bf", None),
        P(None, "bf", None),
        P(None, "bf", None),
        P(("bf", "fr"), None),
        P(None, ("bf", "fr")),
        P(("bf", "fr"), None),
        P(("bf", "fr"), None),
        P(("bf", "fr"), None),
    )
    return jax.shard_map(
        body,
        mesh=mesh,
        in_specs=placed,
        out_specs=(P("fr", "bf"), P(None, ("bf", "fr"))),
        check_vma=False,
    )
```

profile of v0, /device:TPU:1, one launch (start us, length us, event | category | flops | bytes accessed | tf_op | source)
XLA Modules:
  0.0 78.4 jit_solution(2747352012829024200)
XLA Ops:
  0.6 0.8 fusion.19
  1.4 0.9 %copy.36 = bf16[32,512]{0,1:T(8,128)(2,1)S(1)} copy(bf16[32,512]{1,0:T(8,128)(2,1)} %param.17) | data formatting | bytes 65536 | tf_op args[0]
  2.3 1.3 %gather_fusion.1 = bf16[512,32]{1,0:T(8,128)(2,1)S(1)} fusion(bf16[32,512]{0,1:T(8,128)(2,1)S(1)} %copy.36, s32[1024]{0:T(1024)S(1)} %pad_clamp_fusion.3), kind=kCustom, calls=%fused_computation.clone | custom fusion | bytes 67584 | tf_op jit(solution)/shard_map/jit(_take)/gather | solution.py:55
  3.7 0.1 fusion.42
  3.8 2.1 %collective-permute-start.1 = (bf16[32,512]{0,1:T(8,128)(2,1)S(1)}, bf16[32,512]{0,1:T(8,128)(2,1)S(1)}, u32[]{:S(2)}, u32[]{:S(2)}) collective-permute-start(bf16[32,512]{0,1:T(8,128)(2,1)S(1)} %fusion.42), channel_id=1, source_target_pairs={{0,4},{4,0},{8,12},{12,8},{16,20},{20,16},{24,28},{28,24},{1,5},{5... | collective-permute-start | bytes 98312 | tf_op jit(solution)/shard_map/ppermute | solution.py:10
  5.9 0.1 broadcast_select_fusion.2
  6.2 0.7 compare_select_fusion
  6.8 0.7 compare_and_fusion.3
  7.5 1.1 %fusion.11 = f32[32,2,256]{2,0,1:T(8,128)S(1)} fusion(bf16[32,2,256]{0,2,1:T(8,128)(2,1)S(1)} %bitcast.73, bf16[3,256,256]{2,1,0:T(8,128)(2,1)} %param.19), kind=kOutput, calls=%fused_computation.22 | convolution fusion | flops 8388608 | bytes 229376 | tf_op jit(solution)/shard_map/vjr,rs->vjs/dot_general | solution.py:28
  8.7 4.1 %convert_element_type.55 = f32[1024,1024]{1,0:T(8,128)} convert(bf16[1024,1024]{1,0:T(8,128)(2,1)} %param.23) | non-fusion elementwise | flops 1048576 | bytes 6291456 | tf_op jit(solution)/shard_map/convert_element_type | solution.py:67
  12.7 0.1 convert_element_type.53
  12.8 0.1 convert_element_type.54
  13.0 0.2 fusion
  13.2 0.1 copy.59
  13.3 1.3 %gather_fusion.2 = bf16[512,32]{1,0:T(8,128)(2,1)S(1)} fusion(bf16[32,512]{0,1:T(8,128)(2,1)S(1)} %bitcast.71, s32[1024]{0:T(1024)S(1)} %pad_clamp_fusion.2), kind=kCustom, calls=%fused_computation.1.clone | custom fusion | bytes 67584 | tf_op jit(solution)/shard_map/jit(_take)/gather | solution.py:55
  14.6 0.1 fusion.41
  14.8 0.1 broadcast_select_fusion.1
  14.9 1.4 %collective-permute-start.2 = (bf16[32,512]{0,1:T(8,128)(2,1)S(1)}, bf16[32,512]{0,1:T(8,128)(2,1)S(1)}, u32[]{:S(2)}, u32[]{:S(2)}) collective-permute-start(bf16[32,512]{0,1:T(8,128)(2,1)S(1)} %fusion.41), channel_id=1, source_target_pairs={{0,8},{4,12},{8,0},{12,4},{16,24},{20,28},{24,16},{28,20},{1,9},{5... | collective-permute-start | bytes 98312 | tf_op jit(solution)/shard_map/ppermute | solution.py:10
  16.3 0.2 fusion.8
  16.5 2.3 %collective-permute-done.2 = bf16[32,512]{0,1:T(8,128)(2,1)S(1)} collective-permute-done((bf16[32,512]{0,1:T(8,128)(2,1)S(1)}, bf16[32,512]{0,1:T(8,128)(2,1)S(1)}, u32[]{:S(2)}, u32[]{:S(2)}) %collective-permute-start.2) | collective-permute-done | bytes 32800 | tf_op jit(solution)/shard_map/ppermute | solution.py:10
  18.8 0.2 fusion.1
  19.0 0.1 copy.62
  19.1 1.3 %gather_fusion.3 = bf16[512,32]{1,0:T(8,128)(2,1)S(1)} fusion(bf16[32,512]{0,1:T(8,128)(2,1)S(1)} %bitcast.72, s32[1024]{0:T(1024)S(1)} %pad_clamp_fusion.1), kind=kCustom, calls=%fused_computation.2.clone | custom fusion | bytes 67584 | tf_op jit(solution)/shard_map/jit(_take)/gather | solution.py:55
  20.5 0.1 fusion.40
  20.6 0.1 broadcast_select_fusion
  20.8 2.4 %collective-permute-start.3 = (bf16[32,512]{0,1:T(8,128)(2,1)S(1)}, bf16[32,512]{0,1:T(8,128)(2,1)S(1)}, u32[]{:S(2)}, u32[]{:S(2)}) collective-permute-start(bf16[32,512]{0,1:T(8,128)(2,1)S(1)} %fusion.40), channel_id=1, source_target_pairs={{0,16},{4,20},{8,24},{12,28},{16,0},{20,4},{24,8},{28,12},{1,17},{... | collective-permute-start | bytes 98312 | tf_op jit(solution)/shard_map/ppermute | solution.py:10
  23.2 0.2 fusion.5
  23.3 4.1 %collective-permute-done.3 = bf16[32,512]{0,1:T(8,128)(2,1)S(1)} collective-permute-done((bf16[32,512]{0,1:T(8,128)(2,1)S(1)}, bf16[32,512]{0,1:T(8,128)(2,1)S(1)}, u32[]{:S(2)}, u32[]{:S(2)}) %collective-permute-start.3) | collective-permute-done | bytes 32800 | tf_op jit(solution)/shard_map/ppermute | solution.py:10
  27.4 0.2 fusion.3
  27.6 0.0 copy-start.5
  27.7 0.6 copy-done.5
  28.3 8.3 %all_gather.3 = bf16[128,512]{1,0:T(8,128)(2,1)S(1)} all-gather(bf16[32,512]{1,0:T(8,128)(2,1)S(1)} %bitcast.76), channel_id=1, replica_groups=mesh['bf'=8,'fr'=4] {'fr'}, dimensions={0}, use_global_device_ids=true | all-gather | bytes 163840 | tf_op jit(solution)/shard_map/all_gather | solution.py:60
  36.5 0.1 copy.51
  36.7 0.9 %gather_fusion = bf16[256,128]{1,0:T(8,128)(2,1)S(1)} fusion(bf16[128,512]{0,1:T(8,128)(2,1)S(1)} %copy.51, s32[1024]{0:T(1024)S(1)} %pad_clamp_fusion), kind=kCustom, calls=%fused_computation.3 | custom fusion | bytes 132096 | tf_op jit(solution)/shard_map/jit(_take)/gather | solution.py:61
  37.5 0.1 select_bitcast_fusion
  37.6 0.1 copy.52
  37.9 39.8 %while.21 = (s32[]{:T(128)}, f32[128,1024]{1,0:T(8,128)S(1)}, f32[128,1024]{1,0:T(8,128)S(1)}, s32[]{:T(128)}, bf16[128,1024]{1,0:T(8,128)(2,1)S(1)}, /*index=5*...) while((s32[]{:T(128)}, f32[128,1024]{1,0:T(8,128)S(1)}, ...), condition=%wide.region_3.5_spmd, body=%wide.region_0.4_spmd.sunk | while | flops 2416246784 | bytes 11075795 | solution.py:83
  37.9 3.2 %collective-permute-start = (f32[128,1024]{1,0:T(8,128)S(1)}, f32[128,1024]{1,0:T(8,128)S(1)}, u32[]{:S(2)}, u32[]{:S(2)}) collective-permute-start(f32[128,1024]{1,0:T(8,128)S(1)} %get-tuple-element.368), channel_id=1, source_target_pairs={{0,1},{1,2},{2,3},{4,5},{5,6},{6,7},{8,9},{9,10},{10,11},{12,13},{... | collective-permute-start | bytes 1572872 | tf_op jit(solution)/shard_map/while/body/eval_jaxpr/ppermute | solution.py:16
  41.1 6.1 %collective-permute-done = f32[128,1024]{1,0:T(8,128)S(1)} collective-permute-done((f32[128,1024]{1,0:T(8,128)S(1)}, f32[128,1024]{1,0:T(8,128)S(1)}, u32[]{:S(2)}, u32[]{:S(2)}) %collective-permute-start) | collective-permute-done | bytes 524320 | tf_op jit(solution)/shard_map/while/body/eval_jaxpr/ppermute | solution.py:16
  47.2 6.0 %conditional.4 = (f32[128,1024]{1,0:T(8,128)S(1)}) conditional(s32[]{:T(128)} %convert_element_type.67, f32[128,1024]{1,0:T(8,128)S(1)} %get-tuple-element.349, (bf16[128,1024]{1,0:T(8,128)(2,1)S(1)}, f32[128,1024]{1,0:T(8,128)S(1)}, f32[1024,256]{1,0:T(8,128)S(1)}, bf16[128,256]{1,0:T(8,128)(2,1)S(1)}, f32[256,1024]{1,0:T(8,128)S(1)}, ...), branch_computations={%region_1.2_spmd, %region_2.3_spmd} | conditional | flops 2416246784 | bytes 8978440 | solution.py:79
  47.2 0.6 convolution_add_fusion
  47.8 0.7 convolution_subtract_fusion
  48.6 4.6 %fusion.20 = f32[128,1024]{1,0:T(8,128)S(1)} fusion(f32[128,1024]{1,0:T(8,128)S(1)} %convolution_subtract_fusion, f32[1024,1024]{1,0:T(8,128)} %get-tuple-element.191), kind=kOutput, calls=%fused_computation.48 | convolution fusion | flops 1610612736 | bytes 5242880 | tf_op jit(solution)/shard_map/while/body/eval_jaxpr/cond/branch_1_fun/dot_general | solution.py:20
  53.2 1.9 %collective-permute-start = (f32[128,1024]{1,0:T(8,128)S(1)}, f32[128,1024]{1,0:T(8,128)S(1)}, u32[]{:S(2)}, u32[]{:S(2)}) collective-permute-start(f32[128,1024]{1,0:T(8,128)S(1)} %get-tuple-element.368), channel_id=1, source_target_pairs={{0,1},{1,2},{2,3},{4,5},{5,6},{6,7},{8,9},{9,10},{10,11},{12,13},{... | collective-permute-start | bytes 1572872 | tf_op jit(solution)/shard_map/while/body/eval_jaxpr/ppermute | solution.py:16
  55.1 6.1 %collective-permute-done = f32[128,1024]{1,0:T(8,128)S(1)} collective-permute-done((f32[128,1024]{1,0:T(8,128)S(1)}, f32[128,1024]{1,0:T(8,128)S(1)}, u32[]{:S(2)}, u32[]{:S(2)}) %collective-permute-start) | collective-permute-done | bytes 524320 | tf_op jit(solution)/shard_map/while/body/eval_jaxpr/ppermute | solution.py:16
  61.2 10.4 %collective-permute-start = (f32[128,1024]{1,0:T(8,128)S(1)}, f32[128,1024]{1,0:T(8,128)S(1)}, u32[]{:S(2)}, u32[]{:S(2)}) collective-permute-start(f32[128,1024]{1,0:T(8,128)S(1)} %get-tuple-element.368), channel_id=1, source_target_pairs={{0,1},{1,2},{2,3},{4,5},{5,6},{6,7},{8,9},{9,10},{10,11},{12,13},{... | collective-permute-start | bytes 1572872 | tf_op jit(solution)/shard_map/while/body/eval_jaxpr/ppermute | solution.py:16
  71.6 6.1 %collective-permute-done = f32[128,1024]{1,0:T(8,128)S(1)} collective-permute-done((f32[128,1024]{1,0:T(8,128)S(1)}, f32[128,1024]{1,0:T(8,128)S(1)}, u32[]{:S(2)}, u32[]{:S(2)}) %collective-permute-start) | collective-permute-done | bytes 524320 | tf_op jit(solution)/shard_map/while/body/eval_jaxpr/ppermute | solution.py:16
  77.7 0.7 convert_element_type.56
  (27 shorter events, 0.2 us)
Async XLA Ops:
  0.6 12.1 %copy-start.1 = (bf16[1024,256]{1,0:T(8,128)(2,1)S(1)}, bf16[1024,256]{1,0:T(8,128)(2,1)}, u32[]{:S(2)}) copy-start(bf16[1024,256]{1,0:T(8,128)(2,1)} %param.24) | copy-start | bytes 1572868
  3.8 9.0 %copy-start.2 = (bf16[256,1024]{1,0:T(8,128)(2,1)S(1)}, bf16[256,1024]{1,0:T(8,128)(2,1)}, u32[]{:S(2)}) copy-start(bf16[256,1024]{1,0:T(8,128)(2,1)} %param.25) | copy-start | bytes 1572868
  3.8 9.1 %collective-permute-start.1 = (bf16[32,512]{0,1:T(8,128)(2,1)S(1)}, bf16[32,512]{0,1:T(8,128)(2,1)S(1)}, u32[]{:S(2)}, u32[]{:S(2)}) collective-permute-start(bf16[32,512]{0,1:T(8,128)(2,1)S(1)} %fusion.42), channel_id=1, source_target_pairs={{0,4},{4,0},{8,12},{12,8},{16,20},{20,16},{24,28},{28,24},{1,5},{5... | collective-permute-start | bytes 98312 | tf_op jit(solution)/shard_map/ppermute | solution.py:10
  8.6 4.3 %copy-start.4 = (bf16[3,256,256]{2,1,0:T(8,128)(2,1)S(1)}, bf16[3,256,256]{2,1,0:T(8,128)(2,1)}, u32[]{:S(2)}) copy-start(bf16[3,256,256]{2,1,0:T(8,128)(2,1)} %param.20) | copy-start | bytes 1179652
  8.6 7.7 %copy-start.3 = (bf16[3,256,256]{2,1,0:T(8,128)(2,1)S(1)}, bf16[3,256,256]{2,1,0:T(8,128)(2,1)}, u32[]{:S(2)}) copy-start(bf16[3,256,256]{2,1,0:T(8,128)(2,1)} %param.19) | copy-start | bytes 1179652
  12.8 25.0 %copy-start = (bf16[128,1024]{1,0:T(8,128)(2,1)S(1)}, bf16[128,1024]{1,0:T(8,128)(2,1)}, u32[]{:S(2)}) copy-start(bf16[128,1024]{1,0:T(8,128)(2,1)} %param.22) | copy-start | bytes 786436
  14.9 3.9 %collective-permute-start.2 = (bf16[32,512]{0,1:T(8,128)(2,1)S(1)}, bf16[32,512]{0,1:T(8,128)(2,1)S(1)}, u32[]{:S(2)}, u32[]{:S(2)}) collective-permute-start(bf16[32,512]{0,1:T(8,128)(2,1)S(1)} %fusion.41), channel_id=1, source_target_pairs={{0,8},{4,12},{8,0},{12,4},{16,24},{20,28},{24,16},{28,20},{1,9},{5... | collective-permute-start | bytes 98312 | tf_op jit(solution)/shard_map/ppermute | solution.py:10
  20.8 6.7 %collective-permute-start.3 = (bf16[32,512]{0,1:T(8,128)(2,1)S(1)}, bf16[32,512]{0,1:T(8,128)(2,1)S(1)}, u32[]{:S(2)}, u32[]{:S(2)}) collective-permute-start(bf16[32,512]{0,1:T(8,128)(2,1)S(1)} %fusion.40), channel_id=1, source_target_pairs={{0,16},{4,20},{8,24},{12,28},{16,0},{20,4},{24,8},{28,12},{1,17},{... | collective-permute-start | bytes 98312 | tf_op jit(solution)/shard_map/ppermute | solution.py:10
  27.6 0.6 copy-start.5
  37.9 9.3 %collective-permute-start = (f32[128,1024]{1,0:T(8,128)S(1)}, f32[128,1024]{1,0:T(8,128)S(1)}, u32[]{:S(2)}, u32[]{:S(2)}) collective-permute-start(f32[128,1024]{1,0:T(8,128)S(1)} %get-tuple-element.368), channel_id=1, source_target_pairs={{0,1},{1,2},{2,3},{4,5},{5,6},{6,7},{8,9},{9,10},{10,11},{12,13},{... | collective-permute-start | bytes 1572872 | tf_op jit(solution)/shard_map/while/body/eval_jaxpr/ppermute | solution.py:16
  53.2 8.0 %collective-permute-start = (f32[128,1024]{1,0:T(8,128)S(1)}, f32[128,1024]{1,0:T(8,128)S(1)}, u32[]{:S(2)}, u32[]{:S(2)}) collective-permute-start(f32[128,1024]{1,0:T(8,128)S(1)} %get-tuple-element.368), channel_id=1, source_target_pairs={{0,1},{1,2},{2,3},{4,5},{5,6},{6,7},{8,9},{9,10},{10,11},{12,13},{... | collective-permute-start | bytes 1572872 | tf_op jit(solution)/shard_map/while/body/eval_jaxpr/ppermute | solution.py:16
  61.2 16.5 %collective-permute-start = (f32[128,1024]{1,0:T(8,128)S(1)}, f32[128,1024]{1,0:T(8,128)S(1)}, u32[]{:S(2)}, u32[]{:S(2)}) collective-permute-start(f32[128,1024]{1,0:T(8,128)S(1)} %get-tuple-element.368), channel_id=1, source_target_pairs={{0,1},{1,2},{2,3},{4,5},{5,6},{6,7},{8,9},{9,10},{10,11},{12,13},{... | collective-permute-start | bytes 1572872 | tf_op jit(solution)/shard_map/while/body/eval_jaxpr/ppermute | solution.py:16
where the time goes:
time: 78.8 us; the launch traced here: 78.4 us
  waiting for transfers between devices  24.7 us (31%)
  starting transfers between devices  21.3 us (27%)
  blocking collectives  8.27 us (10%)
  matrix products  7.97 us (10%)
  local copies, waits for them, and re-layouts  7.75 us (10%)
  other arithmetic  7.34 us (9%)
  between operations  0.94 us (1%)
    ppermute x3, waiting for transfers between devices, passed_along(): return lax.ppermute(array, axis, pairs)  18.3 us
    ppermute x3, starting transfers between devices, passed_along(): return lax.ppermute(array, axis, pairs)  15.5 us
    all_gather x1, blocking collectives, body(): top_whole = lax.all_gather(current, 'fr', axis=0, tiled=True)  8.27 us
    ppermute x3, waiting for transfers between devices, swapped(): return lax.ppermute(value, axis, pairs)  6.43 us
    dot_general x3, matrix products, exact_dot(): jnp.dot(left, right, precision=lax.Precision.HIGHEST, preferred_element_t...  5.94 us
    ppermute x3, starting transfers between devices, swapped(): return lax.ppermute(value, axis, pairs)  5.84 us
    convert_element_type x1, other arithmetic, body(): inverse_float = panel_inverse.astype(jnp.float32)  4.08 us
    gather x3, local copies, waits for them, and re-layouts, body(): shuffled = jnp.take(current, level_ordering[level_index, 0], axis=1)  4.02 us
  transfers between devices with their start and end apart: 6, of which 5 were waited for; matrix products, arithmetic and copies ran while one was open for 9% of the time, Pallas kernels for 0%

commit v1 on v0

v1 whole, which is shorter than its diff:
```python
import jax
import jax.numpy as jnp
from jax import lax
from jax.sharding import PartitionSpec as P

BF16 = jnp.bfloat16


def dot(left, right):
    return jnp.dot(left, right, preferred_element_type=jnp.float32)


def swapped(value, axis, stride):
    mask = 2**stride
    pairs = [(source, source ^ mask) for source in range(lax.axis_size(axis))]
    return lax.ppermute(value, axis, pairs)


def moved(array, axis, by):
    devices = lax.axis_size(axis)
    pairs = [(i, i + by) for i in range(devices) if 0 <= i + by < devices]
    return lax.ppermute(array, axis, pairs)


def picker(columns, size):
    rows = lax.broadcasted_iota(jnp.int32, (size, columns.shape[0]), 0)
    return (rows == columns[None, :]).astype(BF16)


def doubled(factor, blocks):
    zero = jnp.zeros_like(factor)
    return jnp.concatenate(
        [
            jnp.concatenate([factor if i == j else zero for j in range(blocks)], axis=1)
            for i in range(blocks)
        ],
        axis=0,
    )


def body(
    top_source,
    level_ordering,
    butterfly_own,
    butterfly_cross,
    parent_rows,
    front_source,
    panel_inverse,
    coupling_read,
    coupling_write,
):
    level_count = level_ordering.shape[0]
    top_rows = top_source.shape[1]
    block_size = butterfly_own.shape[1]
    blocks = top_rows // block_size
    chain_length = lax.axis_size("fr")
    vectors = front_source.shape[0]
    rank = coupling_write.shape[0]

    next_read = moved(coupling_read, "fr", -1)

    pickers = [picker(level_ordering[level, 0], top_rows) for level in range(level_count)]

    def shuffled_factor(factor, level):
        if level + 1 == level_count:
            return doubled(factor, blocks)
        pieces = pickers[level + 1].reshape(blocks, block_size, top_rows)
        return jnp.concatenate(
            [dot(factor, pieces[j]).astype(BF16) for j in range(blocks)], axis=0
        )

    own = [shuffled_factor(butterfly_own[level], level) for level in range(level_count)]
    cross = [shuffled_factor(butterfly_cross[level], level) for level in range(level_count)]

    write_inverse = dot(coupling_write, panel_inverse).astype(BF16)
    source_inverse = dot(front_source, panel_inverse)

    shuffled = dot(top_source, pickers[0]).astype(BF16)
    for level in range(level_count):
        partner = swapped(shuffled, "bf", level)
        shuffled = (dot(shuffled, own[level]) + dot(partner, cross[level])).astype(BF16)
    top = shuffled

    carry = jnp.concatenate(
        [
            dot(source_inverse.astype(BF16), next_read).astype(BF16),
            dot(write_inverse, next_read).astype(BF16),
            jnp.broadcast_to((parent_rows // rank).astype(BF16), (8, rank)),
            jnp.broadcast_to((parent_rows % rank).astype(BF16), (8, rank)),
        ],
        axis=0,
    )
    state = jnp.zeros((vectors + top_rows, rank), jnp.float32)
    pad = jnp.zeros((vectors, rank), BF16)
    for distance in range(chain_length - 1, 0, -1):
        block = moved(carry, "fr", distance)
        base = block[:vectors].astype(jnp.float32)
        step = block[vectors : vectors + rank]
        high = block[vectors + rank].astype(jnp.int32)
        low = block[vectors + rank + 8].astype(jnp.int32)
        picks = picker(high * rank + low, top_rows)
        link = (state + jnp.concatenate([pad, picks], axis=0)).astype(BF16)
        mixed = dot(link, step)
        state = jnp.concatenate([base - mixed[:vectors], -mixed[vectors:]], axis=0)
    link = state + jnp.concatenate([pad, picker(parent_rows[0], top_rows)], axis=0)
    link = link.astype(BF16)
    fixed = source_inverse - dot(link[:vectors], write_inverse)
    reach = link[vectors:]

    rows = top.shape[0]
    place = lax.axis_index("fr")
    order = [(0, top)]
    for shift in range(1, chain_length):
        pairs = [(i, (i + shift) % chain_length) for i in range(chain_length)]
        order.append((shift, lax.ppermute(top, "fr", pairs)))
    whole = jnp.zeros((vectors, top_rows), BF16)
    for shift, piece in order:
        owner = lax.rem(place + chain_length - shift, chain_length)
        whole = lax.dynamic_update_slice(whole, piece, (owner * rows, 0))
    linked = dot(whole, reach).astype(BF16)
    solved = fixed - dot(linked, write_inverse)
    return (top, solved.astype(BF16))


def solution(mesh):
    placed = (
        P("fr", "bf"),
        P(None, "bf", None),
        P(None, "bf", None),
        P(None, "bf", None),
        P(("bf", "fr"), None),
        P(None, ("bf", "fr")),
        P(("bf", "fr"), None),
        P(("bf", "fr"), None),
        P(("bf", "fr"), None),
    )
    return jax.shard_map(
        body,
        mesh=mesh,
        in_specs=placed,
        out_specs=(P("fr", "bf"), P(None, ("bf", "fr"))),
        check_vma=False,
    )
```

time: 78.8 us -> 56 us (0.71)
  the two profiles are of different devices: /device:TPU:1 before, /device:TPU:0 now
where the time goes in v1:
time: 56 us; the launch traced here: 55.4 us
  matrix products  25.3 us (45%)
  starting transfers between devices  17.9 us (32%)
  waiting for transfers between devices  8.39 us (15%)
  local copies, waits for them, and re-layouts  1.9 us (3%)
  between operations  1.01 us (2%)
  other arithmetic  0.88 us (2%)
    dot_general x24, matrix products, dot(): return jnp.dot(left, right, preferred_element_type=jnp.float32)  25.3 us
    ppermute x3, starting transfers between devices, swapped(): return lax.ppermute(value, axis, pairs)  7.24 us
    ppermute x4, starting transfers between devices, moved(): return lax.ppermute(array, axis, pairs)  7.14 us
    ppermute x4, waiting for transfers between devices, moved(): return lax.ppermute(array, axis, pairs)  4.68 us
    ppermute x3, waiting for transfers between devices, swapped(): return lax.ppermute(value, axis, pairs)  3.7 us
    ppermute x3, starting transfers between devices, body(): order.append((shift, lax.ppermute(top, 'fr', pairs)))  3.54 us
  transfers between devices with their start and end apart: 10, of which 4 were waited for; matrix products, arithmetic and copies ran while one was open for 38% of the time, Pallas kernels for 0%

profile of v1, /device:TPU:0, one launch (start us, length us, event | category | flops | bytes accessed | tf_op | source)
XLA Modules:
  0.0 55.4 jit_solution(9023455097195281566)
XLA Ops:
  0.6 0.0 copy-start
  0.7 0.9 %fusion.103 = (s32[1,1,512]{2,1,0:T(1,128)S(1)}, s32[1,1,512]{2,1,0:T(1,128)S(1)}, s32[1,1,512]{2,1,0:T(1,128)S(1)}) fusion(s32[3,1,512]{2,1,0:T(1,128)} %param.10), kind=kLoop, calls=%fused_computation.158 | loop fusion | bytes 12288 | tf_op jit(solution)/shard_map/slice | solution.py:62
  1.6 1.7 %convolution_convert_fusion.12 = bf16[512,32]{0,1:T(8,128)(2,1)} fusion(bf16[32,512]{1,0:T(8,128)(2,1)} %param.9, s32[512]{0:T(512)S(1)} %bitcast.71), kind=kOutput, calls=%fused_computation.26 | convolution fusion | flops 17055744 | bytes 67584 | tf_op jit(solution)/shard_map/dot_general | solution.py:10
  3.2 2.9 %collective-permute-start = (bf16[32,512]{1,0:T(8,128)(2,1)}, bf16[32,512]{1,0:T(8,128)(2,1)}, u32[]{:S(2)}, u32[]{:S(2)}) collective-permute-start(bf16[32,512]{1,0:T(8,128)(2,1)} %bitcast.5), channel_id=1, source_target_pairs={{0,4},{4,0},{8,12},{12,8},{16,20},{20,16},{24,28},{28,24},{1,5},{5... | collective-permute-start | bytes 98312 | tf_op jit(solution)/shard_map/ppermute | solution.py:16
  6.1 1.3 %collective-permute-start.3 = (bf16[1024,256]{1,0:T(8,128)(2,1)}, bf16[1024,256]{1,0:T(8,128)(2,1)}, u32[]{:S(2)}, u32[]{:S(2)}) collective-permute-start(bf16[1024,256]{1,0:T(8,128)(2,1)} %param.16), channel_id=1, source_target_pairs={{1,0},{2,1},{3,2},{5,4},{6,5},{7,6},{9,8},{10,9},{11,10},{13,12},{... | collective-permute-start | bytes 1572872 | tf_op jit(solution)/shard_map/ppermute | solution.py:22
  7.4 0.2 iota_compare_fusion.3
  7.6 1.2 %fusion.1 = bf16[256,512]{0,1:T(8,128)(2,1)S(1)} fusion(pred[512,512]{1,0:T(32,128)(4,1)S(1)} %iota_compare_fusion.3, bf16[3,256,256]{2,1,0:T(8,128)(2,1)} %param.11), kind=kOutput, calls=%fused_computation.12 | convolution fusion | flops 67371008 | bytes 524288 | tf_op jit(solution)/shard_map/dot_general | solution.py:10
  8.8 1.2 %fusion.2 = bf16[256,512]{0,1:T(8,128)(2,1)S(1)} fusion(pred[512,512]{1,0:T(32,128)(4,1)S(1)} %iota_compare_fusion.3, bf16[3,256,256]{2,1,0:T(8,128)(2,1)} %param.11), kind=kOutput, calls=%fused_computation.13 | convolution fusion | flops 67371008 | bytes 524288 | tf_op jit(solution)/shard_map/dot_general | solution.py:10
  10.0 1.9 %fusion.3 = bf16[256,512]{0,1:T(8,128)(2,1)} fusion(pred[512,512]{1,0:T(32,128)(4,1)S(1)} %iota_compare_fusion.3, bf16[3,256,256]{2,1,0:T(8,128)(2,1)} %param.12), kind=kOutput, calls=%fused_computation.14 | convolution fusion | flops 67371008 | bytes 524288 | tf_op jit(solution)/shard_map/dot_general | solution.py:10
  12.0 1.0 %fusion.4 = bf16[256,512]{0,1:T(8,128)(2,1)} fusion(pred[512,512]{1,0:T(32,128)(4,1)S(1)} %iota_compare_fusion.3, bf16[3,256,256]{2,1,0:T(8,128)(2,1)S(1)} %copy-done.5), kind=kOutput, calls=%fused_computation.15 | convolution fusion | flops 67371008 | bytes 524288 | tf_op jit(solution)/shard_map/dot_general | solution.py:10
  13.0 0.2 iota_compare_fusion.2
  13.2 1.0 %fusion.5 = bf16[256,512]{0,1:T(8,128)(2,1)} fusion(pred[512,512]{1,0:T(32,128)(4,1)S(1)} %iota_compare_fusion.2, bf16[3,256,256]{2,1,0:T(8,128)(2,1)S(1)} %copy-done.4), kind=kOutput, calls=%fused_computation.16 | convolution fusion | flops 67371008 | bytes 524288 | tf_op jit(solution)/shard_map/dot_general | solution.py:10
  14.2 1.0 %fusion.6 = bf16[256,512]{0,1:T(8,128)(2,1)} fusion(pred[512,512]{1,0:T(32,128)(4,1)S(1)} %iota_compare_fusion.2, bf16[3,256,256]{2,1,0:T(8,128)(2,1)S(1)} %copy-done.4), kind=kOutput, calls=%fused_computation.17 | convolution fusion | flops 67371008 | bytes 524288 | tf_op jit(solution)/shard_map/dot_general | solution.py:10
  15.2 1.0 %fusion.7 = bf16[256,512]{0,1:T(8,128)(2,1)} fusion(pred[512,512]{1,0:T(32,128)(4,1)S(1)} %iota_compare_fusion.2, bf16[3,256,256]{2,1,0:T(8,128)(2,1)S(1)} %copy-done.5), kind=kOutput, calls=%fused_computation.18 | convolution fusion | flops 67371008 | bytes 524288 | tf_op jit(solution)/shard_map/dot_general | solution.py:10
  16.2 1.0 %fusion.8 = bf16[256,512]{0,1:T(8,128)(2,1)} fusion(pred[512,512]{1,0:T(32,128)(4,1)S(1)} %iota_compare_fusion.2, bf16[3,256,256]{2,1,0:T(8,128)(2,1)S(1)} %copy-done.5), kind=kOutput, calls=%fused_computation.19 | convolution fusion | flops 67371008 | bytes 524288 | tf_op jit(solution)/shard_map/dot_general | solution.py:10
  17.3 0.7 %convolution_convert_fusion = bf16[256,1024]{1,0:T(8,128)(2,1)S(1)} fusion(bf16[256,1024]{1,0:T(8,128)(2,1)S(1)} %copy-done.7, bf16[1024,1024]{1,0:T(8,128)(2,1)S(1)} %copy-done), kind=kOutput, calls=%fused_computation | convolution fusion | flops 537133056 | bytes 3145728 | tf_op jit(solution)/shard_map/dot_general | solution.py:10
  18.0 0.2 copy-done.3
  18.2 0.4 fusion.104
  18.7 0.2 copy-done.6
  18.9 0.1 iota_compare_fusion.6
  19.0 1.6 %fusion.29 = f32[32,512]{1,0:T(8,128)} fusion(bf16[512,32]{0,1:T(8,128)(2,1)} %convolution_convert_fusion.12, bf16[256,512]{0,1:T(8,128)(2,1)S(1)} %fusion.2, bf16[256,512]{0,1:T(8,128)(2,1)S(1)} %fusion.1), kind=kOutput, calls=%fused_computation.58 | convolution fusion | flops 17825792 | bytes 622592 | tf_op jit(solution)/shard_map/dot_general | solution.py:10
  20.6 1.3 %fusion.9 = bf16[32,512]{1,0:T(8,128)(2,1)S(1)} fusion(f32[32,512]{1,0:T(8,128)} %fusion.29, bf16[32,512]{1,0:T(8,128)(2,1)} %collective-permute-done, bf16[256,512]{0,1:T(8,128)(2,1)} %fusion.4, bf16[256,512]{0,1:T(8,128)(2,1)} %fusion.3), kind=kOutput, calls=%fused_computation.27 | convolution fusion | flops 17858560 | bytes 655360 | tf_op jit(solution)/shard_map/dot_general | solution.py:10
  21.9 1.6 %collective-permute-start.1 = (bf16[32,512]{1,0:T(8,128)(2,1)S(1)}, bf16[32,512]{1,0:T(8,128)(2,1)S(1)}, u32[]{:S(2)}, u32[]{:S(2)}) collective-permute-start(bf16[32,512]{1,0:T(8,128)(2,1)S(1)} %fusion.9), channel_id=1, source_target_pairs={{0,8},{4,12},{8,0},{12,4},{16,24},{20,28},{24,16},{28,20},{1,9},{5... | collective-permute-start | bytes 98312 | tf_op jit(solution)/shard_map/ppermute | solution.py:16
  23.6 1.3 %fusion.36 = f32[32,512]{1,0:T(8,128)S(1)} fusion(bf16[32,512]{1,0:T(8,128)(2,1)S(1)} %fusion.9, bf16[256,512]{0,1:T(8,128)(2,1)} %fusion.6, bf16[256,512]{0,1:T(8,128)(2,1)} %fusion.5), kind=kOutput, calls=%fused_computation.65 | convolution fusion | flops 17825792 | bytes 622592 | tf_op jit(solution)/shard_map/dot_general | solution.py:10
  24.8 1.3 %collective-permute-done.1 = bf16[32,512]{1,0:T(8,128)(2,1)S(1)} collective-permute-done((bf16[32,512]{1,0:T(8,128)(2,1)S(1)}, bf16[32,512]{1,0:T(8,128)(2,1)S(1)}, u32[]{:S(2)}, u32[]{:S(2)}) %collective-permute-start.1) | collective-permute-done | bytes 32800 | tf_op jit(solution)/shard_map/ppermute | solution.py:16
  26.1 1.3 %fusion.10 = bf16[32,512]{1,0:T(8,128)(2,1)S(1)} fusion(f32[32,512]{1,0:T(8,128)S(1)} %fusion.36, bf16[32,512]{1,0:T(8,128)(2,1)S(1)} %collective-permute-done.1, bf16[256,512]{0,1:T(8,128)(2,1)} %fusion.8, bf16[256,512]{0,1:T(8,128)(2,1)} %fusion.7), kind=kOutput, calls=%fused_computation.28 | convolution fusion | flops 17858560 | bytes 655360 | tf_op jit(solution)/shard_map/dot_general | solution.py:10
  27.4 2.7 %collective-permute-start.2 = (bf16[32,512]{1,0:T(8,128)(2,1)S(1)}, bf16[32,512]{1,0:T(8,128)(2,1)S(1)}, u32[]{:S(2)}, u32[]{:S(2)}) collective-permute-start(bf16[32,512]{1,0:T(8,128)(2,1)S(1)} %fusion.10), channel_id=1, source_target_pairs={{0,16},{4,20},{8,24},{12,28},{16,0},{20,4},{24,8},{28,12},{1,17},{... | collective-permute-start | bytes 98312 | tf_op jit(solution)/shard_map/ppermute | solution.py:16
  30.1 0.1 fusion.44
  30.2 2.4 %collective-permute-done.2 = bf16[32,512]{1,0:T(8,128)(2,1)S(1)} collective-permute-done((bf16[32,512]{1,0:T(8,128)(2,1)S(1)}, bf16[32,512]{1,0:T(8,128)(2,1)S(1)}, u32[]{:S(2)}, u32[]{:S(2)}) %collective-permute-start.2) | collective-permute-done | bytes 32800 | tf_op jit(solution)/shard_map/ppermute | solution.py:16
  32.6 0.8 %constant_dynamic-update-slice_fusion.3 = (bf16[128,512]{1,0:T(8,128)(2,1)S(1)}, bf16[32,512]{1,0:T(8,128)(2,1)}) fusion(bf16[128,512]{1,0:T(8,128)(2,1)S(1)} %broadcast_in_dim.25, s32[]{:T(128)S(6)} %select_n.26, f32[32,512]{1,0:T(8,128)S(1)} %fusion.44, bf16[32,512]{1,0:T(8,128)(2,1)S(1)} %collective-permute-done.2, ...), kind=kOutput, calls=%fused_computation.137 | convolution fusion | flops 18907136 | bytes 294916 | tf_op jit(solution)/shard_map/dot_general | solution.py:10
  33.5 2.1 %collective-permute-start.8 = (bf16[32,512]{1,0:T(8,128)(2,1)}, bf16[32,512]{1,0:T(8,128)(2,1)S(1)}, u32[]{:S(2)}, u32[]{:S(2)}) collective-permute-start(bf16[32,512]{1,0:T(8,128)(2,1)} %get-tuple-element.8), channel_id=1, source_target_pairs={{0,2},{1,3},{2,0},{3,1},{4,6},{5,7},{6,4},{7,5},{8,10},{9,11},{10,... | collective-permute-start | bytes 98312 | tf_op jit(solution)/shard_map/ppermute | solution.py:115
  35.6 1.5 %collective-permute-start.9 = (bf16[32,512]{1,0:T(8,128)(2,1)}, bf16[32,512]{1,0:T(8,128)(2,1)S(1)}, u32[]{:S(2)}, u32[]{:S(2)}) collective-permute-start(bf16[32,512]{1,0:T(8,128)(2,1)} %get-tuple-element.8), channel_id=1, source_target_pairs={{0,3},{1,0},{2,1},{3,2},{4,7},{5,4},{6,5},{7,6},{8,11},{9,8},{10,9... | collective-permute-start | bytes 98312 | tf_op jit(solution)/shard_map/ppermute | solution.py:115
  37.0 1.3 %convolution_convert_fusion.9 = bf16[256,256]{1,0:T(8,128)(2,1)S(1)} fusion(bf16[256,1024]{1,0:T(8,128)(2,1)S(1)} %convolution_convert_fusion, bf16[1024,256]{1,0:T(8,128)(2,1)} %collective-permute-done.3), kind=kOutput, calls=%fused_computation.20 | convolution fusion | flops 134283264 | bytes 1179648 | tf_op jit(solution)/shard_map/dot_general | solution.py:10
  38.4 1.3 %convolution_convert_fusion.11 = bf16[128,256]{1,0:T(8,128)(2,1)S(1)} fusion(bf16[1024,256]{1,0:T(8,128)(2,1)} %collective-permute-done.3, f32[128,1024]{1,0:T(8,128)S(1)} %fusion.104), kind=kOutput, calls=%fused_computation.22 | convolution fusion | flops 67272704 | bytes 1114112 | tf_op jit(solution)/shard_map/dot_general | solution.py:10
  39.7 1.9 %collective-permute-start.6 = (bf16[400,256]{1,0:T(8,128)(2,1)S(1)}, bf16[400,256]{1,0:T(8,128)(2,1)S(1)}, u32[]{:S(2)}, u32[]{:S(2)}) collective-permute-start(bf16[400,256]{1,0:T(8,128)(2,1)S(1)} %pad_maximum_fusion.1), channel_id=1, source_target_pairs={{0,3},{4,7},{8,11},{12,15},{16,19},{20,23},{24,27},{28,31}} | collective-permute-start | bytes 614408 | tf_op jit(solution)/shard_map/ppermute | solution.py:22
  41.7 2.6 %collective-permute-start.5 = (bf16[400,256]{1,0:T(8,128)(2,1)S(1)}, bf16[400,256]{1,0:T(8,128)(2,1)S(1)}, u32[]{:S(2)}, u32[]{:S(2)}) collective-permute-start(bf16[400,256]{1,0:T(8,128)(2,1)S(1)} %pad_maximum_fusion.1), channel_id=1, source_target_pairs={{0,2},{1,3},{4,6},{5,7},{8,10},{9,11},{12,14},{13,15},{16,18},{17,... | collective-permute-start | bytes 614408 | tf_op jit(solution)/shard_map/ppermute | solution.py:22
  44.3 1.3 %collective-permute-start.4 = (bf16[400,256]{1,0:T(8,128)(2,1)S(1)}, bf16[400,256]{1,0:T(8,128)(2,1)S(1)}, u32[]{:S(2)}, u32[]{:S(2)}) collective-permute-start(bf16[400,256]{1,0:T(8,128)(2,1)S(1)} %pad_maximum_fusion.1), channel_id=1, source_target_pairs={{0,1},{1,2},{2,3},{4,5},{5,6},{6,7},{8,9},{9,10},{10,11},{12,13},{... | collective-permute-start | bytes 614408 | tf_op jit(solution)/shard_map/ppermute | solution.py:22
  45.7 0.7 %collective-permute-done.6 = bf16[400,256]{1,0:T(8,128)(2,1)S(1)} collective-permute-done((bf16[400,256]{1,0:T(8,128)(2,1)S(1)}, bf16[400,256]{1,0:T(8,128)(2,1)S(1)}, u32[]{:S(2)}, u32[]{:S(2)}) %collective-permute-start.6) | collective-permute-done | bytes 204832 | tf_op jit(solution)/shard_map/ppermute | solution.py:22
  46.4 0.1 iota_compare_fusion.9
  46.4 0.3 fusion.18
  46.7 4.0 %collective-permute-done.5 = bf16[400,256]{1,0:T(8,128)(2,1)S(1)} collective-permute-done((bf16[400,256]{1,0:T(8,128)(2,1)S(1)}, bf16[400,256]{1,0:T(8,128)(2,1)S(1)}, u32[]{:S(2)}, u32[]{:S(2)}) %collective-permute-start.5) | collective-permute-done | bytes 204832 | tf_op jit(solution)/shard_map/ppermute | solution.py:22
  50.7 0.1 iota_compare_fusion.8
  50.9 0.3 fusion.48
  51.2 0.1 iota_compare_fusion.7
  51.3 0.3 fusion.46
  51.6 0.5 copy-done.2
  52.2 1.0 %convolution_subtract_fusion.1 = f32[128,1024]{1,0:T(8,128)} fusion(f32[128,1024]{1,0:T(8,128)S(1)} %copy-done.2, bf16[256,1024]{1,0:T(8,128)(2,1)S(1)} %convolution_convert_fusion, f32[512,256]{1,0:T(8,128)S(1)} %slice_negate_fusion, f32[128,256]{1,0:T(8,128)S(1)} %slice_subtract_fusion, pred[512,256]{1,0:T(32,128)(4,1)S(1)} %iota_compare_fusion.6), kind=kOutput, calls=%fused_computation.2 | convolution fusion | flops 67403776 | bytes 2359296 | tf_op jit(solution)/shard_map/dot_general | solution.py:10
  53.2 2.2 %fusion = bf16[128,1024]{1,0:T(8,128)(2,1)} fusion(f32[128,1024]{1,0:T(8,128)} %convolution_subtract_fusion.1, bf16[256,1024]{1,0:T(8,128)(2,1)S(1)} %convolution_convert_fusion, bf16[128,512]{1,0:T(8,128)(2,1)S(1)} %constant_dynamic-update-slice_fusion, f32[512,256]{1,0:T(8,128)S(1)} %slice_negate_fusion, f32[128,256]{1,0:T(8,128)S(1)} %slice_subtract_fusion, ...), kind=kOutput, calls=%fused_computation.11 | convolution fusion | flops 101613568 | bytes 2228224 | tf_op jit(solution)/shard_map/dot_general | solution.py:10
  (38 shorter events, 0.3 us)
Async XLA Ops:
  0.6 16.7 %copy-start = (bf16[1024,1024]{1,0:T(8,128)(2,1)S(1)}, bf16[1024,1024]{1,0:T(8,128)(2,1)}, u32[]{:S(2)}) copy-start(bf16[1024,1024]{1,0:T(8,128)(2,1)} %param.15) | copy-start | bytes 6291460
  0.6 12.5 %copy-start.4 = (bf16[3,256,256]{2,1,0:T(8,128)(2,1)S(1)}, bf16[3,256,256]{2,1,0:T(8,128)(2,1)}, u32[]{:S(2)}) copy-start(bf16[3,256,256]{2,1,0:T(8,128)(2,1)} %param.11) | copy-start | bytes 1179652
  0.7 11.3 %copy-start.5 = (bf16[3,256,256]{2,1,0:T(8,128)(2,1)S(1)}, bf16[3,256,256]{2,1,0:T(8,128)(2,1)}, u32[]{:S(2)}) copy-start(bf16[3,256,256]{2,1,0:T(8,128)(2,1)} %param.12) | copy-start | bytes 1179652
  3.2 17.4 %collective-permute-start = (bf16[32,512]{1,0:T(8,128)(2,1)}, bf16[32,512]{1,0:T(8,128)(2,1)}, u32[]{:S(2)}, u32[]{:S(2)}) collective-permute-start(bf16[32,512]{1,0:T(8,128)(2,1)} %bitcast.5), channel_id=1, source_target_pairs={{0,4},{4,0},{8,12},{12,8},{16,20},{20,16},{24,28},{28,24},{1,5},{5... | collective-permute-start | bytes 98312 | tf_op jit(solution)/shard_map/ppermute | solution.py:16
  6.1 30.9 %collective-permute-start.3 = (bf16[1024,256]{1,0:T(8,128)(2,1)}, bf16[1024,256]{1,0:T(8,128)(2,1)}, u32[]{:S(2)}, u32[]{:S(2)}) collective-permute-start(bf16[1024,256]{1,0:T(8,128)(2,1)} %param.16), channel_id=1, source_target_pairs={{1,0},{2,1},{3,2},{5,4},{6,5},{7,6},{9,8},{10,9},{11,10},{13,12},{... | collective-permute-start | bytes 1572872 | tf_op jit(solution)/shard_map/ppermute | solution.py:22
  12.0 5.3 %copy-start.7 = (bf16[256,1024]{1,0:T(8,128)(2,1)S(1)}, bf16[256,1024]{1,0:T(8,128)(2,1)}, u32[]{:S(2)}) copy-start(bf16[256,1024]{1,0:T(8,128)(2,1)} %param.17) | copy-start | bytes 1572868
  17.3 0.9 %copy-start.3 = (bf16[128,1024]{1,0:T(8,128)(2,1)S(1)}, bf16[128,1024]{1,0:T(8,128)(2,1)}, u32[]{:S(2)}) copy-start(bf16[128,1024]{1,0:T(8,128)(2,1)} %param.14) | copy-start | bytes 786436
  18.2 0.7 %copy-start.6 = (s32[1,256]{1,0:T(1,128)S(1)}, s32[1,256]{1,0:T(1,128)}, u32[]{:S(2)}) copy-start(s32[1,256]{1,0:T(1,128)} %param.13) | copy-start | bytes 3076
  18.7 19.7 %copy-start.1 = (f32[128,1024]{1,0:T(8,128)}, f32[128,1024]{1,0:T(8,128)S(1)}, u32[]{:S(2)}) copy-start(f32[128,1024]{1,0:T(8,128)S(1)} %fusion.104) | copy-start | bytes 1572868
  21.9 4.2 %collective-permute-start.1 = (bf16[32,512]{1,0:T(8,128)(2,1)S(1)}, bf16[32,512]{1,0:T(8,128)(2,1)S(1)}, u32[]{:S(2)}, u32[]{:S(2)}) collective-permute-start(bf16[32,512]{1,0:T(8,128)(2,1)S(1)} %fusion.9), channel_id=1, source_target_pairs={{0,8},{4,12},{8,0},{12,4},{16,24},{20,28},{24,16},{28,20},{1,9},{5... | collective-permute-start | bytes 98312 | tf_op jit(solution)/shard_map/ppermute | solution.py:16
  27.4 5.2 %collective-permute-start.2 = (bf16[32,512]{1,0:T(8,128)(2,1)S(1)}, bf16[32,512]{1,0:T(8,128)(2,1)S(1)}, u32[]{:S(2)}, u32[]{:S(2)}) collective-permute-start(bf16[32,512]{1,0:T(8,128)(2,1)S(1)} %fusion.10), channel_id=1, source_target_pairs={{0,16},{4,20},{8,24},{12,28},{16,0},{20,4},{24,8},{28,12},{1,17},{... | collective-permute-start | bytes 98312 | tf_op jit(solution)/shard_map/ppermute | solution.py:16
  33.4 3.6 %collective-permute-start.7 = (bf16[32,512]{1,0:T(8,128)(2,1)}, bf16[32,512]{1,0:T(8,128)(2,1)S(1)}, u32[]{:S(2)}, u32[]{:S(2)}) collective-permute-start(bf16[32,512]{1,0:T(8,128)(2,1)} %get-tuple-element.8), channel_id=1, source_target_pairs={{0,1},{1,2},{2,3},{3,0},{4,5},{5,6},{6,7},{7,4},{8,9},{9,10},{10,1... | collective-permute-start | bytes 98312 | tf_op jit(solution)/shard_map/ppermute | solution.py:115
  33.5 8.2 %collective-permute-start.8 = (bf16[32,512]{1,0:T(8,128)(2,1)}, bf16[32,512]{1,0:T(8,128)(2,1)S(1)}, u32[]{:S(2)}, u32[]{:S(2)}) collective-permute-start(bf16[32,512]{1,0:T(8,128)(2,1)} %get-tuple-element.8), channel_id=1, source_target_pairs={{0,2},{1,3},{2,0},{3,1},{4,6},{5,7},{6,4},{7,5},{8,10},{9,11},{10,... | collective-permute-start | bytes 98312 | tf_op jit(solution)/shard_map/ppermute | solution.py:115
  35.6 6.1 %collective-permute-start.9 = (bf16[32,512]{1,0:T(8,128)(2,1)}, bf16[32,512]{1,0:T(8,128)(2,1)S(1)}, u32[]{:S(2)}, u32[]{:S(2)}) collective-permute-start(bf16[32,512]{1,0:T(8,128)(2,1)} %get-tuple-element.8), channel_id=1, source_target_pairs={{0,3},{1,0},{2,1},{3,2},{4,7},{5,4},{6,5},{7,6},{8,11},{9,8},{10,9... | collective-permute-start | bytes 98312 | tf_op jit(solution)/shard_map/ppermute | solution.py:115
  39.7 6.6 %collective-permute-start.6 = (bf16[400,256]{1,0:T(8,128)(2,1)S(1)}, bf16[400,256]{1,0:T(8,128)(2,1)S(1)}, u32[]{:S(2)}, u32[]{:S(2)}) collective-permute-start(bf16[400,256]{1,0:T(8,128)(2,1)S(1)} %pad_maximum_fusion.1), channel_id=1, source_target_pairs={{0,3},{4,7},{8,11},{12,15},{16,19},{20,23},{24,27},{28,31}} | collective-permute-start | bytes 614408 | tf_op jit(solution)/shard_map/ppermute | solution.py:22
  41.7 9.0 %collective-permute-start.5 = (bf16[400,256]{1,0:T(8,128)(2,1)S(1)}, bf16[400,256]{1,0:T(8,128)(2,1)S(1)}, u32[]{:S(2)}, u32[]{:S(2)}) collective-permute-start(bf16[400,256]{1,0:T(8,128)(2,1)S(1)} %pad_maximum_fusion.1), channel_id=1, source_target_pairs={{0,2},{1,3},{4,6},{5,7},{8,10},{9,11},{12,14},{13,15},{16,18},{17,... | collective-permute-start | bytes 614408 | tf_op jit(solution)/shard_map/ppermute | solution.py:22
  44.3 6.8 %collective-permute-start.4 = (bf16[400,256]{1,0:T(8,128)(2,1)S(1)}, bf16[400,256]{1,0:T(8,128)(2,1)S(1)}, u32[]{:S(2)}, u32[]{:S(2)}) collective-permute-start(bf16[400,256]{1,0:T(8,128)(2,1)S(1)} %pad_maximum_fusion.1), channel_id=1, source_target_pairs={{0,1},{1,2},{2,3},{4,5},{5,6},{6,7},{8,9},{9,10},{10,11},{12,13},{... | collective-permute-start | bytes 614408 | tf_op jit(solution)/shard_map/ppermute | solution.py:22
  51.1 1.0 %copy-start.2 = (f32[128,1024]{1,0:T(8,128)S(1)}, f32[128,1024]{1,0:T(8,128)}, u32[]{:S(2)}) copy-start(f32[128,1024]{1,0:T(8,128)} %copy-done.1) | copy-start | bytes 1572868

commit v2 on v0

v2 whole, which is shorter than its diff:
```python
import functools

import jax
import jax.numpy as jnp
from jax import lax
from jax.experimental import pallas as pl
from jax.experimental.pallas import tpu as pltpu
from jax.sharding import PartitionSpec as P

BF16 = jnp.bfloat16
F32 = jnp.float32
LOW_BITS = 8
INDEX_ROWS = 16


def dot(left, right):
    return jnp.dot(left, right, preferred_element_type=F32)


def picker(columns, size):
    rows = lax.broadcasted_iota(jnp.int32, (size, columns.shape[1]), 0)
    return jnp.where(rows == columns, 1.0, 0.0).astype(BF16)


def kernel_call(kernel, outs, scratch, operands, flops=0, after=()):
    taken = len(operands)
    operands = [*operands, *after]

    def run(*refs):
        kernel(*refs[:taken], *refs[len(operands) :])

    vmem = pl.BlockSpec(memory_space=pltpu.VMEM)
    shapes = [
        pltpu.VMEM(shape, dtype) if inside else jax.ShapeDtypeStruct(shape, dtype)
        for shape, dtype, inside in outs
    ]
    placed = [pltpu.with_memory_space_constraint(x, pltpu.VMEM) for x in operands]
    return pl.pallas_call(
        run,
        out_shape=shapes,
        in_specs=[vmem] * len(placed),
        out_specs=[vmem] * len(shapes),
        scratch_shapes=scratch,
        compiler_params=pltpu.CompilerParams(vmem_limit_bytes=24 * 1024 * 1024),
        cost_estimate=pl.CostEstimate(flops=flops, bytes_accessed=0, transcendentals=0),
    )(*placed)


def pickers_kernel(order_ref, pick_ref):
    for level in range(pick_ref.shape[0]):
        pick_ref[level] = picker(order_ref[level], pick_ref.shape[1])


def panel_kernel(write_ref, inverse_ref, source_ref, gain_ref, base_ref):
    inverse = inverse_ref[...]
    gain_ref[...] = dot(write_ref[...], inverse).astype(BF16)
    base_ref[...] = dot(source_ref[...], inverse)


def block_kernel(gain_ref, base_ref, read_ref, rows_ref, block_ref):
    vectors, rank = base_ref.shape[0], gain_ref.shape[0]
    read = read_ref[...]
    block_ref[:vectors] = dot(base_ref[...].astype(BF16), read).astype(BF16)
    block_ref[vectors : vectors + rank] = dot(gain_ref[...], read).astype(BF16)
    rows = rows_ref[...]
    low = jnp.bitwise_and(rows, 2**LOW_BITS - 1)
    high = lax.shift_right_logical(rows, jnp.full(rows.shape, LOW_BITS, jnp.int32))
    at = vectors + rank
    for part in (low, high):
        wide = jnp.broadcast_to(part.astype(F32), (INDEX_ROWS, rank))
        block_ref[at : at + INDEX_ROWS] = wide.astype(BF16)
        at += INDEX_ROWS


def mixed(own_part, partner_part, own, cross):
    size = own.shape[0]
    pieces = []
    for start in range(0, own_part.shape[1], size):
        cut = slice(start, start + size)
        pieces.append(dot(own_part[:, cut], own) + dot(partner_part[:, cut], cross))
    return jnp.concatenate(pieces, axis=1)


def first_kernel(chips, pick_ref, order_ref, own_ref, cross_ref, *refs):
    slabs, partners, (out_ref, held, swap) = refs[:chips], refs[chips : 2 * chips], refs[2 * chips :]
    rows, size = slabs[0].shape
    chip = lax.axis_index("fr") // 2
    partner_pick = picker(order_ref[0], size)
    for shift in range(chips):
        slot = pl.ds(pl.multiple_of(lax.rem(chip + chips - shift, chips) * rows, rows), rows)
        held[slot, :] = dot(slabs[shift][...], pick_ref[0])
        swap[slot, :] = dot(partners[shift][...], partner_pick)
    level = mixed(held[...].astype(BF16), swap[...].astype(BF16), own_ref[0], cross_ref[0])
    out_ref[...] = dot(level.astype(BF16), pick_ref[1]).astype(BF16)


def level_kernel(level, pick_ref, own_ref, cross_ref, held_ref, swap_ref, out_ref):
    mix = mixed(held_ref[...], swap_ref[...], own_ref[level], cross_ref[level])
    out_ref[...] = dot(mix.astype(BF16), pick_ref[level + 1]).astype(BF16)


def chain_kernel(
    gain_ref, base_ref, block_ref, other_ref, fixed_ref, reach_ref, slope_ref, hop_fixed_ref, hop_ref, *hop_slope
):
    vectors, rank = base_ref.shape[0], gain_ref.shape[0]
    top_rows = hop_ref.shape[0]
    odd = lax.rem(lax.axis_index("fr"), 2) == 1

    def parts(ref):
        at = vectors + rank
        low = ref[at : at + INDEX_ROWS].astype(F32)[:1].astype(jnp.int32)
        at += INDEX_ROWS
        high = ref[at : at + INDEX_ROWS].astype(F32)[:1].astype(jnp.int32)
        return ref[:vectors], ref[vectors : vectors + rank], high * 2**LOW_BITS + low

    base_own, step_own, rows_own = parts(block_ref)
    base_other, step_other, rows_other = parts(other_ref)
    base_even = jnp.where(odd, base_other, base_own)
    base_odd = jnp.where(odd, base_own, base_other)
    step_even = jnp.where(odd, step_other, step_own)
    step_odd = jnp.where(odd, step_own, step_other)
    pick_even = picker(jnp.where(odd, rows_other, rows_own), top_rows)
    pick_odd = picker(jnp.where(odd, rows_own, rows_other), top_rows)

    past = (dot(pick_even, step_even) - pick_odd.astype(F32)).astype(BF16)
    hop_fixed_ref[...] = base_odd.astype(F32) - dot(base_even, step_odd)
    hop_ref[...] = dot(past, step_odd).astype(BF16)
    for ref in hop_slope:
        ref[...] = dot(step_even, step_odd).astype(BF16)
    reach_ref[...] = jnp.where(odd, -past, pick_even)
    gain = gain_ref[...]
    fixed_ref[...] = base_ref[...] - dot(jnp.where(odd, base_even, jnp.zeros_like(base_even)), gain)
    slope_ref[...] = jnp.where(odd, -dot(step_even, gain), gain.astype(F32)).astype(BF16)


def last_kernel(
    chips, level, own_ref, cross_ref, held_ref, swap_ref, hop_fixed_ref, hop_ref, top_ref, pass_ref, out_ref, wide
):
    rows = out_ref.shape[0]
    place = lax.axis_index("fr")
    mix = mixed(held_ref[...], swap_ref[...], own_ref[level], cross_ref[level])
    wide[...] = mix
    top = mix.astype(BF16)
    top_ref[...] = top
    out_ref[...] = wide[pl.ds(pl.multiple_of(place // 2 * rows, rows), rows), :].astype(BF16)
    moved = dot(top, hop_ref[...])
    for chip in range(chips):
        start = pl.multiple_of((2 * chip + lax.rem(place, 2)) * rows, rows)
        cut = slice(chip * rows, (chip + 1) * rows)
        wide[cut, : moved.shape[1]] = moved[cut] + hop_fixed_ref[pl.ds(start, rows), :]
    pass_ref[...] = wide[:, : moved.shape[1]].astype(BF16)


def in_order(wide, own, other, rows):
    core = lax.rem(lax.axis_index("fr"), 2)
    for chip in range(own.shape[0] // rows):
        cut = slice(chip * rows, (chip + 1) * rows)
        for piece, side in ((own, core), (other, 1 - core)):
            wide[pl.ds(pl.multiple_of((2 * chip + side) * rows, rows), rows), :] = piece[cut]
    return wide[...]


def link_kernel(rows, fixed_ref, reach_ref, gain_ref, top_ref, other_ref, out_ref, wide):
    reach = reach_ref[...]
    link = in_order(wide, dot(top_ref[...], reach), dot(other_ref[...], reach), rows)
    out_ref[...] = fixed_ref[...] - dot(link.astype(BF16), gain_ref[...])


def final_kernel(rows, fixed_ref, slope_ref, own_ref, other_ref, out_ref, wide):
    arrived = in_order(wide, own_ref[...].astype(F32), other_ref[...].astype(F32), rows)
    arrived = jnp.where(lax.axis_index("fr") >= 2, arrived, 0.0).astype(BF16)
    out_ref[...] = (fixed_ref[...] - dot(arrived, slope_ref[...])).astype(BF16)


def body(
    top_source,
    level_ordering,
    butterfly_own,
    butterfly_cross,
    parent_rows,
    front_source,
    panel_inverse,
    coupling_read,
    coupling_write,
):
    levels = level_ordering.shape[0]
    rows, top_rows = top_source.shape
    vectors, panel = front_source.shape
    rank = coupling_write.shape[0]
    groups, chain = lax.axis_size("bf"), lax.axis_size("fr")
    chips = chain // 2
    local = rows * chips

    def turned(array, by, flip=0):
        pairs = [(i, (i + by) % chain ^ flip) for i in range(chain)]
        return lax.ppermute(array, "fr", pairs)

    def swapped(array, bit, by=0):
        if not by:
            return lax.ppermute(array, "bf", [(g, g ^ bit) for g in range(groups)])
        pairs = [
            (g * chain + i, (g ^ bit) * chain + (i + by) % chain)
            for g in range(groups)
            for i in range(chain)
        ]
        return lax.ppermute(array, ("bf", "fr"), pairs)

    partner_order = swapped(level_ordering, 1)
    slabs = [top_source] + [turned(top_source, 2 * shift) for shift in range(1, chips)]
    partners = [swapped(top_source, 1, 2 * shift) for shift in range(chips)]
    next_read = turned(coupling_read, -1)

    (pick,) = kernel_call(
        pickers_kernel, [((levels, top_rows, top_rows), BF16, True)], [], [level_ordering]
    )
    gain, base = kernel_call(
        panel_kernel,
        [((rank, panel), BF16, True), ((vectors, panel), F32, True)],
        [],
        [coupling_write, panel_inverse, front_source],
        2 * (rank + vectors) * panel * panel,
    )

    wide = pltpu.VMEM((local, top_rows), F32)
    factors = [butterfly_own, butterfly_cross]
    (held,) = kernel_call(
        functools.partial(first_kernel, chips),
        [((local, top_rows), BF16, True)],
        [wide, wide],
        [pick, partner_order, *factors, *slabs, *partners],
    )
    for level in range(1, levels - 1):
        swap = swapped(held, 2**level)
        (held,) = kernel_call(
            functools.partial(level_kernel, level),
            [((local, top_rows), BF16, True)],
            [],
            [pick, *factors, held, swap],
        )
    swap = swapped(held, 2 ** (levels - 1))

    (block,) = kernel_call(
        block_kernel,
        [((vectors + rank + 2 * INDEX_ROWS, rank), BF16, True)],
        [],
        [gain, base, next_read, parent_rows],
        2 * (vectors + rank) * panel * rank,
        [held],
    )
    other = turned(block, 0, 1)
    outs = [
        ((vectors, panel), F32, True),
        ((top_rows, rank), BF16, True),
        ((rank, panel), BF16, True),
        ((vectors, rank), F32, True),
        ((top_rows, rank), BF16, True),
    ] + [((rank, rank), BF16, True)] * (chips > 2)
    fixed, reach, slope, hop_fixed, hop, *hop_slope = kernel_call(
        chain_kernel, outs, [], [gain, base, block, other], 2 * rank * rank * panel
    )

    top, passed, top_own = kernel_call(
        functools.partial(last_kernel, chips, levels - 1),
        [
            ((local, top_rows), BF16, True),
            ((local, rank), BF16, True),
            ((rows, top_rows), BF16, False),
        ],
        [wide],
        [*factors, held, swap, hop_fixed, hop],
    )
    start = passed
    for _ in range(chips - 2):
        here = jnp.where(lax.axis_index("fr") >= 2, turned(passed, 2), 0)
        passed = (start.astype(F32) + dot(here, hop_slope[0])).astype(BF16)
    arrived_cross = turned(passed, 2, 1)
    arrived = turned(passed, 2)
    top_other = turned(top, 0, 1)
    (ready,) = kernel_call(
        functools.partial(link_kernel, rows),
        [((vectors, panel), F32, True)],
        [pltpu.VMEM((vectors, rank), F32)],
        [fixed, reach, gain, top, top_other],
    )
    (solved,) = kernel_call(
        functools.partial(final_kernel, rows),
        [((vectors, panel), BF16, False)],
        [pltpu.VMEM((vectors, rank), F32)],
        [ready, slope, arrived, arrived_cross],
    )
    return (top_own, solved)


def solution(mesh):
    placed = (
        P("fr", "bf"),
        P(None, "bf", None),
        P(None, "bf", None),
        P(None, "bf", None),
        P(("bf", "fr"), None),
        P(None, ("bf", "fr")),
        P(("bf", "fr"), None),
        P(("bf", "fr"), None),
        P(("bf", "fr"), None),
    )
    return jax.shard_map(
        body,
        mesh=mesh,
        in_specs=placed,
        out_specs=(P("fr", "bf"), P(None, ("bf", "fr"))),
        check_vma=False,
    )
```

time: 78.8 us -> 35.7 us (0.45)
  the two profiles are of different devices: /device:TPU:1 before, /device:TPU:0 now
where the time goes in v2:
time: 35.7 us; the launch traced here: 35.4 us
  starting transfers between devices  14.3 us (40%)
  waiting for transfers between devices  11.1 us (31%)
  Pallas kernels  5.72 us (16%)
  local copies, waits for them, and re-layouts  3.5 us (10%)
  between operations  0.75 us (2%)
    ppermute x4, starting transfers between devices, swapped(): return lax.ppermute(array, 'bf', [(g, g ^ bit) for g in range(groups)])  7.64 us
    ppermute x4, waiting for transfers between devices, swapped(): return lax.ppermute(array, 'bf', [(g, g ^ bit) for g in range(groups)])  6.28 us
    pallas_call x9, Pallas kernels, kernel_call(): pl.pallas_call(run, out_shape=shapes, in_specs=[vmem] * len(placed), out_...  5.72 us
    ppermute x6, starting transfers between devices, turned(): return lax.ppermute(array, 'fr', pairs)  5.31 us
    ppermute x6, waiting for transfers between devices, turned(): return lax.ppermute(array, 'fr', pairs)  4.83 us
    unnamed x20, local copies, waits for them, and re-layouts  3.5 us
    ppermute x1, starting transfers between devices, swapped(): return lax.ppermute(array, ('bf', 'fr'), pairs)  1.36 us
  transfers between devices with their start and end apart: 11, of which 6 were waited for; matrix products, arithmetic and copies ran while one was open for 0% of the time, Pallas kernels for 10%

profile of v2, /device:TPU:0, one launch (start us, length us, event | category | flops | bytes accessed | tf_op | source)
XLA Modules:
  0.0 35.4 jit_solution(7480976674682068106)
XLA Ops:
  0.6 2.5 %collective-permute-start.6 = (bf16[1024,256]{1,0:T(8,128)(2,1)}, bf16[1024,256]{1,0:T(8,128)(2,1)S(1)}, u32[]{:S(2)}, u32[]{:S(2)}) collective-permute-start(bf16[1024,256]{1,0:T(8,128)(2,1)} %param.16), channel_id=1, source_target_pairs={{0,3},{1,0},{2,1},{3,2},{4,7},{5,4},{6,5},{7,6},{8,11},{9,8},{10,9... | collective-permute-start | bytes 1572872 | tf_op jit(solution)/shard_map/ppermute | solution.py:196
  3.1 0.6 %collective-permute-start.1 = (bf16[32,512]{1,0:T(8,128)(2,1)}, bf16[32,512]{1,0:T(8,128)(2,1)S(1)}, u32[]{:S(2)}, u32[]{:S(2)}) collective-permute-start(bf16[32,512]{1,0:T(8,128)(2,1)} %refs_4_.1), channel_id=1, source_target_pairs={{0,2},{1,3},{2,0},{3,1},{4,6},{5,7},{6,4},{7,5},{8,10},{9,11},{10,... | collective-permute-start | bytes 98312 | tf_op jit(solution)/shard_map/ppermute | solution.py:196
  3.7 1.5 %collective-permute-start.2 = (bf16[32,512]{1,0:T(8,128)(2,1)}, bf16[32,512]{1,0:T(8,128)(2,1)S(1)}, u32[]{:S(2)}, u32[]{:S(2)}) collective-permute-start(bf16[32,512]{1,0:T(8,128)(2,1)} %refs_4_.1), channel_id=1, source_target_pairs={{0,4},{4,0},{8,12},{12,8},{16,20},{20,16},{24,28},{28,24},{1,5},{5... | collective-permute-start | bytes 98312 | tf_op jit(solution)/shard_map/ppermute | solution.py:200
  5.2 1.4 %collective-permute-start.3 = (bf16[32,512]{1,0:T(8,128)(2,1)}, bf16[32,512]{1,0:T(8,128)(2,1)S(1)}, u32[]{:S(2)}, u32[]{:S(2)}) collective-permute-start(bf16[32,512]{1,0:T(8,128)(2,1)} %refs_4_.1), channel_id=1, source_target_pairs={{0,6},{1,7},{2,4},{3,5},{4,2},{5,3},{6,0},{7,1},{8,14},{9,15},{10,... | collective-permute-start | bytes 98312 | tf_op jit(solution)/shard_map/ppermute | solution.py:206
  6.6 1.5 %collective-permute-start = (s32[3,1,512]{2,1,0:T(1,128)}, s32[3,1,512]{2,1,0:T(1,128)S(1)}, u32[]{:S(2)}, u32[]{:S(2)}) collective-permute-start(s32[3,1,512]{2,1,0:T(1,128)} %refs_0_.3), channel_id=1, source_target_pairs={{0,4},{4,0},{8,12},{12,8},{16,20},{20,16},{24,28},{28,24},{1,5},{5... | collective-permute-start | bytes 18440 | tf_op jit(solution)/shard_map/ppermute | solution.py:200
  8.1 0.0 copy-start.5
  8.1 0.7 %copy-done.5 = s32[3,1,512]{2,1,0:T(1,128)S(1)} copy-done((s32[3,1,512]{2,1,0:T(1,128)S(1)}, s32[3,1,512]{2,1,0:T(1,128)}, u32[]{:S(2)}) %copy-start.5) | copy-done | bytes 6168
  8.8 0.0 copy-start.8
  8.8 0.0 copy-start.9
  8.8 0.3 shard_map.104.refs_0_
  9.1 1.3 %collective-permute-done.refs_1_ = s32[3,1,512]{2,1,0:T(1,128)S(1)} collective-permute-done((s32[3,1,512]{2,1,0:T(1,128)}, s32[3,1,512]{2,1,0:T(1,128)S(1)}, u32[]{:S(2)}, u32[]{:S(2)}) %collective-permute-start) | collective-permute-done | bytes 6176 | tf_op jit(solution)/shard_map/ppermute | solution.py:200
  10.4 1.8 %collective-permute-done.1.refs_5_ = bf16[32,512]{1,0:T(8,128)(2,1)S(1)} collective-permute-done((bf16[32,512]{1,0:T(8,128)(2,1)}, bf16[32,512]{1,0:T(8,128)(2,1)S(1)}, u32[]{:S(2)}, u32[]{:S(2)}) %collective-permute-start.1) | collective-permute-done | bytes 32800 | tf_op jit(solution)/shard_map/ppermute | solution.py:196
  12.2 0.0 collective-permute-done.2.refs_6_
  12.2 0.0 collective-permute-done.3.refs_7_
  12.3 0.0 copy-start
  12.3 1.0 %copy-done = bf16[3,256,256]{2,1,0:T(8,128)(2,1)S(1)} copy-done((bf16[3,256,256]{2,1,0:T(8,128)(2,1)S(1)}, bf16[3,256,256]{2,1,0:T(8,128)(2,1)}, u32[]{:S(2)}) %copy-start) | copy-done | bytes 393240
  13.3 1.0 %copy-done.2 = bf16[3,256,256]{2,1,0:T(8,128)(2,1)S(1)} copy-done((bf16[3,256,256]{2,1,0:T(8,128)(2,1)S(1)}, bf16[3,256,256]{2,1,0:T(8,128)(2,1)}, u32[]{:S(2)}) %copy-start.2) | copy-done | bytes 393240
  14.2 0.8 %copy-done.4 = bf16[32,512]{1,0:T(8,128)(2,1)S(1)} copy-done((bf16[32,512]{1,0:T(8,128)(2,1)S(1)}, bf16[32,512]{1,0:T(8,128)(2,1)}, u32[]{:S(2)}) %copy-start.4) | copy-done | bytes 32792
  15.0 0.9 %shard_map.105.refs_3_ = bf16[64,512]{1,0:T(8,128)(2,1)S(1)} custom-call(bf16[3,512,512]{2,1,0:T(8,128)(2,1)S(1)} %shard_map.104.refs_0_, s32[3,1,512]{2,1,0:T(1,128)S(1)} %collective-permute-done.refs_1_, bf16[3,256,256]{2,1,0:T(8,128)(2,1)S(1)} %copy-done, bf16[3,256,256]{2,1,0:T(8,128)(2,1)S(1)} %copy-done.2, bf16[32,512]{1,0:T(8,128)(2,1)S(1)} %copy-done.4, ...), custom_call_target="tpu_custom_call" | custom-call | tf_op jit(solution)/shard_map/pallas_call | solution.py:38
  15.9 0.0 copy-start.1
  15.9 0.0 copy-start.3
  15.9 0.0 copy-start.6
  15.9 1.8 %collective-permute-start.4 = (bf16[64,512]{1,0:T(8,128)(2,1)S(1)}, bf16[64,512]{1,0:T(8,128)(2,1)S(1)}, u32[]{:S(2)}, u32[]{:S(2)}) collective-permute-start(bf16[64,512]{1,0:T(8,128)(2,1)S(1)} %shard_map.105.refs_3_), channel_id=1, source_target_pairs={{0,8},{4,12},{8,0},{12,4},{16,24},{20,28},{24,16},{28,20},{1,9},{5... | collective-permute-start | bytes 196616 | tf_op jit(solution)/shard_map/ppermute | solution.py:200
  17.7 0.0 copy-done.8
  17.7 0.0 copy-done.9
  17.7 0.0 copy-done.7
  17.7 1.0 %shard_map.107 = (bf16[256,1024]{1,0:T(8,128)(2,1)S(1)}, f32[128,1024]{1,0:T(8,128)S(1)}) custom-call(bf16[256,1024]{1,0:T(8,128)(2,1)S(1)} %copy-done.8, bf16[1024,1024]{1,0:T(8,128)(2,1)S(1)} %copy-done.7, bf16[128,1024]{1,0:T(8,128)(2,1)S(1)} %copy-done.9), custom_call_target="tpu_custom_call" | custom-call | flops 805306368 | tf_op jit(solution)/shard_map/pallas_call | solution.py:38
  18.7 1.5 %collective-permute-done.4.refs_4_ = bf16[64,512]{1,0:T(8,128)(2,1)S(1)} collective-permute-done((bf16[64,512]{1,0:T(8,128)(2,1)S(1)}, bf16[64,512]{1,0:T(8,128)(2,1)S(1)}, u32[]{:S(2)}, u32[]{:S(2)}) %collective-permute-start.4) | collective-permute-done | bytes 65568 | tf_op jit(solution)/shard_map/ppermute | solution.py:200
  20.2 0.0 copy-done.1
  20.2 0.0 copy-done.3
  20.2 0.4 %shard_map.106.refs_4_.refs_2_ = bf16[64,512]{1,0:T(8,128)(2,1)S(1)} custom-call(bf16[3,512,512]{2,1,0:T(8,128)(2,1)S(1)} %shard_map.104.refs_0_, bf16[3,256,256]{2,1,0:T(8,128)(2,1)S(1)} %copy-done.1, bf16[3,256,256]{2,1,0:T(8,128)(2,1)S(1)} %copy-done.3, bf16[64,512]{1,0:T(8,128)(2,1)S(1)} %shard_map.105.refs_3_, ...), custom_call_target="tpu_custom_call" | custom-call | tf_op jit(solution)/shard_map/pallas_call | solution.py:38
  20.6 0.0 collective-permute-done.6.refs_2_
  20.6 0.0 copy-done.6
  20.6 0.4 %shard_map.108.refs_2_ = bf16[416,256]{1,0:T(8,128)(2,1)S(1)} custom-call(bf16[256,1024]{1,0:T(8,128)(2,1)S(1)} %get-tuple-element.12.refs_0_.refs_2_, f32[128,1024]{1,0:T(8,128)S(1)} %get-tuple-element.13.refs_1_, bf16[1024,256]{1,0:T(8,128)(2,1)S(1)} %collective-permute-done.6.refs_2_, s32[1,256]{1,0:T(1,128)S(1)} %copy-done.6, ...), custom_call_target="tpu_custom_call" | custom-call | flops 201326592 | tf_op jit(solution)/shard_map/pallas_call | solution.py:38
  21.0 0.1 collective-permute-start.7
  21.1 2.8 %collective-permute-start.5 = (bf16[64,512]{1,0:T(8,128)(2,1)S(1)}, bf16[64,512]{1,0:T(8,128)(2,1)S(1)}, u32[]{:S(2)}, u32[]{:S(2)}) collective-permute-start(bf16[64,512]{1,0:T(8,128)(2,1)S(1)} %shard_map.106.refs_4_.refs_2_), channel_id=1, source_target_pairs={{0,16},{4,20},{8,24},{12,28},{16,0},{20,4},{24,8},{28,12},{1,17},{... | collective-permute-start | bytes 196616 | tf_op jit(solution)/shard_map/ppermute | solution.py:200
  23.9 0.0 collective-permute-done.7.refs_3_
  23.9 0.6 %shard_map.109 = (f32[128,1024]{1,0:T(8,128)S(1)}, bf16[512,256]{1,0:T(8,128)(2,1)S(1)}, bf16[256,1024]{1,0:T(8,128)(2,1)S(1)}, f32[128,256]{1,0:T(8,128)S(1)}, bf16[512,256]{1,0:T(8,128)(2,1)S(1)}) custom-call(bf16[256,1024]{1,0:T(8,128)(2,1)S(1)} %get-tuple-element.12.refs_0_.refs_2_, f32[128,1024]{1,0:T(8,128)S(1)} %get-tuple-element.13.refs_1_, ...), custom_call_target="tpu_custom_call" | custom-call | flops 134217728 | tf_op jit(solution)/shard_map/pallas_call | solution.py:38
  24.6 3.4 %collective-permute-done.5.refs_3_ = bf16[64,512]{1,0:T(8,128)(2,1)S(1)} collective-permute-done((bf16[64,512]{1,0:T(8,128)(2,1)S(1)}, bf16[64,512]{1,0:T(8,128)(2,1)S(1)}, u32[]{:S(2)}, u32[]{:S(2)}) %collective-permute-start.5) | collective-permute-done | bytes 65568 | tf_op jit(solution)/shard_map/ppermute | solution.py:200
  28.0 0.9 %shard_map.110 = (bf16[64,512]{1,0:T(8,128)(2,1)S(1)}, bf16[64,256]{1,0:T(8,128)(2,1)S(1)}, bf16[32,512]{1,0:T(8,128)(2,1)}) custom-call(bf16[3,256,256]{2,1,0:T(8,128)(2,1)S(1)} %copy-done.1, bf16[3,256,256]{2,1,0:T(8,128)(2,1)S(1)} %copy-done.3, bf16[64,512]{1,0:T(8,128)(2,1)S(1)} %shard_map.106.refs_4_.refs_2_, ...), custom_call_target="tpu_custom_call" | custom-call | tf_op jit(solution)/shard_map/pallas_call | solution.py:38
  28.9 0.0 collective-permute-start.8
  28.9 1.6 %collective-permute-start.10 = (bf16[64,256]{1,0:T(8,128)(2,1)S(1)}, bf16[64,256]{1,0:T(8,128)(2,1)S(1)}, u32[]{:S(2)}, u32[]{:S(2)}) collective-permute-start(bf16[64,256]{1,0:T(8,128)(2,1)S(1)} %get-tuple-element.21), channel_id=1, source_target_pairs={{0,3},{1,2},{2,1},{3,0},{4,7},{5,6},{6,5},{7,4},{8,11},{9,10},{10,... | collective-permute-start | bytes 98312 | tf_op jit(solution)/shard_map/ppermute | solution.py:196
  30.5 0.5 %collective-permute-start.9 = (bf16[64,256]{1,0:T(8,128)(2,1)S(1)}, bf16[64,256]{1,0:T(8,128)(2,1)S(1)}, u32[]{:S(2)}, u32[]{:S(2)}) collective-permute-start(bf16[64,256]{1,0:T(8,128)(2,1)S(1)} %get-tuple-element.21), channel_id=1, source_target_pairs={{0,2},{1,3},{2,0},{3,1},{4,6},{5,7},{6,4},{7,5},{8,10},{9,11},{10,... | collective-permute-start | bytes 98312 | tf_op jit(solution)/shard_map/ppermute | solution.py:196
  31.0 0.0 collective-permute-done.8.refs_4_
  31.0 0.4 %shard_map.111.refs_0_ = f32[128,1024]{1,0:T(8,128)S(1)} custom-call(f32[128,1024]{1,0:T(8,128)S(1)} %get-tuple-element.17.refs_0_, bf16[512,256]{1,0:T(8,128)(2,1)S(1)} %get-tuple-element.18.refs_1_, bf16[256,1024]{1,0:T(8,128)(2,1)S(1)} %get-tuple-element.12.refs_0_.refs_2_, bf16[64,512]{1,0:T(8,128)(2,1)S(1)} %get-tuple-element.19.refs_3_, ...), custom_call_target="tpu_custom_call" | custom-call | tf_op jit(solution)/shard_map/pallas_call | solution.py:38
  31.5 0.8 %collective-permute-done.10.refs_3_ = bf16[64,256]{1,0:T(8,128)(2,1)S(1)} collective-permute-done((bf16[64,256]{1,0:T(8,128)(2,1)S(1)}, bf16[64,256]{1,0:T(8,128)(2,1)S(1)}, u32[]{:S(2)}, u32[]{:S(2)}) %collective-permute-start.10) | collective-permute-done | bytes 32800 | tf_op jit(solution)/shard_map/ppermute | solution.py:196
  32.2 2.2 %collective-permute-done.9.refs_2_ = bf16[64,256]{1,0:T(8,128)(2,1)S(1)} collective-permute-done((bf16[64,256]{1,0:T(8,128)(2,1)S(1)}, bf16[64,256]{1,0:T(8,128)(2,1)S(1)}, u32[]{:S(2)}, u32[]{:S(2)}) %collective-permute-start.9) | collective-permute-done | bytes 32800 | tf_op jit(solution)/shard_map/ppermute | solution.py:196
  34.5 0.9 %shard_map.112 = bf16[128,1024]{1,0:T(8,128)(2,1)} custom-call(f32[128,1024]{1,0:T(8,128)S(1)} %shard_map.111.refs_0_, bf16[256,1024]{1,0:T(8,128)(2,1)S(1)} %get-tuple-element.20.refs_1_, bf16[64,256]{1,0:T(8,128)(2,1)S(1)} %collective-permute-done.9.refs_2_, bf16[64,256]{1,0:T(8,128)(2,1)S(1)} %collective-permute-done.10.refs_3_), custom_call_target="tpu_custom_call" | custom-call | tf_op jit(solution)/shard_map/pallas_call | solution.py:38
  (3 shorter events, 0.0 us)
Async XLA Ops:
  0.6 20.0 %collective-permute-start.6 = (bf16[1024,256]{1,0:T(8,128)(2,1)}, bf16[1024,256]{1,0:T(8,128)(2,1)S(1)}, u32[]{:S(2)}, u32[]{:S(2)}) collective-permute-start(bf16[1024,256]{1,0:T(8,128)(2,1)} %param.16), channel_id=1, source_target_pairs={{0,3},{1,0},{2,1},{3,2},{4,7},{5,4},{6,5},{7,6},{8,11},{9,8},{10,9... | collective-permute-start | bytes 1572872 | tf_op jit(solution)/shard_map/ppermute | solution.py:196
  3.1 9.2 %collective-permute-start.1 = (bf16[32,512]{1,0:T(8,128)(2,1)}, bf16[32,512]{1,0:T(8,128)(2,1)S(1)}, u32[]{:S(2)}, u32[]{:S(2)}) collective-permute-start(bf16[32,512]{1,0:T(8,128)(2,1)} %refs_4_.1), channel_id=1, source_target_pairs={{0,2},{1,3},{2,0},{3,1},{4,6},{5,7},{6,4},{7,5},{8,10},{9,11},{10,... | collective-permute-start | bytes 98312 | tf_op jit(solution)/shard_map/ppermute | solution.py:196
  3.7 8.5 %collective-permute-start.2 = (bf16[32,512]{1,0:T(8,128)(2,1)}, bf16[32,512]{1,0:T(8,128)(2,1)S(1)}, u32[]{:S(2)}, u32[]{:S(2)}) collective-permute-start(bf16[32,512]{1,0:T(8,128)(2,1)} %refs_4_.1), channel_id=1, source_target_pairs={{0,4},{4,0},{8,12},{12,8},{16,20},{20,16},{24,28},{28,24},{1,5},{5... | collective-permute-start | bytes 98312 | tf_op jit(solution)/shard_map/ppermute | solution.py:200
  5.2 7.0 %collective-permute-start.3 = (bf16[32,512]{1,0:T(8,128)(2,1)}, bf16[32,512]{1,0:T(8,128)(2,1)S(1)}, u32[]{:S(2)}, u32[]{:S(2)}) collective-permute-start(bf16[32,512]{1,0:T(8,128)(2,1)} %refs_4_.1), channel_id=1, source_target_pairs={{0,6},{1,7},{2,4},{3,5},{4,2},{5,3},{6,0},{7,1},{8,14},{9,15},{10,... | collective-permute-start | bytes 98312 | tf_op jit(solution)/shard_map/ppermute | solution.py:206
  6.6 3.8 %collective-permute-start = (s32[3,1,512]{2,1,0:T(1,128)}, s32[3,1,512]{2,1,0:T(1,128)S(1)}, u32[]{:S(2)}, u32[]{:S(2)}) collective-permute-start(s32[3,1,512]{2,1,0:T(1,128)} %refs_0_.3), channel_id=1, source_target_pairs={{0,4},{4,0},{8,12},{12,8},{16,20},{20,16},{24,28},{28,24},{1,5},{5... | collective-permute-start | bytes 18440 | tf_op jit(solution)/shard_map/ppermute | solution.py:200
  8.1 0.7 %copy-start.5 = (s32[3,1,512]{2,1,0:T(1,128)S(1)}, s32[3,1,512]{2,1,0:T(1,128)}, u32[]{:S(2)}) copy-start(s32[3,1,512]{2,1,0:T(1,128)} %refs_0_.3) | copy-start | bytes 18436
  8.8 8.9 %copy-start.8 = (bf16[256,1024]{1,0:T(8,128)(2,1)S(1)}, bf16[256,1024]{1,0:T(8,128)(2,1)}, u32[]{:S(2)}) copy-start(bf16[256,1024]{1,0:T(8,128)(2,1)} %refs_0_.4) | copy-start | bytes 1572868
  8.8 8.9 %copy-start.9 = (bf16[128,1024]{1,0:T(8,128)(2,1)S(1)}, bf16[128,1024]{1,0:T(8,128)(2,1)}, u32[]{:S(2)}) copy-start(bf16[128,1024]{1,0:T(8,128)(2,1)} %refs_2_.5) | copy-start | bytes 786436
  12.3 1.0 %copy-start = (bf16[3,256,256]{2,1,0:T(8,128)(2,1)S(1)}, bf16[3,256,256]{2,1,0:T(8,128)(2,1)}, u32[]{:S(2)}) copy-start(bf16[3,256,256]{2,1,0:T(8,128)(2,1)} %refs_0_.5) | copy-start | bytes 1179652
  13.2 1.0 %copy-start.2 = (bf16[3,256,256]{2,1,0:T(8,128)(2,1)S(1)}, bf16[3,256,256]{2,1,0:T(8,128)(2,1)}, u32[]{:S(2)}) copy-start(bf16[3,256,256]{2,1,0:T(8,128)(2,1)} %refs_1_.5) | copy-start | bytes 1179652
  14.2 0.8 %copy-start.4 = (bf16[32,512]{1,0:T(8,128)(2,1)S(1)}, bf16[32,512]{1,0:T(8,128)(2,1)}, u32[]{:S(2)}) copy-start(bf16[32,512]{1,0:T(8,128)(2,1)} %refs_4_.1) | copy-start | bytes 98308
  15.0 2.7 %copy-start.7 = (bf16[1024,1024]{1,0:T(8,128)(2,1)S(1)}, bf16[1024,1024]{1,0:T(8,128)(2,1)}, u32[]{:S(2)}) copy-start(bf16[1024,1024]{1,0:T(8,128)(2,1)} %refs_1_.4) | copy-start | bytes 6291460
  15.9 4.4 %copy-start.1 = (bf16[3,256,256]{2,1,0:T(8,128)(2,1)S(1)}, bf16[3,256,256]{2,1,0:T(8,128)(2,1)}, u32[]{:S(2)}) copy-start(bf16[3,256,256]{2,1,0:T(8,128)(2,1)} %refs_0_.5) | copy-start | bytes 1179652
  15.9 4.4 %copy-start.3 = (bf16[3,256,256]{2,1,0:T(8,128)(2,1)S(1)}, bf16[3,256,256]{2,1,0:T(8,128)(2,1)}, u32[]{:S(2)}) copy-start(bf16[3,256,256]{2,1,0:T(8,128)(2,1)} %refs_1_.5) | copy-start | bytes 1179652
  15.9 4.7 %copy-start.6 = (s32[1,256]{1,0:T(1,128)S(1)}, s32[1,256]{1,0:T(1,128)}, u32[]{:S(2)}) copy-start(s32[1,256]{1,0:T(1,128)} %refs_3_.3) | copy-start | bytes 3076
  15.9 4.3 %collective-permute-start.4 = (bf16[64,512]{1,0:T(8,128)(2,1)S(1)}, bf16[64,512]{1,0:T(8,128)(2,1)S(1)}, u32[]{:S(2)}, u32[]{:S(2)}) collective-permute-start(bf16[64,512]{1,0:T(8,128)(2,1)S(1)} %shard_map.105.refs_3_), channel_id=1, source_target_pairs={{0,8},{4,12},{8,0},{12,4},{16,24},{20,28},{24,16},{28,20},{1,9},{5... | collective-permute-start | bytes 196616 | tf_op jit(solution)/shard_map/ppermute | solution.py:200
  21.0 2.9 %collective-permute-start.7 = (bf16[416,256]{1,0:T(8,128)(2,1)S(1)}, bf16[416,256]{1,0:T(8,128)(2,1)S(1)}, u32[]{:S(2)}, u32[]{:S(2)}) collective-permute-start(bf16[416,256]{1,0:T(8,128)(2,1)S(1)} %shard_map.108.refs_2_), channel_id=1, source_target_pairs={{0,1},{1,0},{2,3},{3,2},{4,5},{5,4},{6,7},{7,6},{8,9},{9,8},{10,11... | collective-permute-start | bytes 638984 | tf_op jit(solution)/shard_map/ppermute | solution.py:196
  21.1 6.9 %collective-permute-start.5 = (bf16[64,512]{1,0:T(8,128)(2,1)S(1)}, bf16[64,512]{1,0:T(8,128)(2,1)S(1)}, u32[]{:S(2)}, u32[]{:S(2)}) collective-permute-start(bf16[64,512]{1,0:T(8,128)(2,1)S(1)} %shard_map.106.refs_4_.refs_2_), channel_id=1, source_target_pairs={{0,16},{4,20},{8,24},{12,28},{16,0},{20,4},{24,8},{28,12},{1,17},{... | collective-permute-start | bytes 196616 | tf_op jit(solution)/shard_map/ppermute | solution.py:200
  28.9 2.1 %collective-permute-start.8 = (bf16[64,512]{1,0:T(8,128)(2,1)S(1)}, bf16[64,512]{1,0:T(8,128)(2,1)S(1)}, u32[]{:S(2)}, u32[]{:S(2)}) collective-permute-start(bf16[64,512]{1,0:T(8,128)(2,1)S(1)} %get-tuple-element.19.refs_3_), channel_id=1, source_target_pairs={{0,1},{1,0},{2,3},{3,2},{4,5},{5,4},{6,7},{7,6},{8,9},{9,8},{10,11... | collective-permute-start | bytes 196616 | tf_op jit(solution)/shard_map/ppermute | solution.py:196
  28.9 3.3 %collective-permute-start.10 = (bf16[64,256]{1,0:T(8,128)(2,1)S(1)}, bf16[64,256]{1,0:T(8,128)(2,1)S(1)}, u32[]{:S(2)}, u32[]{:S(2)}) collective-permute-start(bf16[64,256]{1,0:T(8,128)(2,1)S(1)} %get-tuple-element.21), channel_id=1, source_target_pairs={{0,3},{1,2},{2,1},{3,0},{4,7},{5,6},{6,5},{7,4},{8,11},{9,10},{10,... | collective-permute-start | bytes 98312 | tf_op jit(solution)/shard_map/ppermute | solution.py:196
  30.5 3.9 %collective-permute-start.9 = (bf16[64,256]{1,0:T(8,128)(2,1)S(1)}, bf16[64,256]{1,0:T(8,128)(2,1)S(1)}, u32[]{:S(2)}, u32[]{:S(2)}) collective-permute-start(bf16[64,256]{1,0:T(8,128)(2,1)S(1)} %get-tuple-element.21), channel_id=1, source_target_pairs={{0,2},{1,3},{2,0},{3,1},{4,6},{5,7},{6,4},{7,5},{8,10},{9,11},{10,... | collective-permute-start | bytes 98312 | tf_op jit(solution)/shard_map/ppermute | solution.py:196

commit v3 on v2

v3 whole, which is shorter than its diff:
```python
import functools

import jax
import jax.numpy as jnp
from jax import lax
from jax.experimental import pallas as pl
from jax.experimental.pallas import tpu as pltpu
from jax.sharding import PartitionSpec as P

BF16 = jnp.bfloat16
F32 = jnp.float32
LOW_BITS = 8
INDEX_ROWS = 16
LEVEL_COST = 4 * 10**9


def dot(left, right):
    return jnp.dot(left, right, preferred_element_type=F32)


def picker(columns, size):
    rows = lax.broadcasted_iota(jnp.int32, (size, columns.shape[1]), 0)
    return jnp.where(rows == columns, 1.0, 0.0).astype(BF16)


def kernel_call(kernel, outs, scratch, operands, flops=0, remote=()):
    vmem, hbm = pl.BlockSpec(memory_space=pltpu.VMEM), pl.BlockSpec(memory_space=pltpu.HBM)
    shapes = [
        pltpu.VMEM(shape, dtype) if inside else jax.ShapeDtypeStruct(shape, dtype)
        for shape, dtype, inside in outs
    ]
    placed = [pltpu.with_memory_space_constraint(x, pltpu.VMEM) for x in operands]
    return pl.pallas_call(
        kernel,
        out_shape=shapes,
        in_specs=[vmem] * len(placed) + [hbm] * len(remote),
        out_specs=[vmem if inside else hbm for _, _, inside in outs],
        scratch_shapes=scratch,
        compiler_params=pltpu.CompilerParams(vmem_limit_bytes=24 * 1024 * 1024),
        cost_estimate=pl.CostEstimate(flops=flops, bytes_accessed=0, transcendentals=0),
    )(*placed, *[pltpu.with_memory_space_constraint(x, pltpu.HBM) for x in remote])


def shuffle_kernel(source_hbm, order_hbm, own_hbm, cross_hbm, out_ref, order_ref, own_ref, cross_ref, source, sems):
    pairs = [(order_hbm, order_ref), (source_hbm, source), (own_hbm, own_ref), (cross_hbm, cross_ref)]
    copies = [pltpu.make_async_copy(a, b, sems.at[i]) for i, (a, b) in enumerate(pairs)]
    for copy in copies:
        copy.start()
    copies[0].wait()
    pick = picker(order_ref[0], source.shape[1])
    copies[1].wait()
    out_ref[...] = dot(source[...], pick).astype(BF16)
    copies[2].wait()
    copies[3].wait()


def panel_kernel(order_ref, write_hbm, inverse_hbm, source_hbm, gain_ref, base_ref, pick_ref, left, inverse, sems):
    rank, size = gain_ref.shape
    part = rank
    copies = [
        pltpu.make_async_copy(write_hbm, left.at[:rank], sems.at[0]),
        pltpu.make_async_copy(source_hbm, left.at[rank:], sems.at[1]),
    ]
    for start in range(0, size, part):
        block = (pl.ds(start, part), pl.ds(0, start + part))
        copies.append(
            pltpu.make_async_copy(inverse_hbm.at[block], inverse.at[block], sems.at[2 + start // part])
        )
    for copy in copies:
        copy.start()
    for level in range(pick_ref.shape[0]):
        pick_ref[level] = picker(order_ref[level + 1], pick_ref.shape[1])
    for copy in copies:
        copy.wait()
    for start in range(0, size, part):
        cut = slice(start, start + part)
        product = dot(left[:, start:], inverse[start:, cut])
        gain_ref[:, cut] = product[:rank].astype(BF16)
        base_ref[:, cut] = product[rank:]


def block_kernel(gain_ref, base_ref, read_ref, rows_ref, block_ref):
    vectors, rank = base_ref.shape[0], gain_ref.shape[0]
    read = read_ref[...]
    block_ref[:vectors] = dot(base_ref[...].astype(BF16), read).astype(BF16)
    block_ref[vectors : vectors + rank] = dot(gain_ref[...], read).astype(BF16)
    rows = rows_ref[...]
    low = jnp.bitwise_and(rows, 2**LOW_BITS - 1)
    high = lax.shift_right_logical(rows, jnp.full(rows.shape, LOW_BITS, jnp.int32))
    at = vectors + rank
    for part in (low, high):
        wide = jnp.broadcast_to(part.astype(F32), (INDEX_ROWS, rank))
        block_ref[at : at + INDEX_ROWS] = wide.astype(BF16)
        at += INDEX_ROWS


def mixed(own_part, partner_part, own, cross):
    size = own.shape[0]
    pieces = []
    for start in range(0, own_part.shape[1], size):
        cut = slice(start, start + size)
        pieces.append(dot(own_part[:, cut], own) + dot(partner_part[:, cut], cross))
    return jnp.concatenate(pieces, axis=1)


def level_kernel(level, pick_ref, own_ref, cross_ref, held_ref, swap_ref, out_ref):
    mix = mixed(held_ref[...], swap_ref[...], own_ref[level], cross_ref[level])
    out_ref[...] = dot(mix.astype(BF16), pick_ref[level]).astype(BF16)


def chain_kernel(
    gain_ref, base_ref, block_ref, other_ref, fixed_ref, reach_ref, slope_ref, hop_fixed_ref, hop_ref, *hop_slope
):
    vectors, rank = base_ref.shape[0], gain_ref.shape[0]
    top_rows = hop_ref.shape[0]
    odd = lax.rem(lax.axis_index("fr"), 2) == 1

    def parts(ref):
        at = vectors + rank
        low = ref[at : at + INDEX_ROWS].astype(F32)[:1].astype(jnp.int32)
        at += INDEX_ROWS
        high = ref[at : at + INDEX_ROWS].astype(F32)[:1].astype(jnp.int32)
        return ref[:vectors], ref[vectors : vectors + rank], high * 2**LOW_BITS + low

    base_own, step_own, rows_own = parts(block_ref)
    base_other, step_other, rows_other = parts(other_ref)
    base_even = jnp.where(odd, base_other, base_own)
    base_odd = jnp.where(odd, base_own, base_other)
    step_even = jnp.where(odd, step_other, step_own)
    step_odd = jnp.where(odd, step_own, step_other)
    pick_even = picker(jnp.where(odd, rows_other, rows_own), top_rows)
    pick_odd = picker(jnp.where(odd, rows_own, rows_other), top_rows)

    past = (dot(pick_even, step_even) - pick_odd.astype(F32)).astype(BF16)
    hop_fixed_ref[...] = base_odd.astype(F32) - dot(base_even, step_odd)
    hop_ref[...] = dot(past, step_odd).astype(BF16)
    for ref in hop_slope:
        ref[...] = dot(step_even, step_odd).astype(BF16)
    reach_ref[...] = jnp.where(odd, -past, pick_even)
    gain = gain_ref[...]
    fixed_ref[...] = base_ref[...] - dot(jnp.where(odd, base_even, jnp.zeros_like(base_even)), gain)
    slope_ref[...] = jnp.where(odd, -dot(step_even, gain), gain.astype(F32)).astype(BF16)


def last_kernel(level, own_ref, cross_ref, held_ref, swap_ref, top_ref):
    top_ref[...] = mixed(held_ref[...], swap_ref[...], own_ref[level], cross_ref[level]).astype(BF16)


def pass_kernel(hop_fixed_ref, hop_ref, *refs):
    *slabs, top_ref, pass_ref, wide = refs
    rows = slabs[0].shape[0]
    place = lax.axis_index("fr")
    for flip, slab in enumerate(slabs):
        start = pl.multiple_of(jnp.bitwise_xor(place, flip) * rows, rows)
        wide[pl.ds(start, rows), :] = slab[...].astype(F32)
    top = wide[...].astype(BF16)
    top_ref[...] = top
    pass_ref[...] = (hop_fixed_ref[...] + dot(top, hop_ref[...])).astype(BF16)


def link_kernel(fixed_ref, reach_ref, gain_ref, top_ref, out_ref):
    link = dot(top_ref[...], reach_ref[...]).astype(BF16)
    out_ref[...] = fixed_ref[...] - dot(link, gain_ref[...])


def final_kernel(fixed_ref, slope_ref, arrived_ref, top_ref, out_hbm, top_hbm, held, sems):
    first = pltpu.make_async_copy(top_ref, top_hbm, sems.at[0])
    first.start()
    arrived = jnp.where(lax.axis_index("fr") >= 2, arrived_ref[...].astype(F32), 0.0).astype(BF16)
    parts = sems.shape[0] - 1
    width = held.shape[1] // parts
    copies = [first]
    for part in range(parts):
        cut = pl.ds(part * width, width)
        held[:, cut] = (fixed_ref[:, cut] - dot(arrived, slope_ref[:, cut])).astype(BF16)
        copies.append(pltpu.make_async_copy(held.at[:, cut], out_hbm.at[:, cut], sems.at[part + 1]))
        copies[-1].start()
    for copy in copies:
        copy.wait()


def body(
    top_source,
    level_ordering,
    butterfly_own,
    butterfly_cross,
    parent_rows,
    front_source,
    panel_inverse,
    coupling_read,
    coupling_write,
):
    levels = level_ordering.shape[0]
    rows, top_rows = top_source.shape
    vectors, panel = front_source.shape
    rank = coupling_write.shape[0]
    groups, chain = lax.axis_size("bf"), lax.axis_size("fr")
    chips = chain // 2

    def flipped(array, mask):
        return lax.ppermute(array, "fr", [(i, i ^ mask) for i in range(chain)])

    def turned(array, by):
        return lax.ppermute(array, "fr", [(i, (i + by) % chain) for i in range(chain)])

    def swapped(array, mask):
        return lax.ppermute(array, "bf", [(g, g ^ mask) for g in range(groups)])

    held, order, own, cross = kernel_call(
        shuffle_kernel,
        [
            ((rows, top_rows), BF16, True),
            (level_ordering.shape, jnp.int32, True),
            (butterfly_own.shape, BF16, True),
            (butterfly_cross.shape, BF16, True),
        ],
        [pltpu.VMEM((rows, top_rows), BF16), pltpu.SemaphoreType.DMA((4,))],
        [],
        remote=[top_source, level_ordering, butterfly_own, butterfly_cross],
    )
    swap = swapped(held, 1)
    gain, base, pick = kernel_call(
        panel_kernel,
        [
            ((rank, panel), BF16, True),
            ((vectors, panel), F32, True),
            ((levels - 1, top_rows, top_rows), BF16, True),
        ],
        [
            pltpu.VMEM((rank + vectors, panel), BF16),
            pltpu.VMEM((panel, panel), BF16),
            pltpu.SemaphoreType.DMA((2 + panel // rank,)),
        ],
        [order],
        2 * (rank + vectors) * panel * panel,
        [coupling_write, panel_inverse, front_source],
    )
    coupling_read, gain = lax.optimization_barrier((coupling_read, gain))
    next_read = turned(coupling_read, -1)

    for level in range(levels - 1):
        (held,) = kernel_call(
            functools.partial(level_kernel, level),
            [((rows, top_rows), BF16, True)],
            [],
            [pick, own, cross, held, swap],
            LEVEL_COST,
        )
        swap = swapped(held, 2 ** (level + 1))

    next_read, held = lax.optimization_barrier((next_read, held))
    (block,) = kernel_call(
        block_kernel,
        [((vectors + rank + 2 * INDEX_ROWS, rank), BF16, True)],
        [],
        [gain, base, next_read, parent_rows],
        2 * (vectors + rank) * panel * rank,
    )
    other = flipped(block, 1)
    outs = [
        ((vectors, panel), F32, True),
        ((top_rows, rank), BF16, True),
        ((rank, panel), BF16, True),
        ((vectors, rank), F32, True),
        ((top_rows, rank), BF16, True),
    ] + [((rank, rank), BF16, True)] * (chips > 2)
    fixed, reach, slope, hop_fixed, hop, *hop_slope = kernel_call(
        chain_kernel, outs, [], [gain, base, block, other], 2 * rank * rank * panel
    )

    (top,) = kernel_call(
        functools.partial(last_kernel, levels - 1),
        [((rows, top_rows), BF16, True)],
        [],
        [own, cross, held, swap],
    )
    slabs = [top] + [flipped(top, mask) for mask in range(1, chain)]
    whole, passed = kernel_call(
        pass_kernel,
        [((vectors, top_rows), BF16, True), ((vectors, rank), BF16, True)],
        [pltpu.VMEM((vectors, top_rows), F32)],
        [hop_fixed, hop, *slabs],
    )
    start = passed
    for _ in range(chips - 2):
        here = jnp.where(lax.axis_index("fr") >= 2, turned(passed, 2), 0)
        passed = (start.astype(F32) + dot(here, hop_slope[0])).astype(BF16)
    arrived = turned(passed, 2)
    (ready,) = kernel_call(
        link_kernel, [((vectors, panel), F32, True)], [], [fixed, reach, gain, whole]
    )
    solved, top = kernel_call(
        final_kernel,
        [((vectors, panel), BF16, False), ((rows, top_rows), BF16, False)],
        [pltpu.VMEM((vectors, panel), BF16), pltpu.SemaphoreType.DMA((5,))],
        [ready, slope, arrived, top],
    )
    return (top, solved)


def solution(mesh):
    placed = (
        P("fr", "bf"),
        P(None, "bf", None),
        P(None, "bf", None),
        P(None, "bf", None),
        P(("bf", "fr"), None),
        P(None, ("bf", "fr")),
        P(("bf", "fr"), None),
        P(("bf", "fr"), None),
        P(("bf", "fr"), None),
    )
    return jax.shard_map(
        body,
        mesh=mesh,
        in_specs=placed,
        out_specs=(P("fr", "bf"), P(None, ("bf", "fr"))),
        check_vma=False,
    )
```

time: 35.7 us -> 31.2 us (0.87)
  local copies, waits for them, and re-layouts: 3.5 us -> 0.01 us
  starting transfers between devices: 14.3 us -> 12.4 us
  Pallas kernels: 5.72 us -> 6.91 us
    unnamed x20 -> x4, local copies, waits for them, and re-layouts: 3.5 us -> 0.01 us
    ppermute x11 -> x9, starting transfers between devices: 14.3 us -> 12.4 us  [the longest x3 7.2 us: swapped(): return lax.ppermute(array, 'bf', [(g, g ^ mask) for g in range(groups)])]
    pallas_call x9 -> x10, Pallas kernels: 5.72 us -> 6.91 us  [kernel_call(): pl.pallas_call(kernel, out_shape=shapes, in_specs=[vmem] * len(placed) +...]
    ppermute x11 -> x9, waiting for transfers between devices: 11.1 us -> 11 us  [the longest x3 4.92 us: swapped(): return lax.ppermute(array, 'bf', [(g, g ^ mask) for g in range(groups)])]
  transfers between devices with their start and end apart: 11 -> 9, of which waited for: 6 -> 6; matrix products, arithmetic and copies ran while one was open for 0% -> 0% of each run, Pallas kernels for 10% -> 13%
where the time goes in v3:
time: 31.2 us; the launch traced here: 31.1 us
  starting transfers between devices  12.4 us (40%)
  waiting for transfers between devices  11 us (35%)
  Pallas kernels  6.91 us (22%)
  between operations  0.71 us (2%)
    ppermute x3, starting transfers between devices, swapped(): return lax.ppermute(array, 'bf', [(g, g ^ mask) for g in range(groups)])  7.2 us
    pallas_call x10, Pallas kernels, kernel_call(): pl.pallas_call(kernel, out_shape=shapes, in_specs=[vmem] * len(placed) +...  6.91 us
    ppermute x3, waiting for transfers between devices, swapped(): return lax.ppermute(array, 'bf', [(g, g ^ mask) for g in range(groups)])  4.92 us
    ppermute x2, waiting for transfers between devices, turned(): lax.ppermute(array, 'fr', [(i, (i + by) % chain) for i in range(chain)])  4.53 us
    ppermute x4, starting transfers between devices, flipped(): return lax.ppermute(array, 'fr', [(i, i ^ mask) for i in range(chain)])  3.06 us
    ppermute x2, starting transfers between devices, turned(): lax.ppermute(array, 'fr', [(i, (i + by) % chain) for i in range(chain)])  2.17 us
    ppermute x4, waiting for transfers between devices, flipped(): return lax.ppermute(array, 'fr', [(i, i ^ mask) for i in range(chain)])  1.55 us
  transfers between devices with their start and end apart: 9, of which 6 were waited for; matrix products, arithmetic and copies ran while one was open for 0% of the time, Pallas kernels for 13%

profile of v3, /device:TPU:0, one launch (start us, length us, event | category | flops | bytes accessed | tf_op | source)
XLA Modules:
  0.0 31.1 jit_solution(10076233291443163691)
XLA Ops:
  0.6 0.0 copy-start.1
  0.6 1.2 %shard_map.104 = (bf16[32,512]{1,0:T(8,128)(2,1)S(1)}, s32[3,1,512]{2,1,0:T(1,128)S(1)}, bf16[3,256,256]{2,1,0:T(8,128)(2,1)S(1)}, bf16[3,256,256]{2,1,0:T(8,128)(2,1)S(1)}) custom-call(bf16[32,512]{1,0:T(8,128)(2,1)} %source_hbm.2, s32[3,1,512]{2,1,0:T(1,128)} %order_hbm.1, bf16[3,256,256]{2,1,0:T(8,128)(2,1)} %own_hbm.1, bf16[3,256,256]{2,1,0:T(8,128)(2,1)} %cross_hbm.1), custom_call_target="tpu_custom_call" | custom-call | tf_op jit(solution)/shard_map/pallas_call | solution.py:33
  1.9 3.0 %collective-permute-start.1 = (bf16[32,512]{1,0:T(8,128)(2,1)S(1)}, bf16[32,512]{1,0:T(8,128)(2,1)S(1)}, u32[]{:S(2)}, u32[]{:S(2)}) collective-permute-start(bf16[32,512]{1,0:T(8,128)(2,1)S(1)} %get-tuple-element.30.held_ref), channel_id=1, source_target_pairs={{0,4},{4,0},{8,12},{12,8},{16,20},{20,16},{24,28},{28,24},{1,5},{5... | collective-permute-start | bytes 98312 | tf_op jit(solution)/shard_map/ppermute | solution.py:207
  4.9 2.2 %shard_map.105 = (bf16[256,1024]{1,0:T(8,128)(2,1)S(1)}, f32[128,1024]{1,0:T(8,128)S(1)}, bf16[2,512,512]{2,1,0:T(8,128)(2,1)S(1)}) custom-call(s32[3,1,512]{2,1,0:T(1,128)S(1)} %get-tuple-element.22.order_ref, bf16[256,1024]{1,0:T(8,128)(2,1)} %write_hbm.1, bf16[1024,1024]{1,0:T(8,128)(2,1)} %inverse_hbm.1, bf16[128,1024]{1,0:T(8,128)(2,1)} %source_hbm.3), custom_call_target="tpu_custom_call" | custom-call | flops 805306368 | tf_op jit(solution)/shard_map/pallas_call | solution.py:33
  7.1 0.0 copy-done.1
  7.2 0.7 %collective-permute-start = (bf16[1024,256]{1,0:T(8,128)(2,1)S(1)}, bf16[1024,256]{1,0:T(8,128)(2,1)S(1)}, u32[]{:S(2)}, u32[]{:S(2)}) collective-permute-start(bf16[1024,256]{1,0:T(8,128)(2,1)S(1)} %copy-done.1), channel_id=1, source_target_pairs={{0,3},{1,0},{2,1},{3,2},{4,7},{5,4},{6,5},{7,6},{8,11},{9,8},{10,9... | collective-permute-start | bytes 1572872 | tf_op jit(solution)/shard_map/ppermute | solution.py:204
  7.9 0.0 collective-permute-done.1.swap_ref
  7.9 0.3 %shard_map.106.held_ref = bf16[32,512]{1,0:T(8,128)(2,1)S(1)} custom-call(bf16[2,512,512]{2,1,0:T(8,128)(2,1)S(1)} %get-tuple-element.27.pick_ref, bf16[3,256,256]{2,1,0:T(8,128)(2,1)S(1)} %get-tuple-element.28.own_ref, bf16[3,256,256]{2,1,0:T(8,128)(2,1)S(1)} %get-tuple-element.29.cross_ref, bf16[32,512]{1,0:T(8,128)(2,1)S(1)} %get-tuple-element.30.held_ref, ...), custom_call_target="tpu_custom_call" | custom-call | flops 4000000000 | tf_op jit(solution)/shard_map/pallas_call | solution.py:33
  8.2 0.0 copy-start
  8.2 1.6 %collective-permute-start.2 = (bf16[32,512]{1,0:T(8,128)(2,1)S(1)}, bf16[32,512]{1,0:T(8,128)(2,1)S(1)}, u32[]{:S(2)}, u32[]{:S(2)}) collective-permute-start(bf16[32,512]{1,0:T(8,128)(2,1)S(1)} %shard_map.106.held_ref), channel_id=1, source_target_pairs={{0,8},{4,12},{8,0},{12,4},{16,24},{20,28},{24,16},{28,20},{1,9},{5... | collective-permute-start | bytes 98312 | tf_op jit(solution)/shard_map/ppermute | solution.py:207
  9.8 2.3 %collective-permute-done.2.swap_ref = bf16[32,512]{1,0:T(8,128)(2,1)S(1)} collective-permute-done((bf16[32,512]{1,0:T(8,128)(2,1)S(1)}, bf16[32,512]{1,0:T(8,128)(2,1)S(1)}, u32[]{:S(2)}, u32[]{:S(2)}) %collective-permute-start.2) | collective-permute-done | bytes 32800 | tf_op jit(solution)/shard_map/ppermute | solution.py:207
  12.2 0.3 %shard_map.107.held_ref = bf16[32,512]{1,0:T(8,128)(2,1)S(1)} custom-call(bf16[2,512,512]{2,1,0:T(8,128)(2,1)S(1)} %get-tuple-element.27.pick_ref, bf16[3,256,256]{2,1,0:T(8,128)(2,1)S(1)} %get-tuple-element.28.own_ref, bf16[3,256,256]{2,1,0:T(8,128)(2,1)S(1)} %get-tuple-element.29.cross_ref, bf16[32,512]{1,0:T(8,128)(2,1)S(1)} %shard_map.106.held_ref, ...), custom_call_target="tpu_custom_call" | custom-call | flops 4000000000 | tf_op jit(solution)/shard_map/pallas_call | solution.py:33
  12.5 2.1 %collective-permute-done.read_ref = bf16[1024,256]{1,0:T(8,128)(2,1)S(1)} collective-permute-done((bf16[1024,256]{1,0:T(8,128)(2,1)S(1)}, bf16[1024,256]{1,0:T(8,128)(2,1)S(1)}, u32[]{:S(2)}, u32[]{:S(2)}) %collective-permute-start) | collective-permute-done | bytes 524320 | tf_op jit(solution)/shard_map/ppermute | solution.py:204
  14.6 0.0 copy-done
  14.6 0.4 %shard_map.108.block_ref = bf16[416,256]{1,0:T(8,128)(2,1)S(1)} custom-call(bf16[256,1024]{1,0:T(8,128)(2,1)S(1)} %get-tuple-element.24.gain_ref, f32[128,1024]{1,0:T(8,128)S(1)} %get-tuple-element.25.base_ref, bf16[1024,256]{1,0:T(8,128)(2,1)S(1)} %collective-permute-done.read_ref, s32[1,256]{1,0:T(1,128)S(1)} %copy-done), custom_call_target="tpu_custom_call" | custom-call | flops 201326592 | tf_op jit(solution)/shard_map/pallas_call | solution.py:33
  15.0 1.2 %collective-permute-start.3 = (bf16[416,256]{1,0:T(8,128)(2,1)S(1)}, bf16[416,256]{1,0:T(8,128)(2,1)S(1)}, u32[]{:S(2)}, u32[]{:S(2)}) collective-permute-start(bf16[416,256]{1,0:T(8,128)(2,1)S(1)} %shard_map.108.block_ref), channel_id=1, source_target_pairs={{0,1},{1,0},{2,3},{3,2},{4,5},{5,4},{6,7},{7,6},{8,9},{9,8},{10,11... | collective-permute-start | bytes 638984 | tf_op jit(solution)/shard_map/ppermute | solution.py:201
  16.2 2.6 %collective-permute-start.4 = (bf16[32,512]{1,0:T(8,128)(2,1)S(1)}, bf16[32,512]{1,0:T(8,128)(2,1)S(1)}, u32[]{:S(2)}, u32[]{:S(2)}) collective-permute-start(bf16[32,512]{1,0:T(8,128)(2,1)S(1)} %shard_map.107.held_ref), channel_id=1, source_target_pairs={{0,16},{4,20},{8,24},{12,28},{16,0},{20,4},{24,8},{28,12},{1,17},{... | collective-permute-start | bytes 98312 | tf_op jit(solution)/shard_map/ppermute | solution.py:207
  18.8 2.6 %collective-permute-done.4.swap_ref = bf16[32,512]{1,0:T(8,128)(2,1)S(1)} collective-permute-done((bf16[32,512]{1,0:T(8,128)(2,1)S(1)}, bf16[32,512]{1,0:T(8,128)(2,1)S(1)}, u32[]{:S(2)}, u32[]{:S(2)}) %collective-permute-start.4) | collective-permute-done | bytes 32800 | tf_op jit(solution)/shard_map/ppermute | solution.py:207
  21.3 0.2 shard_map.110.refs_0_.top_ref
  21.5 0.0 collective-permute-start.7
  21.5 1.2 %collective-permute-start.6 = (bf16[32,512]{1,0:T(8,128)(2,1)S(1)}, bf16[32,512]{1,0:T(8,128)(2,1)S(1)}, u32[]{:S(2)}, u32[]{:S(2)}) collective-permute-start(bf16[32,512]{1,0:T(8,128)(2,1)S(1)} %shard_map.110.refs_0_.top_ref), channel_id=1, source_target_pairs={{0,2},{1,3},{2,0},{3,1},{4,6},{5,7},{6,4},{7,5},{8,10},{9,11},{10,... | collective-permute-start | bytes 98312 | tf_op jit(solution)/shard_map/ppermute | solution.py:201
  22.8 0.6 %collective-permute-start.5 = (bf16[32,512]{1,0:T(8,128)(2,1)S(1)}, bf16[32,512]{1,0:T(8,128)(2,1)S(1)}, u32[]{:S(2)}, u32[]{:S(2)}) collective-permute-start(bf16[32,512]{1,0:T(8,128)(2,1)S(1)} %shard_map.110.refs_0_.top_ref), channel_id=1, source_target_pairs={{0,1},{1,0},{2,3},{3,2},{4,5},{5,4},{6,7},{7,6},{8,9},{9,8},{10,11... | collective-permute-start | bytes 98312 | tf_op jit(solution)/shard_map/ppermute | solution.py:201
  23.4 0.0 collective-permute-done.3.other_ref
  23.4 0.6 %shard_map.109 = (f32[128,1024]{1,0:T(8,128)S(1)}, bf16[512,256]{1,0:T(8,128)(2,1)S(1)}, bf16[256,1024]{1,0:T(8,128)(2,1)S(1)}, f32[128,256]{1,0:T(8,128)S(1)}, bf16[512,256]{1,0:T(8,128)(2,1)S(1)}) custom-call(bf16[256,1024]{1,0:T(8,128)(2,1)S(1)} %get-tuple-element.24.gain_ref, f32[128,1024]{1,0:T(8,128)S(1)} %get-tuple-element.25.base_ref, ...), custom_call_target="tpu_custom_call" | custom-call | flops 134217728 | tf_op jit(solution)/shard_map/pallas_call | solution.py:33
  24.0 0.9 %collective-permute-done.7.refs_3_ = bf16[32,512]{1,0:T(8,128)(2,1)S(1)} collective-permute-done((bf16[32,512]{1,0:T(8,128)(2,1)S(1)}, bf16[32,512]{1,0:T(8,128)(2,1)S(1)}, u32[]{:S(2)}, u32[]{:S(2)}) %collective-permute-start.7) | collective-permute-done | bytes 32800 | tf_op jit(solution)/shard_map/ppermute | solution.py:201
  25.0 0.6 %collective-permute-done.6.refs_2_ = bf16[32,512]{1,0:T(8,128)(2,1)S(1)} collective-permute-done((bf16[32,512]{1,0:T(8,128)(2,1)S(1)}, bf16[32,512]{1,0:T(8,128)(2,1)S(1)}, u32[]{:S(2)}, u32[]{:S(2)}) %collective-permute-start.6) | collective-permute-done | bytes 32800 | tf_op jit(solution)/shard_map/ppermute | solution.py:201
  25.6 0.0 collective-permute-done.5.refs_1_
  25.6 0.2 shard_map.111
  25.8 1.4 %collective-permute-start.8 = (bf16[128,256]{1,0:T(8,128)(2,1)S(1)}, bf16[128,256]{1,0:T(8,128)(2,1)S(1)}, u32[]{:S(2)}, u32[]{:S(2)}) collective-permute-start(bf16[128,256]{1,0:T(8,128)(2,1)S(1)} %get-tuple-element.39), channel_id=1, source_target_pairs={{0,2},{1,3},{2,0},{3,1},{4,6},{5,7},{6,4},{7,5},{8,10},{9,11},{10,... | collective-permute-start | bytes 196616 | tf_op jit(solution)/shard_map/ppermute | solution.py:204
  27.2 0.4 %shard_map.112.fixed_ref = f32[128,1024]{1,0:T(8,128)S(1)} custom-call(f32[128,1024]{1,0:T(8,128)S(1)} %get-tuple-element.32.fixed_ref, bf16[512,256]{1,0:T(8,128)(2,1)S(1)} %get-tuple-element.33.reach_ref, bf16[256,1024]{1,0:T(8,128)(2,1)S(1)} %get-tuple-element.24.gain_ref, bf16[128,512]{1,0:T(8,128)(2,1)S(1)} %get-tuple-element.37.top_ref), custom_call_target="tpu_custom_call" | custom-call | tf_op jit(solution)/shard_map/pallas_call | solution.py:33
  27.7 2.5 %collective-permute-done.8.arrived_ref = bf16[128,256]{1,0:T(8,128)(2,1)S(1)} collective-permute-done((bf16[128,256]{1,0:T(8,128)(2,1)S(1)}, bf16[128,256]{1,0:T(8,128)(2,1)S(1)}, u32[]{:S(2)}, u32[]{:S(2)}) %collective-permute-start.8) | collective-permute-done | bytes 65568 | tf_op jit(solution)/shard_map/ppermute | solution.py:204
  30.1 0.9 %shard_map.113 = (bf16[128,1024]{1,0:T(8,128)(2,1)}, bf16[32,512]{1,0:T(8,128)(2,1)}) custom-call(f32[128,1024]{1,0:T(8,128)S(1)} %shard_map.112.fixed_ref, bf16[256,1024]{1,0:T(8,128)(2,1)S(1)} %get-tuple-element.38.slope_ref, bf16[128,256]{1,0:T(8,128)(2,1)S(1)} %collective-permute-done.8.arrived_ref, bf16[32,512]{1,0:T(8,128)(2,1)S(1)} %shard_map.110.refs_0_.top_ref), custom_call_target="tpu_custom_call" | custom-call | tf_op jit(solution)/shard_map/pallas_call | solution.py:33
Async XLA Ops:
  0.6 6.5 %copy-start.1 = (bf16[1024,256]{1,0:T(8,128)(2,1)S(1)}, bf16[1024,256]{1,0:T(8,128)(2,1)}, u32[]{:S(2)}) copy-start(bf16[1024,256]{1,0:T(8,128)(2,1)} %param.16) | copy-start | bytes 1572868
  1.9 6.0 %collective-permute-start.1 = (bf16[32,512]{1,0:T(8,128)(2,1)S(1)}, bf16[32,512]{1,0:T(8,128)(2,1)S(1)}, u32[]{:S(2)}, u32[]{:S(2)}) collective-permute-start(bf16[32,512]{1,0:T(8,128)(2,1)S(1)} %get-tuple-element.30.held_ref), channel_id=1, source_target_pairs={{0,4},{4,0},{8,12},{12,8},{16,20},{20,16},{24,28},{28,24},{1,5},{5... | collective-permute-start | bytes 98312 | tf_op jit(solution)/shard_map/ppermute | solution.py:207
  7.2 7.4 %collective-permute-start = (bf16[1024,256]{1,0:T(8,128)(2,1)S(1)}, bf16[1024,256]{1,0:T(8,128)(2,1)S(1)}, u32[]{:S(2)}, u32[]{:S(2)}) collective-permute-start(bf16[1024,256]{1,0:T(8,128)(2,1)S(1)} %copy-done.1), channel_id=1, source_target_pairs={{0,3},{1,0},{2,1},{3,2},{4,7},{5,4},{6,5},{7,6},{8,11},{9,8},{10,9... | collective-permute-start | bytes 1572872 | tf_op jit(solution)/shard_map/ppermute | solution.py:204
  8.2 6.4 %copy-start = (s32[1,256]{1,0:T(1,128)S(1)}, s32[1,256]{1,0:T(1,128)}, u32[]{:S(2)}) copy-start(s32[1,256]{1,0:T(1,128)} %rows_ref.1) | copy-start | bytes 3076
  8.2 3.9 %collective-permute-start.2 = (bf16[32,512]{1,0:T(8,128)(2,1)S(1)}, bf16[32,512]{1,0:T(8,128)(2,1)S(1)}, u32[]{:S(2)}, u32[]{:S(2)}) collective-permute-start(bf16[32,512]{1,0:T(8,128)(2,1)S(1)} %shard_map.106.held_ref), channel_id=1, source_target_pairs={{0,8},{4,12},{8,0},{12,4},{16,24},{20,28},{24,16},{28,20},{1,9},{5... | collective-permute-start | bytes 98312 | tf_op jit(solution)/shard_map/ppermute | solution.py:207
  15.0 8.4 %collective-permute-start.3 = (bf16[416,256]{1,0:T(8,128)(2,1)S(1)}, bf16[416,256]{1,0:T(8,128)(2,1)S(1)}, u32[]{:S(2)}, u32[]{:S(2)}) collective-permute-start(bf16[416,256]{1,0:T(8,128)(2,1)S(1)} %shard_map.108.block_ref), channel_id=1, source_target_pairs={{0,1},{1,0},{2,3},{3,2},{4,5},{5,4},{6,7},{7,6},{8,9},{9,8},{10,11... | collective-permute-start | bytes 638984 | tf_op jit(solution)/shard_map/ppermute | solution.py:201
  16.2 5.2 %collective-permute-start.4 = (bf16[32,512]{1,0:T(8,128)(2,1)S(1)}, bf16[32,512]{1,0:T(8,128)(2,1)S(1)}, u32[]{:S(2)}, u32[]{:S(2)}) collective-permute-start(bf16[32,512]{1,0:T(8,128)(2,1)S(1)} %shard_map.107.held_ref), channel_id=1, source_target_pairs={{0,16},{4,20},{8,24},{12,28},{16,0},{20,4},{24,8},{28,12},{1,17},{... | collective-permute-start | bytes 98312 | tf_op jit(solution)/shard_map/ppermute | solution.py:207
  21.5 3.4 %collective-permute-start.7 = (bf16[32,512]{1,0:T(8,128)(2,1)S(1)}, bf16[32,512]{1,0:T(8,128)(2,1)S(1)}, u32[]{:S(2)}, u32[]{:S(2)}) collective-permute-start(bf16[32,512]{1,0:T(8,128)(2,1)S(1)} %shard_map.110.refs_0_.top_ref), channel_id=1, source_target_pairs={{0,3},{1,2},{2,1},{3,0},{4,7},{5,6},{6,5},{7,4},{8,11},{9,10},{10,... | collective-permute-start | bytes 98312 | tf_op jit(solution)/shard_map/ppermute | solution.py:201
  21.5 4.1 %collective-permute-start.6 = (bf16[32,512]{1,0:T(8,128)(2,1)S(1)}, bf16[32,512]{1,0:T(8,128)(2,1)S(1)}, u32[]{:S(2)}, u32[]{:S(2)}) collective-permute-start(bf16[32,512]{1,0:T(8,128)(2,1)S(1)} %shard_map.110.refs_0_.top_ref), channel_id=1, source_target_pairs={{0,2},{1,3},{2,0},{3,1},{4,6},{5,7},{6,4},{7,5},{8,10},{9,11},{10,... | collective-permute-start | bytes 98312 | tf_op jit(solution)/shard_map/ppermute | solution.py:201
  22.8 2.8 %collective-permute-start.5 = (bf16[32,512]{1,0:T(8,128)(2,1)S(1)}, bf16[32,512]{1,0:T(8,128)(2,1)S(1)}, u32[]{:S(2)}, u32[]{:S(2)}) collective-permute-start(bf16[32,512]{1,0:T(8,128)(2,1)S(1)} %shard_map.110.refs_0_.top_ref), channel_id=1, source_target_pairs={{0,1},{1,0},{2,3},{3,2},{4,5},{5,4},{6,7},{7,6},{8,9},{9,8},{10,11... | collective-permute-start | bytes 98312 | tf_op jit(solution)/shard_map/ppermute | solution.py:201
  25.8 4.3 %collective-permute-start.8 = (bf16[128,256]{1,0:T(8,128)(2,1)S(1)}, bf16[128,256]{1,0:T(8,128)(2,1)S(1)}, u32[]{:S(2)}, u32[]{:S(2)}) collective-permute-start(bf16[128,256]{1,0:T(8,128)(2,1)S(1)} %get-tuple-element.39), channel_id=1, source_target_pairs={{0,2},{1,3},{2,0},{3,1},{4,6},{5,7},{6,4},{7,5},{8,10},{9,11},{10,... | collective-permute-start | bytes 196616 | tf_op jit(solution)/shard_map/ppermute | solution.py:204

commit v4 on v3

--- a/solution.py
+++ b/solution.py
@@ -11,8 +11,8 @@
 F32 = jnp.float32
 LOW_BITS = 8
 INDEX_ROWS = 16
+PANEL_COST = 10**9
 LEVEL_COST = 4 * 10**9
-
 
 def dot(left, right):
     return jnp.dot(left, right, preferred_element_type=F32)
@@ -54,7 +54,12 @@
     copies[3].wait()
 
 
-def panel_kernel(order_ref, write_hbm, inverse_hbm, source_hbm, gain_ref, base_ref, pick_ref, left, inverse, sems):
+def pick_kernel(order_ref, pick_ref):
+    for level in range(pick_ref.shape[0]):
+        pick_ref[level] = picker(order_ref[level + 1], pick_ref.shape[1])
+
+
+def panel_kernel(write_hbm, inverse_hbm, source_hbm, gain_ref, base_ref, left, inverse, sems):
     rank, size = gain_ref.shape
     part = rank
     copies = [
@@ -68,8 +73,6 @@
         )
     for copy in copies:
         copy.start()
-    for level in range(pick_ref.shape[0]):
-        pick_ref[level] = picker(order_ref[level + 1], pick_ref.shape[1])
     for copy in copies:
         copy.wait()
     for start in range(0, size, part):
@@ -219,26 +222,29 @@
         remote=[top_source, level_ordering, butterfly_own, butterfly_cross],
     )
     swap = swapped(held, 1)
-    gain, base, pick = kernel_call(
+    coupling_read, order = lax.optimization_barrier((coupling_read, order))
+    next_read = turned(coupling_read, -1)
+    (pick,) = kernel_call(
+        pick_kernel, [((levels - 1, top_rows, top_rows), BF16, True)], [], [order]
+    )
+
+    panel_inverse, swap = lax.optimization_barrier((panel_inverse, swap))
+    gain, base = kernel_call(
         panel_kernel,
-        [
-            ((rank, panel), BF16, True),
-            ((vectors, panel), F32, True),
-            ((levels - 1, top_rows, top_rows), BF16, True),
-        ],
+        [((rank, panel), BF16, True), ((vectors, panel), F32, True)],
         [
             pltpu.VMEM((rank + vectors, panel), BF16),
             pltpu.VMEM((panel, panel), BF16),
             pltpu.SemaphoreType.DMA((2 + panel // rank,)),
         ],
-        [order],
-        2 * (rank + vectors) * panel * panel,
+        [],
+        PANEL_COST,
         [coupling_write, panel_inverse, front_source],
     )
-    coupling_read, gain = lax.optimization_barrier((coupling_read, gain))
-    next_read = turned(coupling_read, -1)
 
     for level in range(levels - 1):
+        if level:
+            swap, gain = lax.optimization_barrier((swap, gain))
         (held,) = kernel_call(
             functools.partial(level_kernel, level),
             [((rows, top_rows), BF16, True)],
@@ -273,6 +279,7 @@
         [((rows, top_rows), BF16, True)],
         [],
         [own, cross, held, swap],
+        LEVEL_COST,
     )
     slabs = [top] + [flipped(top, mask) for mask in range(1, chain)]
     whole, passed = kernel_call(

time: 31.2 us -> 27.5 us (0.88)
  waiting for transfers between devices: 11 us -> 8.23 us
  starting transfers between devices: 12.4 us -> 11.3 us
    ppermute x3, waiting for transfers between devices: 4.92 us -> 2.72 us  [swapped(): return lax.ppermute(array, 'bf', [(g, g ^ mask) for g in range(groups)])]
    ppermute x2, waiting for transfers between devices: 4.53 us -> 3.05 us  [turned(): lax.ppermute(array, 'fr', [(i, (i + by) % chain) for i in range(chain)])]
    ppermute x4, starting transfers between devices: 3.06 us -> 1.94 us  [flipped(): return lax.ppermute(array, 'fr', [(i, i ^ mask) for i in range(chain)])]
    ppermute x4, waiting for transfers between devices: 1.55 us -> 2.47 us  [flipped(): return lax.ppermute(array, 'fr', [(i, i ^ mask) for i in range(chain)])]
    ppermute x2, starting transfers between devices: 2.17 us -> 1.54 us  [turned(): lax.ppermute(array, 'fr', [(i, (i + by) % chain) for i in range(chain)])]
    ppermute x3, starting transfers between devices: 7.2 us -> 7.8 us  [swapped(): return lax.ppermute(array, 'bf', [(g, g ^ mask) for g in range(groups)])]
    pallas_call x10 -> x11, Pallas kernels: 6.91 us -> 7.04 us  [kernel_call(): pl.pallas_call(kernel, out_shape=shapes, in_specs=[vmem] * len(placed) +...]
  transfers between devices with their start and end apart: 9 -> 9, of which waited for: 6 -> 5; matrix products, arithmetic and copies ran while one was open for 0% -> 0% of each run, Pallas kernels for 13% -> 17%
where the time goes in v4:
time: 27.5 us; the launch traced here: 27.3 us
  starting transfers between devices  11.3 us (41%)
  waiting for transfers between devices  8.23 us (30%)
  Pallas kernels  7.04 us (26%)
  between operations  0.73 us (3%)
    ppermute x3, starting transfers between devices, swapped(): return lax.ppermute(array, 'bf', [(g, g ^ mask) for g in range(groups)])  7.8 us
    pallas_call x11, Pallas kernels, kernel_call(): pl.pallas_call(kernel, out_shape=shapes, in_specs=[vmem] * len(placed) +...  7.04 us
    ppermute x2, waiting for transfers between devices, turned(): lax.ppermute(array, 'fr', [(i, (i + by) % chain) for i in range(chain)])  3.05 us
    ppermute x3, waiting for transfers between devices, swapped(): return lax.ppermute(array, 'bf', [(g, g ^ mask) for g in range(groups)])  2.72 us
    ppermute x4, waiting for transfers between devices, flipped(): return lax.ppermute(array, 'fr', [(i, i ^ mask) for i in range(chain)])  2.47 us
    ppermute x4, starting transfers between devices, flipped(): return lax.ppermute(array, 'fr', [(i, i ^ mask) for i in range(chain)])  1.94 us
    ppermute x2, starting transfers between devices, turned(): lax.ppermute(array, 'fr', [(i, (i + by) % chain) for i in range(chain)])  1.54 us
  transfers between devices with their start and end apart: 9, of which 5 were waited for; matrix products, arithmetic and copies ran while one was open for 0% of the time, Pallas kernels for 17%

profile of v4, /device:TPU:0, one launch (start us, length us, event | category | flops | bytes accessed | tf_op | source)
XLA Modules:
  0.0 27.3 jit_solution(8244612326524024512)
XLA Ops:
  0.6 1.2 %shard_map.104 = (bf16[32,512]{1,0:T(8,128)(2,1)S(1)}, s32[3,1,512]{2,1,0:T(1,128)S(1)}, bf16[3,256,256]{2,1,0:T(8,128)(2,1)S(1)}, bf16[3,256,256]{2,1,0:T(8,128)(2,1)S(1)}) custom-call(bf16[32,512]{1,0:T(8,128)(2,1)} %source_hbm.2, s32[3,1,512]{2,1,0:T(1,128)} %order_hbm.1, bf16[3,256,256]{2,1,0:T(8,128)(2,1)} %own_hbm.1, bf16[3,256,256]{2,1,0:T(8,128)(2,1)} %cross_hbm.1), custom_call_target="tpu_custom_call" | custom-call | tf_op jit(solution)/shard_map/pallas_call | solution.py:33
  1.8 3.0 %collective-permute-start = (bf16[32,512]{1,0:T(8,128)(2,1)S(1)}, bf16[32,512]{1,0:T(8,128)(2,1)S(1)}, u32[]{:S(2)}, u32[]{:S(2)}) collective-permute-start(bf16[32,512]{1,0:T(8,128)(2,1)S(1)} %get-tuple-element.29.held_ref), channel_id=1, source_target_pairs={{0,4},{4,0},{8,12},{12,8},{16,20},{20,16},{24,28},{28,24},{1,5},{5... | collective-permute-start | bytes 98312 | tf_op jit(solution)/shard_map/ppermute | solution.py:210
  4.8 0.7 %collective-permute-start.2 = (bf16[1024,256]{1,0:T(8,128)(2,1)}, bf16[1024,256]{1,0:T(8,128)(2,1)S(1)}, u32[]{:S(2)}, u32[]{:S(2)}) collective-permute-start(bf16[1024,256]{1,0:T(8,128)(2,1)} %param.16), channel_id=1, source_target_pairs={{0,3},{1,0},{2,1},{3,2},{4,7},{5,4},{6,5},{7,6},{8,11},{9,8},{10,9... | collective-permute-start | bytes 1572872 | tf_op jit(solution)/shard_map/ppermute | solution.py:207
  5.5 0.2 shard_map.105.pick_ref
  5.7 1.0 %collective-permute-done.swap_ref = bf16[32,512]{1,0:T(8,128)(2,1)S(1)} collective-permute-done((bf16[32,512]{1,0:T(8,128)(2,1)S(1)}, bf16[32,512]{1,0:T(8,128)(2,1)S(1)}, u32[]{:S(2)}, u32[]{:S(2)}) %collective-permute-start) | collective-permute-done | bytes 32800 | tf_op jit(solution)/shard_map/ppermute | solution.py:210
  6.7 0.3 %shard_map.106.held_ref = bf16[32,512]{1,0:T(8,128)(2,1)S(1)} custom-call(bf16[2,512,512]{2,1,0:T(8,128)(2,1)S(1)} %shard_map.105.pick_ref, bf16[3,256,256]{2,1,0:T(8,128)(2,1)S(1)} %get-tuple-element.27.own_ref, bf16[3,256,256]{2,1,0:T(8,128)(2,1)S(1)} %get-tuple-element.28.cross_ref, bf16[32,512]{1,0:T(8,128)(2,1)S(1)} %get-tuple-element.29.held_ref, ...), custom_call_target="tpu_custom_call" | custom-call | flops 4000000000 | tf_op jit(solution)/shard_map/pallas_call | solution.py:33
  7.1 2.1 %collective-permute-start.1 = (bf16[32,512]{1,0:T(8,128)(2,1)S(1)}, bf16[32,512]{1,0:T(8,128)(2,1)S(1)}, u32[]{:S(2)}, u32[]{:S(2)}) collective-permute-start(bf16[32,512]{1,0:T(8,128)(2,1)S(1)} %shard_map.106.held_ref), channel_id=1, source_target_pairs={{0,8},{4,12},{8,0},{12,4},{16,24},{20,28},{24,16},{28,20},{1,9},{5... | collective-permute-start | bytes 98312 | tf_op jit(solution)/shard_map/ppermute | solution.py:210
  9.2 2.2 %shard_map.107 = (bf16[256,1024]{1,0:T(8,128)(2,1)S(1)}, f32[128,1024]{1,0:T(8,128)S(1)}) custom-call(bf16[256,1024]{1,0:T(8,128)(2,1)} %write_hbm.1, bf16[1024,1024]{1,0:T(8,128)(2,1)} %inverse_hbm, bf16[128,1024]{1,0:T(8,128)(2,1)} %source_hbm.3), custom_call_target="tpu_custom_call" | custom-call | flops 1000000000 | tf_op jit(solution)/shard_map/pallas_call | solution.py:33
  11.4 0.0 collective-permute-done.1.swap_ref
  11.5 0.0 copy-start
  11.5 0.3 %shard_map.108.held_ref = bf16[32,512]{1,0:T(8,128)(2,1)S(1)} custom-call(bf16[2,512,512]{2,1,0:T(8,128)(2,1)S(1)} %shard_map.105.pick_ref, bf16[3,256,256]{2,1,0:T(8,128)(2,1)S(1)} %get-tuple-element.27.own_ref, bf16[3,256,256]{2,1,0:T(8,128)(2,1)S(1)} %get-tuple-element.28.cross_ref, bf16[32,512]{1,0:T(8,128)(2,1)S(1)} %shard_map.106.held_ref, ...), custom_call_target="tpu_custom_call" | custom-call | flops 4000000000 | tf_op jit(solution)/shard_map/pallas_call | solution.py:33
  11.8 2.7 %collective-permute-start.4 = (bf16[32,512]{1,0:T(8,128)(2,1)S(1)}, bf16[32,512]{1,0:T(8,128)(2,1)S(1)}, u32[]{:S(2)}, u32[]{:S(2)}) collective-permute-start(bf16[32,512]{1,0:T(8,128)(2,1)S(1)} %shard_map.108.held_ref), channel_id=1, source_target_pairs={{0,16},{4,20},{8,24},{12,28},{16,0},{20,4},{24,8},{28,12},{1,17},{... | collective-permute-start | bytes 98312 | tf_op jit(solution)/shard_map/ppermute | solution.py:210
  14.5 0.0 collective-permute-done.2.read_ref
  14.5 0.0 copy-done
  14.5 0.4 %shard_map.109.block_ref = bf16[416,256]{1,0:T(8,128)(2,1)S(1)} custom-call(bf16[256,1024]{1,0:T(8,128)(2,1)S(1)} %get-tuple-element.33.gain_ref, f32[128,1024]{1,0:T(8,128)S(1)} %get-tuple-element.34.base_ref, bf16[1024,256]{1,0:T(8,128)(2,1)S(1)} %collective-permute-done.2.read_ref, s32[1,256]{1,0:T(1,128)S(1)} %copy-done), custom_call_target="tpu_custom_call" | custom-call | flops 201326592 | tf_op jit(solution)/shard_map/pallas_call | solution.py:33
  14.9 0.1 collective-permute-start.3
  14.9 1.7 %collective-permute-done.4.swap_ref = bf16[32,512]{1,0:T(8,128)(2,1)S(1)} collective-permute-done((bf16[32,512]{1,0:T(8,128)(2,1)S(1)}, bf16[32,512]{1,0:T(8,128)(2,1)S(1)}, u32[]{:S(2)}, u32[]{:S(2)}) %collective-permute-start.4) | collective-permute-done | bytes 32800 | tf_op jit(solution)/shard_map/ppermute | solution.py:210
  16.6 0.2 shard_map.111.refs_0_.top_ref
  16.8 0.0 collective-permute-start.5
  16.8 1.6 %collective-permute-start.6 = (bf16[32,512]{1,0:T(8,128)(2,1)S(1)}, bf16[32,512]{1,0:T(8,128)(2,1)S(1)}, u32[]{:S(2)}, u32[]{:S(2)}) collective-permute-start(bf16[32,512]{1,0:T(8,128)(2,1)S(1)} %shard_map.111.refs_0_.top_ref), channel_id=1, source_target_pairs={{0,2},{1,3},{2,0},{3,1},{4,6},{5,7},{6,4},{7,5},{8,10},{9,11},{10,... | collective-permute-start | bytes 98312 | tf_op jit(solution)/shard_map/ppermute | solution.py:204
  18.5 0.2 collective-permute-start.7
  18.7 0.0 collective-permute-done.3.other_ref
  18.7 0.6 %shard_map.110 = (f32[128,1024]{1,0:T(8,128)S(1)}, bf16[512,256]{1,0:T(8,128)(2,1)S(1)}, bf16[256,1024]{1,0:T(8,128)(2,1)S(1)}, f32[128,256]{1,0:T(8,128)S(1)}, bf16[512,256]{1,0:T(8,128)(2,1)S(1)}) custom-call(bf16[256,1024]{1,0:T(8,128)(2,1)S(1)} %get-tuple-element.33.gain_ref, f32[128,1024]{1,0:T(8,128)S(1)} %get-tuple-element.34.base_ref, ...), custom_call_target="tpu_custom_call" | custom-call | flops 134217728 | tf_op jit(solution)/shard_map/pallas_call | solution.py:33
  19.4 0.0 collective-permute-done.5.refs_1_
  19.4 1.5 %collective-permute-done.6.refs_2_ = bf16[32,512]{1,0:T(8,128)(2,1)S(1)} collective-permute-done((bf16[32,512]{1,0:T(8,128)(2,1)S(1)}, bf16[32,512]{1,0:T(8,128)(2,1)S(1)}, u32[]{:S(2)}, u32[]{:S(2)}) %collective-permute-start.6) | collective-permute-done | bytes 32800 | tf_op jit(solution)/shard_map/ppermute | solution.py:204
  20.8 1.0 %collective-permute-done.7.refs_3_ = bf16[32,512]{1,0:T(8,128)(2,1)S(1)} collective-permute-done((bf16[32,512]{1,0:T(8,128)(2,1)S(1)}, bf16[32,512]{1,0:T(8,128)(2,1)S(1)}, u32[]{:S(2)}, u32[]{:S(2)}) %collective-permute-start.7) | collective-permute-done | bytes 32800 | tf_op jit(solution)/shard_map/ppermute | solution.py:204
  21.8 0.2 shard_map.112
  22.0 0.9 %collective-permute-start.8 = (bf16[128,256]{1,0:T(8,128)(2,1)S(1)}, bf16[128,256]{1,0:T(8,128)(2,1)S(1)}, u32[]{:S(2)}, u32[]{:S(2)}) collective-permute-start(bf16[128,256]{1,0:T(8,128)(2,1)S(1)} %get-tuple-element.45), channel_id=1, source_target_pairs={{0,2},{1,3},{2,0},{3,1},{4,6},{5,7},{6,4},{7,5},{8,10},{9,11},{10,... | collective-permute-start | bytes 196616 | tf_op jit(solution)/shard_map/ppermute | solution.py:207
  22.9 0.4 %shard_map.113.fixed_ref = f32[128,1024]{1,0:T(8,128)S(1)} custom-call(f32[128,1024]{1,0:T(8,128)S(1)} %get-tuple-element.38.fixed_ref, bf16[512,256]{1,0:T(8,128)(2,1)S(1)} %get-tuple-element.39.reach_ref, bf16[256,1024]{1,0:T(8,128)(2,1)S(1)} %get-tuple-element.33.gain_ref, bf16[128,512]{1,0:T(8,128)(2,1)S(1)} %get-tuple-element.43.top_ref), custom_call_target="tpu_custom_call" | custom-call | tf_op jit(solution)/shard_map/pallas_call | solution.py:33
  23.3 3.0 %collective-permute-done.8.arrived_ref = bf16[128,256]{1,0:T(8,128)(2,1)S(1)} collective-permute-done((bf16[128,256]{1,0:T(8,128)(2,1)S(1)}, bf16[128,256]{1,0:T(8,128)(2,1)S(1)}, u32[]{:S(2)}, u32[]{:S(2)}) %collective-permute-start.8) | collective-permute-done | bytes 65568 | tf_op jit(solution)/shard_map/ppermute | solution.py:207
  26.4 0.9 %shard_map.114 = (bf16[128,1024]{1,0:T(8,128)(2,1)}, bf16[32,512]{1,0:T(8,128)(2,1)}) custom-call(f32[128,1024]{1,0:T(8,128)S(1)} %shard_map.113.fixed_ref, bf16[256,1024]{1,0:T(8,128)(2,1)S(1)} %get-tuple-element.44.slope_ref, bf16[128,256]{1,0:T(8,128)(2,1)S(1)} %collective-permute-done.8.arrived_ref, bf16[32,512]{1,0:T(8,128)(2,1)S(1)} %shard_map.111.refs_0_.top_ref), custom_call_target="tpu_custom_call" | custom-call | tf_op jit(solution)/shard_map/pallas_call | solution.py:33
Async XLA Ops:
  1.8 4.9 %collective-permute-start = (bf16[32,512]{1,0:T(8,128)(2,1)S(1)}, bf16[32,512]{1,0:T(8,128)(2,1)S(1)}, u32[]{:S(2)}, u32[]{:S(2)}) collective-permute-start(bf16[32,512]{1,0:T(8,128)(2,1)S(1)} %get-tuple-element.29.held_ref), channel_id=1, source_target_pairs={{0,4},{4,0},{8,12},{12,8},{16,20},{20,16},{24,28},{28,24},{1,5},{5... | collective-permute-start | bytes 98312 | tf_op jit(solution)/shard_map/ppermute | solution.py:210
  4.8 9.7 %collective-permute-start.2 = (bf16[1024,256]{1,0:T(8,128)(2,1)}, bf16[1024,256]{1,0:T(8,128)(2,1)S(1)}, u32[]{:S(2)}, u32[]{:S(2)}) collective-permute-start(bf16[1024,256]{1,0:T(8,128)(2,1)} %param.16), channel_id=1, source_target_pairs={{0,3},{1,0},{2,1},{3,2},{4,7},{5,4},{6,5},{7,6},{8,11},{9,8},{10,9... | collective-permute-start | bytes 1572872 | tf_op jit(solution)/shard_map/ppermute | solution.py:207
  7.1 4.4 %collective-permute-start.1 = (bf16[32,512]{1,0:T(8,128)(2,1)S(1)}, bf16[32,512]{1,0:T(8,128)(2,1)S(1)}, u32[]{:S(2)}, u32[]{:S(2)}) collective-permute-start(bf16[32,512]{1,0:T(8,128)(2,1)S(1)} %shard_map.106.held_ref), channel_id=1, source_target_pairs={{0,8},{4,12},{8,0},{12,4},{16,24},{20,28},{24,16},{28,20},{1,9},{5... | collective-permute-start | bytes 98312 | tf_op jit(solution)/shard_map/ppermute | solution.py:210
  11.5 3.0 %copy-start = (s32[1,256]{1,0:T(1,128)S(1)}, s32[1,256]{1,0:T(1,128)}, u32[]{:S(2)}) copy-start(s32[1,256]{1,0:T(1,128)} %rows_ref.1) | copy-start | bytes 3076
  11.8 4.8 %collective-permute-start.4 = (bf16[32,512]{1,0:T(8,128)(2,1)S(1)}, bf16[32,512]{1,0:T(8,128)(2,1)S(1)}, u32[]{:S(2)}, u32[]{:S(2)}) collective-permute-start(bf16[32,512]{1,0:T(8,128)(2,1)S(1)} %shard_map.108.held_ref), channel_id=1, source_target_pairs={{0,16},{4,20},{8,24},{12,28},{16,0},{20,4},{24,8},{28,12},{1,17},{... | collective-permute-start | bytes 98312 | tf_op jit(solution)/shard_map/ppermute | solution.py:210
  14.9 3.8 %collective-permute-start.3 = (bf16[416,256]{1,0:T(8,128)(2,1)S(1)}, bf16[416,256]{1,0:T(8,128)(2,1)S(1)}, u32[]{:S(2)}, u32[]{:S(2)}) collective-permute-start(bf16[416,256]{1,0:T(8,128)(2,1)S(1)} %shard_map.109.block_ref), channel_id=1, source_target_pairs={{0,1},{1,0},{2,3},{3,2},{4,5},{5,4},{6,7},{7,6},{8,9},{9,8},{10,11... | collective-permute-start | bytes 638984 | tf_op jit(solution)/shard_map/ppermute | solution.py:204
  16.8 2.5 %collective-permute-start.5 = (bf16[32,512]{1,0:T(8,128)(2,1)S(1)}, bf16[32,512]{1,0:T(8,128)(2,1)S(1)}, u32[]{:S(2)}, u32[]{:S(2)}) collective-permute-start(bf16[32,512]{1,0:T(8,128)(2,1)S(1)} %shard_map.111.refs_0_.top_ref), channel_id=1, source_target_pairs={{0,1},{1,0},{2,3},{3,2},{4,5},{5,4},{6,7},{7,6},{8,9},{9,8},{10,11... | collective-permute-start | bytes 98312 | tf_op jit(solution)/shard_map/ppermute | solution.py:204
  16.8 4.0 %collective-permute-start.6 = (bf16[32,512]{1,0:T(8,128)(2,1)S(1)}, bf16[32,512]{1,0:T(8,128)(2,1)S(1)}, u32[]{:S(2)}, u32[]{:S(2)}) collective-permute-start(bf16[32,512]{1,0:T(8,128)(2,1)S(1)} %shard_map.111.refs_0_.top_ref), channel_id=1, source_target_pairs={{0,2},{1,3},{2,0},{3,1},{4,6},{5,7},{6,4},{7,5},{8,10},{9,11},{10,... | collective-permute-start | bytes 98312 | tf_op jit(solution)/shard_map/ppermute | solution.py:204
  18.5 3.3 %collective-permute-start.7 = (bf16[32,512]{1,0:T(8,128)(2,1)S(1)}, bf16[32,512]{1,0:T(8,128)(2,1)S(1)}, u32[]{:S(2)}, u32[]{:S(2)}) collective-permute-start(bf16[32,512]{1,0:T(8,128)(2,1)S(1)} %shard_map.111.refs_0_.top_ref), channel_id=1, source_target_pairs={{0,3},{1,2},{2,1},{3,0},{4,7},{5,6},{6,5},{7,4},{8,11},{9,10},{10,... | collective-permute-start | bytes 98312 | tf_op jit(solution)/shard_map/ppermute | solution.py:204
  22.0 4.3 %collective-permute-start.8 = (bf16[128,256]{1,0:T(8,128)(2,1)S(1)}, bf16[128,256]{1,0:T(8,128)(2,1)S(1)}, u32[]{:S(2)}, u32[]{:S(2)}) collective-permute-start(bf16[128,256]{1,0:T(8,128)(2,1)S(1)} %get-tuple-element.45), channel_id=1, source_target_pairs={{0,2},{1,3},{2,0},{3,1},{4,6},{5,7},{6,4},{7,5},{8,10},{9,11},{10,... | collective-permute-start | bytes 196616 | tf_op jit(solution)/shard_map/ppermute | solution.py:207

commit v5 on v4

--- a/solution.py
+++ b/solution.py
@@ -23,7 +23,7 @@
     return jnp.where(rows == columns, 1.0, 0.0).astype(BF16)
 
 
-def kernel_call(kernel, outs, scratch, operands, flops=0, remote=()):
+def kernel_call(kernel, outs, scratch, operands, flops=0, remote=(), aliases=None):
     vmem, hbm = pl.BlockSpec(memory_space=pltpu.VMEM), pl.BlockSpec(memory_space=pltpu.HBM)
     shapes = [
         pltpu.VMEM(shape, dtype) if inside else jax.ShapeDtypeStruct(shape, dtype)
@@ -37,26 +37,35 @@
         out_specs=[vmem if inside else hbm for _, _, inside in outs],
         scratch_shapes=scratch,
         compiler_params=pltpu.CompilerParams(vmem_limit_bytes=24 * 1024 * 1024),
+        input_output_aliases=aliases or {},
         cost_estimate=pl.CostEstimate(flops=flops, bytes_accessed=0, transcendentals=0),
     )(*placed, *[pltpu.with_memory_space_constraint(x, pltpu.HBM) for x in remote])
 
 
-def shuffle_kernel(source_hbm, order_hbm, own_hbm, cross_hbm, out_ref, order_ref, own_ref, cross_ref, source, sems):
-    pairs = [(order_hbm, order_ref), (source_hbm, source), (own_hbm, own_ref), (cross_hbm, cross_ref)]
-    copies = [pltpu.make_async_copy(a, b, sems.at[i]) for i, (a, b) in enumerate(pairs)]
+def shuffle_kernel(source_hbm, order_hbm, out_ref, order_ref, source, sems):
+    copies = [
+        pltpu.make_async_copy(order_hbm, order_ref, sems.at[0]),
+        pltpu.make_async_copy(source_hbm, source, sems.at[1]),
+    ]
     for copy in copies:
         copy.start()
     copies[0].wait()
     pick = picker(order_ref[0], source.shape[1])
     copies[1].wait()
     out_ref[...] = dot(source[...], pick).astype(BF16)
-    copies[2].wait()
-    copies[3].wait()
-
-
-def pick_kernel(order_ref, pick_ref):
+
+
+def pick_kernel(order_ref, own_hbm, cross_hbm, pick_ref, own_ref, cross_ref, sems):
+    copies = [
+        pltpu.make_async_copy(own_hbm, own_ref, sems.at[0]),
+        pltpu.make_async_copy(cross_hbm, cross_ref, sems.at[1]),
+    ]
+    for copy in copies:
+        copy.start()
     for level in range(pick_ref.shape[0]):
         pick_ref[level] = picker(order_ref[level + 1], pick_ref.shape[1])
+    for copy in copies:
+        copy.wait()
 
 
 def panel_kernel(write_hbm, inverse_hbm, source_hbm, gain_ref, base_ref, left, inverse, sems):
@@ -153,7 +162,7 @@
     *slabs, top_ref, pass_ref, wide = refs
     rows = slabs[0].shape[0]
     place = lax.axis_index("fr")
-    for flip, slab in enumerate(slabs):
+    for flip, slab in enumerate(reversed(slabs)):
         start = pl.multiple_of(jnp.bitwise_xor(place, flip) * rows, rows)
         wide[pl.ds(start, rows), :] = slab[...].astype(F32)
     top = wide[...].astype(BF16)
@@ -161,25 +170,37 @@
     pass_ref[...] = (hop_fixed_ref[...] + dot(top, hop_ref[...])).astype(BF16)
 
 
-def link_kernel(fixed_ref, reach_ref, gain_ref, top_ref, out_ref):
-    link = dot(top_ref[...], reach_ref[...]).astype(BF16)
-    out_ref[...] = fixed_ref[...] - dot(link, gain_ref[...])
-
-
-def final_kernel(fixed_ref, slope_ref, arrived_ref, top_ref, out_hbm, top_hbm, held, sems):
-    first = pltpu.make_async_copy(top_ref, top_hbm, sems.at[0])
-    first.start()
-    arrived = jnp.where(lax.axis_index("fr") >= 2, arrived_ref[...].astype(F32), 0.0).astype(BF16)
-    parts = sems.shape[0] - 1
+def written(out_hbm, held, sems, part):
+    parts = sems.shape[0]
     width = held.shape[1] // parts
-    copies = [first]
-    for part in range(parts):
-        cut = pl.ds(part * width, width)
-        held[:, cut] = (fixed_ref[:, cut] - dot(arrived, slope_ref[:, cut])).astype(BF16)
-        copies.append(pltpu.make_async_copy(held.at[:, cut], out_hbm.at[:, cut], sems.at[part + 1]))
+    copies = []
+    for index in range(parts):
+        cut = pl.ds(index * width, width)
+        held[:, cut] = part(cut).astype(BF16)
+        copies.append(pltpu.make_async_copy(held.at[:, cut], out_hbm.at[:, cut], sems.at[index]))
         copies[-1].start()
     for copy in copies:
         copy.wait()
+
+
+def link_kernel(fixed_ref, reach_ref, gain_ref, whole_ref, top_ref, ready_ref, out_hbm, top_hbm, held, sems, top_sem):
+    copy = pltpu.make_async_copy(top_ref, top_hbm, top_sem)
+    copy.start()
+    link = dot(whole_ref[...], reach_ref[...]).astype(BF16)
+    ready_ref[...] = fixed_ref[...] - dot(link, gain_ref[...])
+
+    @pl.when(lax.axis_index("fr") < 2)
+    def _():
+        written(out_hbm, held, sems, lambda cut: ready_ref[:, cut])
+
+    copy.wait()
+
+
+def final_kernel(ready_ref, slope_ref, arrived_ref, solved_hbm, out_hbm, held, sems):
+    @pl.when(lax.axis_index("fr") >= 2)
+    def _():
+        arrived = arrived_ref[...]
+        written(out_hbm, held, sems, lambda cut: ready_ref[:, cut] - dot(arrived, slope_ref[:, cut]))
 
 
 def body(
@@ -209,23 +230,26 @@
     def swapped(array, mask):
         return lax.ppermute(array, "bf", [(g, g ^ mask) for g in range(groups)])
 
-    held, order, own, cross = kernel_call(
+    held, order = kernel_call(
         shuffle_kernel,
+        [((rows, top_rows), BF16, True), (level_ordering.shape, jnp.int32, True)],
+        [pltpu.VMEM((rows, top_rows), BF16), pltpu.SemaphoreType.DMA((2,))],
+        [],
+        remote=[top_source, level_ordering],
+    )
+    swap = swapped(held, 1)
+    coupling_read, order = lax.optimization_barrier((coupling_read, order))
+    next_read = turned(coupling_read, -1)
+    pick, own, cross = kernel_call(
+        pick_kernel,
         [
-            ((rows, top_rows), BF16, True),
-            (level_ordering.shape, jnp.int32, True),
+            ((levels - 1, top_rows, top_rows), BF16, True),
             (butterfly_own.shape, BF16, True),
             (butterfly_cross.shape, BF16, True),
         ],
-        [pltpu.VMEM((rows, top_rows), BF16), pltpu.SemaphoreType.DMA((4,))],
-        [],
-        remote=[top_source, level_ordering, butterfly_own, butterfly_cross],
-    )
-    swap = swapped(held, 1)
-    coupling_read, order = lax.optimization_barrier((coupling_read, order))
-    next_read = turned(coupling_read, -1)
-    (pick,) = kernel_call(
-        pick_kernel, [((levels - 1, top_rows, top_rows), BF16, True)], [], [order]
+        [pltpu.SemaphoreType.DMA((2,))],
+        [order],
+        remote=[butterfly_own, butterfly_cross],
     )
 
     panel_inverse, swap = lax.optimization_barrier((panel_inverse, swap))
@@ -281,7 +305,7 @@
         [own, cross, held, swap],
         LEVEL_COST,
     )
-    slabs = [top] + [flipped(top, mask) for mask in range(1, chain)]
+    slabs = [flipped(top, mask) for mask in range(chain - 1, 0, -1)] + [top]
     whole, passed = kernel_call(
         pass_kernel,
         [((vectors, top_rows), BF16, True), ((vectors, rank), BF16, True)],
@@ -293,14 +317,20 @@
         here = jnp.where(lax.axis_index("fr") >= 2, turned(passed, 2), 0)
         passed = (start.astype(F32) + dot(here, hop_slope[0])).astype(BF16)
     arrived = turned(passed, 2)
-    (ready,) = kernel_call(
-        link_kernel, [((vectors, panel), F32, True)], [], [fixed, reach, gain, whole]
-    )
-    solved, top = kernel_call(
+    staging = [pltpu.VMEM((vectors, panel), BF16), pltpu.SemaphoreType.DMA((4,))]
+    ready, solved, top = kernel_call(
+        link_kernel,
+        [((vectors, panel), F32, True), ((vectors, panel), BF16, False), ((rows, top_rows), BF16, False)],
+        [*staging, pltpu.SemaphoreType.DMA],
+        [fixed, reach, gain, whole, top],
+    )
+    (solved,) = kernel_call(
         final_kernel,
-        [((vectors, panel), BF16, False), ((rows, top_rows), BF16, False)],
-        [pltpu.VMEM((vectors, panel), BF16), pltpu.SemaphoreType.DMA((5,))],
-        [ready, slope, arrived, top],
+        [((vectors, panel), BF16, False)],
+        staging,
+        [ready, slope, arrived],
+        remote=[solved],
+        aliases={3: 0},
     )
     return (top, solved)
 

time: 27.5 us -> 25.7 us (0.935)
  waiting for transfers between devices: 8.23 us -> 5 us
  starting transfers between devices: 11.3 us -> 12.1 us
  Pallas kernels: 7.04 us -> 7.68 us
    ppermute x2, waiting for transfers between devices: 3.05 us -> 1.69 us  [turned(): lax.ppermute(array, 'fr', [(i, (i + by) % chain) for i in range(chain)])]
    ppermute x3, waiting for transfers between devices: 2.72 us -> 1.77 us  [swapped(): return lax.ppermute(array, 'bf', [(g, g ^ mask) for g in range(groups)])]
    ppermute x4, waiting for transfers between devices: 2.47 us -> 1.54 us  [flipped(): return lax.ppermute(array, 'fr', [(i, i ^ mask) for i in range(chain)])]
    ppermute x2, starting transfers between devices: 1.54 us -> 2.33 us  [turned(): lax.ppermute(array, 'fr', [(i, (i + by) % chain) for i in range(chain)])]
    pallas_call x11, Pallas kernels: 7.04 us -> 7.68 us  [kernel_call(): pl.pallas_call(kernel, out_shape=shapes, in_specs=[vmem] * len(placed) +...]
  transfers between devices with their start and end apart: 9 -> 9, of which waited for: 5 -> 5; matrix products, arithmetic and copies ran while one was open for 0% -> 0% of each run, Pallas kernels for 17% -> 25%
where the time goes in v5:
time: 25.7 us; the launch traced here: 25.5 us
  starting transfers between devices  12.1 us (47%)
  Pallas kernels  7.68 us (30%)
  waiting for transfers between devices  5 us (19%)
  between operations  0.73 us (3%)
    ppermute x3, starting transfers between devices, swapped(): return lax.ppermute(array, 'bf', [(g, g ^ mask) for g in range(groups)])  7.8 us
    pallas_call x11, Pallas kernels, kernel_call(): pl.pallas_call(kernel, out_shape=shapes, in_specs=[vmem] * len(placed) +...  7.68 us
    ppermute x2, starting transfers between devices, turned(): lax.ppermute(array, 'fr', [(i, (i + by) % chain) for i in range(chain)])  2.33 us
    ppermute x4, starting transfers between devices, flipped(): return lax.ppermute(array, 'fr', [(i, i ^ mask) for i in range(chain)])  1.94 us
    ppermute x3, waiting for transfers between devices, swapped(): return lax.ppermute(array, 'bf', [(g, g ^ mask) for g in range(groups)])  1.77 us
    ppermute x2, waiting for transfers between devices, turned(): lax.ppermute(array, 'fr', [(i, (i + by) % chain) for i in range(chain)])  1.69 us
    ppermute x4, waiting for transfers between devices, flipped(): return lax.ppermute(array, 'fr', [(i, i ^ mask) for i in range(chain)])  1.54 us
  transfers between devices with their start and end apart: 9, of which 5 were waited for; matrix products, arithmetic and copies ran while one was open for 0% of the time, Pallas kernels for 25%

profile of v5, /device:TPU:0, one launch (start us, length us, event | category | flops | bytes accessed | tf_op | source)
XLA Modules:
  0.0 25.5 jit_solution(13757881290881258783)
XLA Ops:
  0.6 1.0 %shard_map.104 = (bf16[32,512]{1,0:T(8,128)(2,1)S(1)}, s32[3,1,512]{2,1,0:T(1,128)S(1)}) custom-call(bf16[32,512]{1,0:T(8,128)(2,1)} %source_hbm.2, s32[3,1,512]{2,1,0:T(1,128)} %order_hbm.1), custom_call_target="tpu_custom_call" | custom-call | tf_op jit(solution)/shard_map/pallas_call | solution.py:33
  1.7 3.0 %collective-permute-start = (bf16[32,512]{1,0:T(8,128)(2,1)S(1)}, bf16[32,512]{1,0:T(8,128)(2,1)S(1)}, u32[]{:S(2)}, u32[]{:S(2)}) collective-permute-start(bf16[32,512]{1,0:T(8,128)(2,1)S(1)} %get-tuple-element.32.held_ref), channel_id=1, source_target_pairs={{0,4},{4,0},{8,12},{12,8},{16,20},{20,16},{24,28},{28,24},{1,5},{5... | collective-permute-start | bytes 98312 | tf_op jit(solution)/shard_map/ppermute | solution.py:231
  4.7 0.7 %collective-permute-start.2 = (bf16[1024,256]{1,0:T(8,128)(2,1)}, bf16[1024,256]{1,0:T(8,128)(2,1)S(1)}, u32[]{:S(2)}, u32[]{:S(2)}) collective-permute-start(bf16[1024,256]{1,0:T(8,128)(2,1)} %param.16), channel_id=1, source_target_pairs={{0,3},{1,0},{2,1},{3,2},{4,7},{5,4},{6,5},{7,6},{8,11},{9,8},{10,9... | collective-permute-start | bytes 1572872 | tf_op jit(solution)/shard_map/ppermute | solution.py:228
  5.4 1.1 %shard_map.105 = (bf16[2,512,512]{2,1,0:T(8,128)(2,1)S(1)}, bf16[3,256,256]{2,1,0:T(8,128)(2,1)S(1)}, bf16[3,256,256]{2,1,0:T(8,128)(2,1)S(1)}) custom-call(s32[3,1,512]{2,1,0:T(1,128)S(1)} %get-tuple-element.28.order_ref, bf16[3,256,256]{2,1,0:T(8,128)(2,1)} %own_hbm.1, bf16[3,256,256]{2,1,0:T(8,128)(2,1)} %cross_hbm.1), custom_call_target="tpu_custom_call" | custom-call | tf_op jit(solution)/shard_map/pallas_call | solution.py:33
  6.5 0.1 collective-permute-done.swap_ref
  6.6 0.3 %shard_map.106.held_ref = bf16[32,512]{1,0:T(8,128)(2,1)S(1)} custom-call(bf16[2,512,512]{2,1,0:T(8,128)(2,1)S(1)} %get-tuple-element.29.pick_ref, bf16[3,256,256]{2,1,0:T(8,128)(2,1)S(1)} %get-tuple-element.30.own_ref, bf16[3,256,256]{2,1,0:T(8,128)(2,1)S(1)} %get-tuple-element.31.cross_ref, bf16[32,512]{1,0:T(8,128)(2,1)S(1)} %get-tuple-element.32.held_ref, ...), custom_call_target="tpu_custom_call" | custom-call | flops 4000000000 | tf_op jit(solution)/shard_map/pallas_call | solution.py:33
  6.9 2.1 %collective-permute-start.1 = (bf16[32,512]{1,0:T(8,128)(2,1)S(1)}, bf16[32,512]{1,0:T(8,128)(2,1)S(1)}, u32[]{:S(2)}, u32[]{:S(2)}) collective-permute-start(bf16[32,512]{1,0:T(8,128)(2,1)S(1)} %shard_map.106.held_ref), channel_id=1, source_target_pairs={{0,8},{4,12},{8,0},{12,4},{16,24},{20,28},{24,16},{28,20},{1,9},{5... | collective-permute-start | bytes 98312 | tf_op jit(solution)/shard_map/ppermute | solution.py:231
  9.0 2.2 %shard_map.107 = (bf16[256,1024]{1,0:T(8,128)(2,1)S(1)}, f32[128,1024]{1,0:T(8,128)S(1)}) custom-call(bf16[256,1024]{1,0:T(8,128)(2,1)} %write_hbm.1, bf16[1024,1024]{1,0:T(8,128)(2,1)} %inverse_hbm, bf16[128,1024]{1,0:T(8,128)(2,1)} %source_hbm.3), custom_call_target="tpu_custom_call" | custom-call | flops 1000000000 | tf_op jit(solution)/shard_map/pallas_call | solution.py:33
  11.3 0.0 collective-permute-done.1.swap_ref
  11.3 0.0 copy-start
  11.3 0.3 %shard_map.108.held_ref = bf16[32,512]{1,0:T(8,128)(2,1)S(1)} custom-call(bf16[2,512,512]{2,1,0:T(8,128)(2,1)S(1)} %get-tuple-element.29.pick_ref, bf16[3,256,256]{2,1,0:T(8,128)(2,1)S(1)} %get-tuple-element.30.own_ref, bf16[3,256,256]{2,1,0:T(8,128)(2,1)S(1)} %get-tuple-element.31.cross_ref, bf16[32,512]{1,0:T(8,128)(2,1)S(1)} %shard_map.106.held_ref, ...), custom_call_target="tpu_custom_call" | custom-call | flops 4000000000 | tf_op jit(solution)/shard_map/pallas_call | solution.py:33
  11.7 2.7 %collective-permute-start.4 = (bf16[32,512]{1,0:T(8,128)(2,1)S(1)}, bf16[32,512]{1,0:T(8,128)(2,1)S(1)}, u32[]{:S(2)}, u32[]{:S(2)}) collective-permute-start(bf16[32,512]{1,0:T(8,128)(2,1)S(1)} %shard_map.108.held_ref), channel_id=1, source_target_pairs={{0,16},{4,20},{8,24},{12,28},{16,0},{20,4},{24,8},{28,12},{1,17},{... | collective-permute-start | bytes 98312 | tf_op jit(solution)/shard_map/ppermute | solution.py:231
  14.3 0.0 collective-permute-done.2.read_ref
  14.3 0.0 copy-done
  14.3 0.4 %shard_map.109.block_ref = bf16[416,256]{1,0:T(8,128)(2,1)S(1)} custom-call(bf16[256,1024]{1,0:T(8,128)(2,1)S(1)} %get-tuple-element.36.gain_ref, f32[128,1024]{1,0:T(8,128)S(1)} %get-tuple-element.37.base_ref, bf16[1024,256]{1,0:T(8,128)(2,1)S(1)} %collective-permute-done.2.read_ref, s32[1,256]{1,0:T(1,128)S(1)} %copy-done), custom_call_target="tpu_custom_call" | custom-call | flops 201326592 | tf_op jit(solution)/shard_map/pallas_call | solution.py:33
  14.7 0.1 collective-permute-start.3
  14.8 1.7 %collective-permute-done.4.swap_ref = bf16[32,512]{1,0:T(8,128)(2,1)S(1)} collective-permute-done((bf16[32,512]{1,0:T(8,128)(2,1)S(1)}, bf16[32,512]{1,0:T(8,128)(2,1)S(1)}, u32[]{:S(2)}, u32[]{:S(2)}) %collective-permute-start.4) | collective-permute-done | bytes 32800 | tf_op jit(solution)/shard_map/ppermute | solution.py:231
  16.5 0.2 shard_map.111.refs_3_.top_ref
  16.7 0.0 collective-permute-start.5
  16.7 1.6 %collective-permute-start.6 = (bf16[32,512]{1,0:T(8,128)(2,1)S(1)}, bf16[32,512]{1,0:T(8,128)(2,1)S(1)}, u32[]{:S(2)}, u32[]{:S(2)}) collective-permute-start(bf16[32,512]{1,0:T(8,128)(2,1)S(1)} %shard_map.111.refs_3_.top_ref), channel_id=1, source_target_pairs={{0,2},{1,3},{2,0},{3,1},{4,6},{5,7},{6,4},{7,5},{8,10},{9,11},{10,... | collective-permute-start | bytes 98312 | tf_op jit(solution)/shard_map/ppermute | solution.py:225
  18.3 0.2 collective-permute-start.7
  18.6 0.0 collective-permute-done.3.other_ref
  18.6 0.6 %shard_map.110 = (f32[128,1024]{1,0:T(8,128)S(1)}, bf16[512,256]{1,0:T(8,128)(2,1)S(1)}, bf16[256,1024]{1,0:T(8,128)(2,1)S(1)}, f32[128,256]{1,0:T(8,128)S(1)}, bf16[512,256]{1,0:T(8,128)(2,1)S(1)}) custom-call(bf16[256,1024]{1,0:T(8,128)(2,1)S(1)} %get-tuple-element.36.gain_ref, f32[128,1024]{1,0:T(8,128)S(1)} %get-tuple-element.37.base_ref, ...), custom_call_target="tpu_custom_call" | custom-call | flops 134217728 | tf_op jit(solution)/shard_map/pallas_call | solution.py:33
  19.2 1.0 %collective-permute-done.5.refs_0_ = bf16[32,512]{1,0:T(8,128)(2,1)S(1)} collective-permute-done((bf16[32,512]{1,0:T(8,128)(2,1)S(1)}, bf16[32,512]{1,0:T(8,128)(2,1)S(1)}, u32[]{:S(2)}, u32[]{:S(2)}) %collective-permute-start.5) | collective-permute-done | bytes 32800 | tf_op jit(solution)/shard_map/ppermute | solution.py:225
  20.3 0.5 %collective-permute-done.6.refs_1_ = bf16[32,512]{1,0:T(8,128)(2,1)S(1)} collective-permute-done((bf16[32,512]{1,0:T(8,128)(2,1)S(1)}, bf16[32,512]{1,0:T(8,128)(2,1)S(1)}, u32[]{:S(2)}, u32[]{:S(2)}) %collective-permute-start.6) | collective-permute-done | bytes 32800 | tf_op jit(solution)/shard_map/ppermute | solution.py:225
  20.7 0.0 collective-permute-done.7.refs_2_
  20.7 0.2 shard_map.112
  20.9 1.6 %collective-permute-start.8 = (bf16[128,256]{1,0:T(8,128)(2,1)S(1)}, bf16[128,256]{1,0:T(8,128)(2,1)S(1)}, u32[]{:S(2)}, u32[]{:S(2)}) collective-permute-start(bf16[128,256]{1,0:T(8,128)(2,1)S(1)} %get-tuple-element.50), channel_id=1, source_target_pairs={{0,2},{1,3},{2,0},{3,1},{4,6},{5,7},{6,4},{7,5},{8,10},{9,11},{10,... | collective-permute-start | bytes 196616 | tf_op jit(solution)/shard_map/ppermute | solution.py:228
  22.6 1.2 %shard_map.113 = (f32[128,1024]{1,0:T(8,128)S(1)}, bf16[128,1024]{1,0:T(8,128)(2,1)}, bf16[32,512]{1,0:T(8,128)(2,1)}) custom-call(f32[128,1024]{1,0:T(8,128)S(1)} %get-tuple-element.41.fixed_ref, bf16[512,256]{1,0:T(8,128)(2,1)S(1)} %get-tuple-element.42.reach_ref, bf16[256,1024]{1,0:T(8,128)(2,1)S(1)} %get-tuple-element.36.gain_ref, ...), custom_call_target="tpu_custom_call" | custom-call | tf_op jit(solution)/shard_map/pallas_call | solution.py:33
  23.8 1.7 %collective-permute-done.8.arrived_ref = bf16[128,256]{1,0:T(8,128)(2,1)S(1)} collective-permute-done((bf16[128,256]{1,0:T(8,128)(2,1)S(1)}, bf16[128,256]{1,0:T(8,128)(2,1)S(1)}, u32[]{:S(2)}, u32[]{:S(2)}) %collective-permute-start.8) | collective-permute-done | bytes 65568 | tf_op jit(solution)/shard_map/ppermute | solution.py:228
  (1 shorter events, 0.0 us)
Async XLA Ops:
  1.7 4.9 %collective-permute-start = (bf16[32,512]{1,0:T(8,128)(2,1)S(1)}, bf16[32,512]{1,0:T(8,128)(2,1)S(1)}, u32[]{:S(2)}, u32[]{:S(2)}) collective-permute-start(bf16[32,512]{1,0:T(8,128)(2,1)S(1)} %get-tuple-element.32.held_ref), channel_id=1, source_target_pairs={{0,4},{4,0},{8,12},{12,8},{16,20},{20,16},{24,28},{28,24},{1,5},{5... | collective-permute-start | bytes 98312 | tf_op jit(solution)/shard_map/ppermute | solution.py:231
  4.7 9.7 %collective-permute-start.2 = (bf16[1024,256]{1,0:T(8,128)(2,1)}, bf16[1024,256]{1,0:T(8,128)(2,1)S(1)}, u32[]{:S(2)}, u32[]{:S(2)}) collective-permute-start(bf16[1024,256]{1,0:T(8,128)(2,1)} %param.16), channel_id=1, source_target_pairs={{0,3},{1,0},{2,1},{3,2},{4,7},{5,4},{6,5},{7,6},{8,11},{9,8},{10,9... | collective-permute-start | bytes 1572872 | tf_op jit(solution)/shard_map/ppermute | solution.py:228
  6.9 4.4 %collective-permute-start.1 = (bf16[32,512]{1,0:T(8,128)(2,1)S(1)}, bf16[32,512]{1,0:T(8,128)(2,1)S(1)}, u32[]{:S(2)}, u32[]{:S(2)}) collective-permute-start(bf16[32,512]{1,0:T(8,128)(2,1)S(1)} %shard_map.106.held_ref), channel_id=1, source_target_pairs={{0,8},{4,12},{8,0},{12,4},{16,24},{20,28},{24,16},{28,20},{1,9},{5... | collective-permute-start | bytes 98312 | tf_op jit(solution)/shard_map/ppermute | solution.py:231
  11.3 3.0 %copy-start = (s32[1,256]{1,0:T(1,128)S(1)}, s32[1,256]{1,0:T(1,128)}, u32[]{:S(2)}) copy-start(s32[1,256]{1,0:T(1,128)} %rows_ref.1) | copy-start | bytes 3076
  11.7 4.8 %collective-permute-start.4 = (bf16[32,512]{1,0:T(8,128)(2,1)S(1)}, bf16[32,512]{1,0:T(8,128)(2,1)S(1)}, u32[]{:S(2)}, u32[]{:S(2)}) collective-permute-start(bf16[32,512]{1,0:T(8,128)(2,1)S(1)} %shard_map.108.held_ref), channel_id=1, source_target_pairs={{0,16},{4,20},{8,24},{12,28},{16,0},{20,4},{24,8},{28,12},{1,17},{... | collective-permute-start | bytes 98312 | tf_op jit(solution)/shard_map/ppermute | solution.py:231
  14.7 3.8 %collective-permute-start.3 = (bf16[416,256]{1,0:T(8,128)(2,1)S(1)}, bf16[416,256]{1,0:T(8,128)(2,1)S(1)}, u32[]{:S(2)}, u32[]{:S(2)}) collective-permute-start(bf16[416,256]{1,0:T(8,128)(2,1)S(1)} %shard_map.109.block_ref), channel_id=1, source_target_pairs={{0,1},{1,0},{2,3},{3,2},{4,5},{5,4},{6,7},{7,6},{8,9},{9,8},{10,11... | collective-permute-start | bytes 638984 | tf_op jit(solution)/shard_map/ppermute | solution.py:225
  16.7 3.6 %collective-permute-start.5 = (bf16[32,512]{1,0:T(8,128)(2,1)S(1)}, bf16[32,512]{1,0:T(8,128)(2,1)S(1)}, u32[]{:S(2)}, u32[]{:S(2)}) collective-permute-start(bf16[32,512]{1,0:T(8,128)(2,1)S(1)} %shard_map.111.refs_3_.top_ref), channel_id=1, source_target_pairs={{0,3},{1,2},{2,1},{3,0},{4,7},{5,6},{6,5},{7,4},{8,11},{9,10},{10,... | collective-permute-start | bytes 98312 | tf_op jit(solution)/shard_map/ppermute | solution.py:225
  16.7 4.0 %collective-permute-start.6 = (bf16[32,512]{1,0:T(8,128)(2,1)S(1)}, bf16[32,512]{1,0:T(8,128)(2,1)S(1)}, u32[]{:S(2)}, u32[]{:S(2)}) collective-permute-start(bf16[32,512]{1,0:T(8,128)(2,1)S(1)} %shard_map.111.refs_3_.top_ref), channel_id=1, source_target_pairs={{0,2},{1,3},{2,0},{3,1},{4,6},{5,7},{6,4},{7,5},{8,10},{9,11},{10,... | collective-permute-start | bytes 98312 | tf_op jit(solution)/shard_map/ppermute | solution.py:225
  18.3 2.4 %collective-permute-start.7 = (bf16[32,512]{1,0:T(8,128)(2,1)S(1)}, bf16[32,512]{1,0:T(8,128)(2,1)S(1)}, u32[]{:S(2)}, u32[]{:S(2)}) collective-permute-start(bf16[32,512]{1,0:T(8,128)(2,1)S(1)} %shard_map.111.refs_3_.top_ref), channel_id=1, source_target_pairs={{0,1},{1,0},{2,3},{3,2},{4,5},{5,4},{6,7},{7,6},{8,9},{9,8},{10,11... | collective-permute-start | bytes 98312 | tf_op jit(solution)/shard_map/ppermute | solution.py:225
  20.9 4.5 %collective-permute-start.8 = (bf16[128,256]{1,0:T(8,128)(2,1)S(1)}, bf16[128,256]{1,0:T(8,128)(2,1)S(1)}, u32[]{:S(2)}, u32[]{:S(2)}) collective-permute-start(bf16[128,256]{1,0:T(8,128)(2,1)S(1)} %get-tuple-element.50), channel_id=1, source_target_pairs={{0,2},{1,3},{2,0},{3,1},{4,6},{5,7},{6,4},{7,5},{8,10},{9,11},{10,... | collective-permute-start | bytes 196616 | tf_op jit(solution)/shard_map/ppermute | solution.py:228

commit v6 on v5

--- a/solution.py
+++ b/solution.py
@@ -55,20 +55,30 @@
     out_ref[...] = dot(source[...], pick).astype(BF16)
 
 
-def pick_kernel(order_ref, own_hbm, cross_hbm, pick_ref, own_ref, cross_ref, sems):
+def fold(factor, pick):
+    size = factor.shape[0]
+    pieces = [dot(factor, pick[start : start + size]) for start in range(0, pick.shape[0], size)]
+    return jnp.concatenate(pieces, axis=0).astype(BF16)
+
+
+def ready_kernel(order_ref, held_ref, own_hbm, cross_hbm, part_ref, fold_ref, own_ref, cross_ref, sems):
     copies = [
         pltpu.make_async_copy(own_hbm, own_ref, sems.at[0]),
         pltpu.make_async_copy(cross_hbm, cross_ref, sems.at[1]),
     ]
     for copy in copies:
         copy.start()
-    for level in range(pick_ref.shape[0]):
-        pick_ref[level] = picker(order_ref[level + 1], pick_ref.shape[1])
+    pick = picker(order_ref[1], held_ref.shape[1])
     for copy in copies:
         copy.wait()
-
-
-def panel_kernel(write_hbm, inverse_hbm, source_hbm, gain_ref, base_ref, left, inverse, sems):
+    part_ref[...] = dot(held_ref[...], fold(own_ref[0], pick))
+    fold_ref[...] = fold(cross_ref[0], pick)
+
+
+def panel_kernel(
+    level, order_ref, held_ref, own_ref, cross_ref, write_hbm, inverse_hbm, source_hbm,
+    part_ref, fold_ref, gain_ref, base_ref, left, inverse, sems,
+):
     rank, size = gain_ref.shape
     part = rank
     copies = [
@@ -82,6 +92,9 @@
         )
     for copy in copies:
         copy.start()
+    pick = picker(order_ref[level + 1], held_ref.shape[1])
+    part_ref[...] = dot(held_ref[...], fold(own_ref[level], pick))
+    fold_ref[...] = fold(cross_ref[level], pick)
     for copy in copies:
         copy.wait()
     for start in range(0, size, part):
@@ -115,9 +128,8 @@
     return jnp.concatenate(pieces, axis=1)
 
 
-def level_kernel(level, pick_ref, own_ref, cross_ref, held_ref, swap_ref, out_ref):
-    mix = mixed(held_ref[...], swap_ref[...], own_ref[level], cross_ref[level])
-    out_ref[...] = dot(mix.astype(BF16), pick_ref[level]).astype(BF16)
+def level_kernel(part_ref, fold_ref, swap_ref, out_ref):
+    out_ref[...] = (part_ref[...] + dot(swap_ref[...], fold_ref[...])).astype(BF16)
 
 
 def chain_kernel(
@@ -162,7 +174,7 @@
     *slabs, top_ref, pass_ref, wide = refs
     rows = slabs[0].shape[0]
     place = lax.axis_index("fr")
-    for flip, slab in enumerate(reversed(slabs)):
+    for flip, slab in enumerate(slabs):
         start = pl.multiple_of(jnp.bitwise_xor(place, flip) * rows, rows)
         wide[pl.ds(start, rows), :] = slab[...].astype(F32)
     top = wide[...].astype(BF16)
@@ -240,43 +252,36 @@
     swap = swapped(held, 1)
     coupling_read, order = lax.optimization_barrier((coupling_read, order))
     next_read = turned(coupling_read, -1)
-    pick, own, cross = kernel_call(
-        pick_kernel,
-        [
-            ((levels - 1, top_rows, top_rows), BF16, True),
-            (butterfly_own.shape, BF16, True),
-            (butterfly_cross.shape, BF16, True),
-        ],
+    ready_outs = [((rows, top_rows), F32, True), ((top_rows, top_rows), BF16, True)]
+    part, folded, own, cross = kernel_call(
+        ready_kernel,
+        [*ready_outs, (butterfly_own.shape, BF16, True), (butterfly_cross.shape, BF16, True)],
         [pltpu.SemaphoreType.DMA((2,))],
-        [order],
+        [order, held],
         remote=[butterfly_own, butterfly_cross],
     )
 
-    panel_inverse, swap = lax.optimization_barrier((panel_inverse, swap))
-    gain, base = kernel_call(
-        panel_kernel,
-        [((rank, panel), BF16, True), ((vectors, panel), F32, True)],
+    def next_level(part, folded, swap):
+        return kernel_call(
+            level_kernel, [((rows, top_rows), BF16, True)], [], [part, folded, swap], LEVEL_COST
+        )[0]
+
+    held = next_level(part, folded, swap)
+    swap = swapped(held, 2)
+    part, folded, gain, base = kernel_call(
+        functools.partial(panel_kernel, 1),
+        [*ready_outs, ((rank, panel), BF16, True), ((vectors, panel), F32, True)],
         [
             pltpu.VMEM((rank + vectors, panel), BF16),
             pltpu.VMEM((panel, panel), BF16),
             pltpu.SemaphoreType.DMA((2 + panel // rank,)),
         ],
-        [],
+        [order, held, own, cross],
         PANEL_COST,
         [coupling_write, panel_inverse, front_source],
     )
-
-    for level in range(levels - 1):
-        if level:
-            swap, gain = lax.optimization_barrier((swap, gain))
-        (held,) = kernel_call(
-            functools.partial(level_kernel, level),
-            [((rows, top_rows), BF16, True)],
-            [],
-            [pick, own, cross, held, swap],
-            LEVEL_COST,
-        )
-        swap = swapped(held, 2 ** (level + 1))
+    held = next_level(part, folded, swap)
+    swap = swapped(held, 4)
 
     next_read, held = lax.optimization_barrier((next_read, held))
     (block,) = kernel_call(
@@ -305,7 +310,7 @@
         [own, cross, held, swap],
         LEVEL_COST,
     )
-    slabs = [flipped(top, mask) for mask in range(chain - 1, 0, -1)] + [top]
+    slabs = [top] + [flipped(top, mask) for mask in range(1, chain)]
     whole, passed = kernel_call(
         pass_kernel,
         [((vectors, top_rows), BF16, True), ((vectors, rank), BF16, True)],

time: 25.7 us -> 25.6 us (level)
  starting transfers between devices: 12.1 us -> 11.4 us
  Pallas kernels: 7.68 us -> 8.24 us
    ppermute x3, starting transfers between devices: 7.8 us -> 7.2 us  [swapped(): return lax.ppermute(array, 'bf', [(g, g ^ mask) for g in range(groups)])]
    pallas_call x11, Pallas kernels: 7.68 us -> 8.24 us  [kernel_call(): pl.pallas_call(kernel, out_shape=shapes, in_specs=[vmem] * len(placed) +...]
  transfers between devices with their start and end apart: 9 -> 9, of which waited for: 5 -> 4; matrix products, arithmetic and copies ran while one was open for 0% -> 0% of each run, Pallas kernels for 25% -> 28%
where the time goes in v6:
time: 25.6 us; the launch traced here: 25.3 us
  starting transfers between devices  11.4 us (45%)
  Pallas kernels  8.24 us (32%)
  waiting for transfers between devices  4.96 us (19%)
  between operations  0.73 us (3%)
    pallas_call x11, Pallas kernels, kernel_call(): pl.pallas_call(kernel, out_shape=shapes, in_specs=[vmem] * len(placed) +...  8.24 us
    ppermute x3, starting transfers between devices, swapped(): return lax.ppermute(array, 'bf', [(g, g ^ mask) for g in range(groups)])  7.2 us
    ppermute x2, starting transfers between devices, turned(): lax.ppermute(array, 'fr', [(i, (i + by) % chain) for i in range(chain)])  2.24 us
    ppermute x4, starting transfers between devices, flipped(): return lax.ppermute(array, 'fr', [(i, i ^ mask) for i in range(chain)])  1.94 us
    ppermute x3, waiting for transfers between devices, swapped(): return lax.ppermute(array, 'bf', [(g, g ^ mask) for g in range(groups)])  1.75 us
    ppermute x2, waiting for transfers between devices, turned(): lax.ppermute(array, 'fr', [(i, (i + by) % chain) for i in range(chain)])  1.68 us
    ppermute x4, waiting for transfers between devices, flipped(): return lax.ppermute(array, 'fr', [(i, i ^ mask) for i in range(chain)])  1.54 us
  transfers between devices with their start and end apart: 9, of which 4 were waited for; matrix products, arithmetic and copies ran while one was open for 0% of the time, Pallas kernels for 28%

profile of v6, /device:TPU:0, one launch (start us, length us, event | category | flops | bytes accessed | tf_op | source)
XLA Modules:
  0.0 25.3 jit_solution(11047395373621644313)
XLA Ops:
  0.6 1.0 %shard_map.104 = (bf16[32,512]{1,0:T(8,128)(2,1)S(1)}, s32[3,1,512]{2,1,0:T(1,128)S(1)}) custom-call(bf16[32,512]{1,0:T(8,128)(2,1)} %source_hbm.2, s32[3,1,512]{2,1,0:T(1,128)} %order_hbm.1), custom_call_target="tpu_custom_call" | custom-call | tf_op jit(solution)/shard_map/pallas_call | solution.py:33
  1.7 3.0 %collective-permute-start = (bf16[32,512]{1,0:T(8,128)(2,1)S(1)}, bf16[32,512]{1,0:T(8,128)(2,1)S(1)}, u32[]{:S(2)}, u32[]{:S(2)}) collective-permute-start(bf16[32,512]{1,0:T(8,128)(2,1)S(1)} %get-tuple-element.28.held_ref), channel_id=1, source_target_pairs={{0,4},{4,0},{8,12},{12,8},{16,20},{20,16},{24,28},{28,24},{1,5},{5... | collective-permute-start | bytes 98312 | tf_op jit(solution)/shard_map/ppermute | solution.py:243
  4.7 0.7 %collective-permute-start.1 = (bf16[1024,256]{1,0:T(8,128)(2,1)}, bf16[1024,256]{1,0:T(8,128)(2,1)S(1)}, u32[]{:S(2)}, u32[]{:S(2)}) collective-permute-start(bf16[1024,256]{1,0:T(8,128)(2,1)} %param.16), channel_id=1, source_target_pairs={{0,3},{1,0},{2,1},{3,2},{4,7},{5,4},{6,5},{7,6},{8,11},{9,8},{10,9... | collective-permute-start | bytes 1572872 | tf_op jit(solution)/shard_map/ppermute | solution.py:240
  5.4 1.7 %shard_map.105 = (f32[32,512]{1,0:T(8,128)S(1)}, bf16[512,512]{1,0:T(8,128)(2,1)S(1)}, bf16[3,256,256]{2,1,0:T(8,128)(2,1)S(1)}, bf16[3,256,256]{2,1,0:T(8,128)(2,1)S(1)}) custom-call(s32[3,1,512]{2,1,0:T(1,128)S(1)} %get-tuple-element.27.order_ref, bf16[32,512]{1,0:T(8,128)(2,1)S(1)} %get-tuple-element.28.held_ref, bf16[3,256,256]{2,1,0:T(8,128)(2,1)} %own_hbm.1, ...), custom_call_target="tpu_custom_call" | custom-call | tf_op jit(solution)/shard_map/pallas_call | solution.py:33
  7.1 0.0 collective-permute-done.swap_ref
  7.1 0.2 shard_map.106.held_ref
  7.3 1.6 %collective-permute-start.2 = (bf16[32,512]{1,0:T(8,128)(2,1)S(1)}, bf16[32,512]{1,0:T(8,128)(2,1)S(1)}, u32[]{:S(2)}, u32[]{:S(2)}) collective-permute-start(bf16[32,512]{1,0:T(8,128)(2,1)S(1)} %shard_map.106.held_ref), channel_id=1, source_target_pairs={{0,8},{4,12},{8,0},{12,4},{16,24},{20,28},{24,16},{28,20},{1,9},{5... | collective-permute-start | bytes 98312 | tf_op jit(solution)/shard_map/ppermute | solution.py:243
  8.9 2.5 %shard_map.107 = (f32[32,512]{1,0:T(8,128)S(1)}, bf16[512,512]{1,0:T(8,128)(2,1)S(1)}, bf16[256,1024]{1,0:T(8,128)(2,1)S(1)}, f32[128,1024]{1,0:T(8,128)S(1)}) custom-call(s32[3,1,512]{2,1,0:T(1,128)S(1)} %get-tuple-element.27.order_ref, bf16[32,512]{1,0:T(8,128)(2,1)S(1)} %shard_map.106.held_ref, bf16[3,256,256]{2,1,0:T(8,128)(2,1)S(1)} %get-tuple-element.31.own_ref, ...), custom_call_target="tpu_custom_call" | custom-call | flops 1000000000 | tf_op jit(solution)/shard_map/pallas_call | solution.py:33
  11.4 0.0 collective-permute-done.2.swap_ref
  11.4 0.0 copy-start
  11.4 0.2 shard_map.108.held_ref
  11.6 2.6 %collective-permute-start.4 = (bf16[32,512]{1,0:T(8,128)(2,1)S(1)}, bf16[32,512]{1,0:T(8,128)(2,1)S(1)}, u32[]{:S(2)}, u32[]{:S(2)}) collective-permute-start(bf16[32,512]{1,0:T(8,128)(2,1)S(1)} %shard_map.108.held_ref), channel_id=1, source_target_pairs={{0,16},{4,20},{8,24},{12,28},{16,0},{20,4},{24,8},{28,12},{1,17},{... | collective-permute-start | bytes 98312 | tf_op jit(solution)/shard_map/ppermute | solution.py:243
  14.2 0.0 collective-permute-done.1.read_ref
  14.2 0.0 copy-done
  14.2 0.4 %shard_map.109.block_ref = bf16[416,256]{1,0:T(8,128)(2,1)S(1)} custom-call(bf16[256,1024]{1,0:T(8,128)(2,1)S(1)} %get-tuple-element.33.gain_ref, f32[128,1024]{1,0:T(8,128)S(1)} %get-tuple-element.34.base_ref, bf16[1024,256]{1,0:T(8,128)(2,1)S(1)} %collective-permute-done.1.read_ref, s32[1,256]{1,0:T(1,128)S(1)} %copy-done), custom_call_target="tpu_custom_call" | custom-call | flops 201326592 | tf_op jit(solution)/shard_map/pallas_call | solution.py:33
  14.6 0.1 collective-permute-start.3
  14.7 1.7 %collective-permute-done.4.swap_ref = bf16[32,512]{1,0:T(8,128)(2,1)S(1)} collective-permute-done((bf16[32,512]{1,0:T(8,128)(2,1)S(1)}, bf16[32,512]{1,0:T(8,128)(2,1)S(1)}, u32[]{:S(2)}, u32[]{:S(2)}) %collective-permute-start.4) | collective-permute-done | bytes 32800 | tf_op jit(solution)/shard_map/ppermute | solution.py:243
  16.4 0.2 shard_map.111.refs_0_.top_ref
  16.6 0.0 collective-permute-start.7
  16.6 1.6 %collective-permute-start.6 = (bf16[32,512]{1,0:T(8,128)(2,1)S(1)}, bf16[32,512]{1,0:T(8,128)(2,1)S(1)}, u32[]{:S(2)}, u32[]{:S(2)}) collective-permute-start(bf16[32,512]{1,0:T(8,128)(2,1)S(1)} %shard_map.111.refs_0_.top_ref), channel_id=1, source_target_pairs={{0,2},{1,3},{2,0},{3,1},{4,6},{5,7},{6,4},{7,5},{8,10},{9,11},{10,... | collective-permute-start | bytes 98312 | tf_op jit(solution)/shard_map/ppermute | solution.py:237
  18.2 0.3 %collective-permute-start.5 = (bf16[32,512]{1,0:T(8,128)(2,1)S(1)}, bf16[32,512]{1,0:T(8,128)(2,1)S(1)}, u32[]{:S(2)}, u32[]{:S(2)}) collective-permute-start(bf16[32,512]{1,0:T(8,128)(2,1)S(1)} %shard_map.111.refs_0_.top_ref), channel_id=1, source_target_pairs={{0,1},{1,0},{2,3},{3,2},{4,5},{5,4},{6,7},{7,6},{8,9},{9,8},{10,11... | collective-permute-start | bytes 98312 | tf_op jit(solution)/shard_map/ppermute | solution.py:237
  18.5 0.0 collective-permute-done.3.other_ref
  18.5 0.6 %shard_map.110 = (f32[128,1024]{1,0:T(8,128)S(1)}, bf16[512,256]{1,0:T(8,128)(2,1)S(1)}, bf16[256,1024]{1,0:T(8,128)(2,1)S(1)}, f32[128,256]{1,0:T(8,128)S(1)}, bf16[512,256]{1,0:T(8,128)(2,1)S(1)}) custom-call(bf16[256,1024]{1,0:T(8,128)(2,1)S(1)} %get-tuple-element.33.gain_ref, f32[128,1024]{1,0:T(8,128)S(1)} %get-tuple-element.34.base_ref, ...), custom_call_target="tpu_custom_call" | custom-call | flops 134217728 | tf_op jit(solution)/shard_map/pallas_call | solution.py:33
  19.2 1.1 %collective-permute-done.7.refs_3_ = bf16[32,512]{1,0:T(8,128)(2,1)S(1)} collective-permute-done((bf16[32,512]{1,0:T(8,128)(2,1)S(1)}, bf16[32,512]{1,0:T(8,128)(2,1)S(1)}, u32[]{:S(2)}, u32[]{:S(2)}) %collective-permute-start.7) | collective-permute-done | bytes 32800 | tf_op jit(solution)/shard_map/ppermute | solution.py:237
  20.3 0.4 %collective-permute-done.6.refs_2_ = bf16[32,512]{1,0:T(8,128)(2,1)S(1)} collective-permute-done((bf16[32,512]{1,0:T(8,128)(2,1)S(1)}, bf16[32,512]{1,0:T(8,128)(2,1)S(1)}, u32[]{:S(2)}, u32[]{:S(2)}) %collective-permute-start.6) | collective-permute-done | bytes 32800 | tf_op jit(solution)/shard_map/ppermute | solution.py:237
  20.7 0.0 collective-permute-done.5.refs_1_
  20.7 0.2 shard_map.112
  20.9 1.6 %collective-permute-start.8 = (bf16[128,256]{1,0:T(8,128)(2,1)S(1)}, bf16[128,256]{1,0:T(8,128)(2,1)S(1)}, u32[]{:S(2)}, u32[]{:S(2)}) collective-permute-start(bf16[128,256]{1,0:T(8,128)(2,1)S(1)} %get-tuple-element.48), channel_id=1, source_target_pairs={{0,2},{1,3},{2,0},{3,1},{4,6},{5,7},{6,4},{7,5},{8,10},{9,11},{10,... | collective-permute-start | bytes 196616 | tf_op jit(solution)/shard_map/ppermute | solution.py:240
  22.5 1.2 %shard_map.113 = (f32[128,1024]{1,0:T(8,128)S(1)}, bf16[128,1024]{1,0:T(8,128)(2,1)}, bf16[32,512]{1,0:T(8,128)(2,1)}) custom-call(f32[128,1024]{1,0:T(8,128)S(1)} %get-tuple-element.39.fixed_ref, bf16[512,256]{1,0:T(8,128)(2,1)S(1)} %get-tuple-element.40.reach_ref, bf16[256,1024]{1,0:T(8,128)(2,1)S(1)} %get-tuple-element.33.gain_ref, ...), custom_call_target="tpu_custom_call" | custom-call | tf_op jit(solution)/shard_map/pallas_call | solution.py:33
  23.6 1.7 %collective-permute-done.8.arrived_ref = bf16[128,256]{1,0:T(8,128)(2,1)S(1)} collective-permute-done((bf16[128,256]{1,0:T(8,128)(2,1)S(1)}, bf16[128,256]{1,0:T(8,128)(2,1)S(1)}, u32[]{:S(2)}, u32[]{:S(2)}) %collective-permute-start.8) | collective-permute-done | bytes 65568 | tf_op jit(solution)/shard_map/ppermute | solution.py:240
  (1 shorter events, 0.0 us)
Async XLA Ops:
  1.7 5.4 %collective-permute-start = (bf16[32,512]{1,0:T(8,128)(2,1)S(1)}, bf16[32,512]{1,0:T(8,128)(2,1)S(1)}, u32[]{:S(2)}, u32[]{:S(2)}) collective-permute-start(bf16[32,512]{1,0:T(8,128)(2,1)S(1)} %get-tuple-element.28.held_ref), channel_id=1, source_target_pairs={{0,4},{4,0},{8,12},{12,8},{16,20},{20,16},{24,28},{28,24},{1,5},{5... | collective-permute-start | bytes 98312 | tf_op jit(solution)/shard_map/ppermute | solution.py:243
  4.7 9.5 %collective-permute-start.1 = (bf16[1024,256]{1,0:T(8,128)(2,1)}, bf16[1024,256]{1,0:T(8,128)(2,1)S(1)}, u32[]{:S(2)}, u32[]{:S(2)}) collective-permute-start(bf16[1024,256]{1,0:T(8,128)(2,1)} %param.16), channel_id=1, source_target_pairs={{0,3},{1,0},{2,1},{3,2},{4,7},{5,4},{6,5},{7,6},{8,11},{9,8},{10,9... | collective-permute-start | bytes 1572872 | tf_op jit(solution)/shard_map/ppermute | solution.py:240
  7.3 4.1 %collective-permute-start.2 = (bf16[32,512]{1,0:T(8,128)(2,1)S(1)}, bf16[32,512]{1,0:T(8,128)(2,1)S(1)}, u32[]{:S(2)}, u32[]{:S(2)}) collective-permute-start(bf16[32,512]{1,0:T(8,128)(2,1)S(1)} %shard_map.106.held_ref), channel_id=1, source_target_pairs={{0,8},{4,12},{8,0},{12,4},{16,24},{20,28},{24,16},{28,20},{1,9},{5... | collective-permute-start | bytes 98312 | tf_op jit(solution)/shard_map/ppermute | solution.py:243
  11.4 2.8 %copy-start = (s32[1,256]{1,0:T(1,128)S(1)}, s32[1,256]{1,0:T(1,128)}, u32[]{:S(2)}) copy-start(s32[1,256]{1,0:T(1,128)} %rows_ref.1) | copy-start | bytes 3076
  11.6 4.8 %collective-permute-start.4 = (bf16[32,512]{1,0:T(8,128)(2,1)S(1)}, bf16[32,512]{1,0:T(8,128)(2,1)S(1)}, u32[]{:S(2)}, u32[]{:S(2)}) collective-permute-start(bf16[32,512]{1,0:T(8,128)(2,1)S(1)} %shard_map.108.held_ref), channel_id=1, source_target_pairs={{0,16},{4,20},{8,24},{12,28},{16,0},{20,4},{24,8},{28,12},{1,17},{... | collective-permute-start | bytes 98312 | tf_op jit(solution)/shard_map/ppermute | solution.py:243
  14.6 3.9 %collective-permute-start.3 = (bf16[416,256]{1,0:T(8,128)(2,1)S(1)}, bf16[416,256]{1,0:T(8,128)(2,1)S(1)}, u32[]{:S(2)}, u32[]{:S(2)}) collective-permute-start(bf16[416,256]{1,0:T(8,128)(2,1)S(1)} %shard_map.109.block_ref), channel_id=1, source_target_pairs={{0,1},{1,0},{2,3},{3,2},{4,5},{5,4},{6,7},{7,6},{8,9},{9,8},{10,11... | collective-permute-start | bytes 638984 | tf_op jit(solution)/shard_map/ppermute | solution.py:237
  16.6 3.7 %collective-permute-start.7 = (bf16[32,512]{1,0:T(8,128)(2,1)S(1)}, bf16[32,512]{1,0:T(8,128)(2,1)S(1)}, u32[]{:S(2)}, u32[]{:S(2)}) collective-permute-start(bf16[32,512]{1,0:T(8,128)(2,1)S(1)} %shard_map.111.refs_0_.top_ref), channel_id=1, source_target_pairs={{0,3},{1,2},{2,1},{3,0},{4,7},{5,6},{6,5},{7,4},{8,11},{9,10},{10,... | collective-permute-start | bytes 98312 | tf_op jit(solution)/shard_map/ppermute | solution.py:237
  16.6 4.0 %collective-permute-start.6 = (bf16[32,512]{1,0:T(8,128)(2,1)S(1)}, bf16[32,512]{1,0:T(8,128)(2,1)S(1)}, u32[]{:S(2)}, u32[]{:S(2)}) collective-permute-start(bf16[32,512]{1,0:T(8,128)(2,1)S(1)} %shard_map.111.refs_0_.top_ref), channel_id=1, source_target_pairs={{0,2},{1,3},{2,0},{3,1},{4,6},{5,7},{6,4},{7,5},{8,10},{9,11},{10,... | collective-permute-start | bytes 98312 | tf_op jit(solution)/shard_map/ppermute | solution.py:237
  18.2 2.5 %collective-permute-start.5 = (bf16[32,512]{1,0:T(8,128)(2,1)S(1)}, bf16[32,512]{1,0:T(8,128)(2,1)S(1)}, u32[]{:S(2)}, u32[]{:S(2)}) collective-permute-start(bf16[32,512]{1,0:T(8,128)(2,1)S(1)} %shard_map.111.refs_0_.top_ref), channel_id=1, source_target_pairs={{0,1},{1,0},{2,3},{3,2},{4,5},{5,4},{6,7},{7,6},{8,9},{9,8},{10,11... | collective-permute-start | bytes 98312 | tf_op jit(solution)/shard_map/ppermute | solution.py:237
  20.9 4.4 %collective-permute-start.8 = (bf16[128,256]{1,0:T(8,128)(2,1)S(1)}, bf16[128,256]{1,0:T(8,128)(2,1)S(1)}, u32[]{:S(2)}, u32[]{:S(2)}) collective-permute-start(bf16[128,256]{1,0:T(8,128)(2,1)S(1)} %get-tuple-element.48), channel_id=1, source_target_pairs={{0,2},{1,3},{2,0},{3,1},{4,6},{5,7},{6,4},{7,5},{8,10},{9,11},{10,... | collective-permute-start | bytes 196616 | tf_op jit(solution)/shard_map/ppermute | solution.py:240

commit v7 on v6

--- a/solution.py
+++ b/solution.py
@@ -12,7 +12,10 @@
 LOW_BITS = 8
 INDEX_ROWS = 16
 PANEL_COST = 10**9
-LEVEL_COST = 4 * 10**9
+CHAIN_COST = 3 * 10**9
+PRIOR_COST = 10**9
+LAST_COST = 10**8
+LEVEL_COST = 2 * 10**9
 
 def dot(left, right):
     return jnp.dot(left, right, preferred_element_type=F32)
@@ -61,10 +64,13 @@
     return jnp.concatenate(pieces, axis=0).astype(BF16)
 
 
-def ready_kernel(order_ref, held_ref, own_hbm, cross_hbm, part_ref, fold_ref, own_ref, cross_ref, sems):
+def ready_kernel(
+    order_ref, held_ref, own_hbm, cross_hbm, rows_hbm, part_ref, fold_ref, own_ref, cross_ref, rows_ref, sems
+):
     copies = [
         pltpu.make_async_copy(own_hbm, own_ref, sems.at[0]),
         pltpu.make_async_copy(cross_hbm, cross_ref, sems.at[1]),
+        pltpu.make_async_copy(rows_hbm, rows_ref, sems.at[2]),
     ]
     for copy in copies:
         copy.start()
@@ -132,11 +138,7 @@
     out_ref[...] = (part_ref[...] + dot(swap_ref[...], fold_ref[...])).astype(BF16)
 
 
-def chain_kernel(
-    gain_ref, base_ref, block_ref, other_ref, fixed_ref, reach_ref, slope_ref, hop_fixed_ref, hop_ref, *hop_slope
-):
-    vectors, rank = base_ref.shape[0], gain_ref.shape[0]
-    top_rows = hop_ref.shape[0]
+def pair_blocks(own_ref, other_ref, vectors, rank, top_rows):
     odd = lax.rem(lax.axis_index("fr"), 2) == 1
 
     def parts(ref):
@@ -146,38 +148,56 @@
         high = ref[at : at + INDEX_ROWS].astype(F32)[:1].astype(jnp.int32)
         return ref[:vectors], ref[vectors : vectors + rank], high * 2**LOW_BITS + low
 
-    base_own, step_own, rows_own = parts(block_ref)
-    base_other, step_other, rows_other = parts(other_ref)
-    base_even = jnp.where(odd, base_other, base_own)
-    base_odd = jnp.where(odd, base_own, base_other)
-    step_even = jnp.where(odd, step_other, step_own)
-    step_odd = jnp.where(odd, step_own, step_other)
-    pick_even = picker(jnp.where(odd, rows_other, rows_own), top_rows)
-    pick_odd = picker(jnp.where(odd, rows_own, rows_other), top_rows)
-
+    own, other = parts(own_ref), parts(other_ref)
+    base_even, step_even, rows_even = (jnp.where(odd, y, x) for x, y in zip(own, other))
+    base_odd, step_odd, rows_odd = (jnp.where(odd, x, y) for x, y in zip(own, other))
+    pick_even, pick_odd = picker(rows_even, top_rows), picker(rows_odd, top_rows)
     past = (dot(pick_even, step_even) - pick_odd.astype(F32)).astype(BF16)
-    hop_fixed_ref[...] = base_odd.astype(F32) - dot(base_even, step_odd)
-    hop_ref[...] = dot(past, step_odd).astype(BF16)
-    for ref in hop_slope:
-        ref[...] = dot(step_even, step_odd).astype(BF16)
+    return odd, base_even, base_odd, step_even, step_odd, pick_even, past
+
+
+def chain_kernel(gain_ref, base_ref, block_ref, other_ref, fixed_ref, reach_ref, slope_ref, *hops):
+    vectors, rank, top_rows = base_ref.shape[0], gain_ref.shape[0], reach_ref.shape[0]
+    odd, base_even, base_odd, step_even, step_odd, pick_even, past = pair_blocks(
+        block_ref, other_ref, vectors, rank, top_rows
+    )
+    if hops:
+        hop_fixed_ref, hop_ref, hop_slope_ref = hops
+        hop_fixed_ref[...] = base_odd.astype(F32) - dot(base_even, step_odd)
+        hop_ref[...] = dot(past, step_odd).astype(BF16)
+        hop_slope_ref[...] = dot(step_even, step_odd).astype(BF16)
     reach_ref[...] = jnp.where(odd, -past, pick_even)
     gain = gain_ref[...]
     fixed_ref[...] = base_ref[...] - dot(jnp.where(odd, base_even, jnp.zeros_like(base_even)), gain)
     slope_ref[...] = jnp.where(odd, -dot(step_even, gain), gain.astype(F32)).astype(BF16)
 
 
+def prior_kernel(block_ref, other_ref, fixed_ref, reach_ref):
+    (vectors, rank), top_rows = fixed_ref.shape, reach_ref.shape[0]
+    _, base_even, base_odd, _, step_odd, _, past = pair_blocks(
+        block_ref, other_ref, vectors, rank, top_rows
+    )
+    later = lax.axis_index("fr") >= 2
+    fixed_ref[...] = jnp.where(later, base_odd.astype(F32) - dot(base_even, step_odd), 0.0)
+    reach_ref[...] = jnp.where(later, dot(past, step_odd), 0.0).astype(BF16)
+
+
 def last_kernel(level, own_ref, cross_ref, held_ref, swap_ref, top_ref):
     top_ref[...] = mixed(held_ref[...], swap_ref[...], own_ref[level], cross_ref[level]).astype(BF16)
 
 
-def pass_kernel(hop_fixed_ref, hop_ref, *refs):
-    *slabs, top_ref, pass_ref, wide = refs
+def gathered(wide, slabs):
     rows = slabs[0].shape[0]
     place = lax.axis_index("fr")
     for flip, slab in enumerate(slabs):
         start = pl.multiple_of(jnp.bitwise_xor(place, flip) * rows, rows)
         wide[pl.ds(start, rows), :] = slab[...].astype(F32)
-    top = wide[...].astype(BF16)
+    return wide[...].astype(BF16)
+
+
+def pass_kernel(hop_fixed_ref, hop_ref, *refs):
+    *slabs, top_ref, pass_ref, wide = refs
+    top = gathered(wide, slabs)
     top_ref[...] = top
     pass_ref[...] = (hop_fixed_ref[...] + dot(top, hop_ref[...])).astype(BF16)
 
@@ -213,6 +233,21 @@
     def _():
         arrived = arrived_ref[...]
         written(out_hbm, held, sems, lambda cut: ready_ref[:, cut] - dot(arrived, slope_ref[:, cut]))
+
+
+def whole_kernel(fixed_ref, reach_ref, gain_ref, slope_ref, prior_fixed_ref, prior_ref, *refs):
+    *slabs, out_hbm, top_hbm, wide, held, sems, top_sem = refs
+    copy = pltpu.make_async_copy(slabs[0], top_hbm, top_sem)
+    copy.start()
+    top = gathered(wide, slabs)
+    link = dot(top, reach_ref[...]).astype(BF16)
+    prior = (prior_fixed_ref[...] + dot(top, prior_ref[...])).astype(BF16)
+
+    def part(cut):
+        return fixed_ref[:, cut] - (dot(link, gain_ref[:, cut]) + dot(prior, slope_ref[:, cut]))
+
+    written(out_hbm, held, sems, part)
+    copy.wait()
 
 
 def body(
@@ -250,15 +285,21 @@
         remote=[top_source, level_ordering],
     )
     swap = swapped(held, 1)
-    coupling_read, order = lax.optimization_barrier((coupling_read, order))
+    if chips > 2:
+        coupling_read, order = lax.optimization_barrier((coupling_read, order))
     next_read = turned(coupling_read, -1)
     ready_outs = [((rows, top_rows), F32, True), ((top_rows, top_rows), BF16, True)]
-    part, folded, own, cross = kernel_call(
+    part, folded, own, cross, parent_rows = kernel_call(
         ready_kernel,
-        [*ready_outs, (butterfly_own.shape, BF16, True), (butterfly_cross.shape, BF16, True)],
-        [pltpu.SemaphoreType.DMA((2,))],
+        [
+            *ready_outs,
+            (butterfly_own.shape, BF16, True),
+            (butterfly_cross.shape, BF16, True),
+            (parent_rows.shape, jnp.int32, True),
+        ],
+        [pltpu.SemaphoreType.DMA((3,))],
         [order, held],
-        remote=[butterfly_own, butterfly_cross],
+        remote=[butterfly_own, butterfly_cross, parent_rows],
     )
 
     def next_level(part, folded, swap):
@@ -281,8 +322,9 @@
         [coupling_write, panel_inverse, front_source],
     )
     held = next_level(part, folded, swap)
-    swap = swapped(held, 4)
-
+
+    if chips > 2:
+        swap = swapped(held, 4)
     next_read, held = lax.optimization_barrier((next_read, held))
     (block,) = kernel_call(
         block_kernel,
@@ -291,16 +333,23 @@
         [gain, base, next_read, parent_rows],
         2 * (vectors + rank) * panel * rank,
     )
+    if chips <= 2:
+        block, held = lax.optimization_barrier((block, held))
+        prior = flipped(block, 2)
+        swap = swapped(held, 4)
     other = flipped(block, 1)
+    hop_outs = [
+        ((vectors, rank), F32, True),
+        ((top_rows, rank), BF16, True),
+        ((rank, rank), BF16, True),
+    ]
     outs = [
         ((vectors, panel), F32, True),
         ((top_rows, rank), BF16, True),
         ((rank, panel), BF16, True),
-        ((vectors, rank), F32, True),
-        ((top_rows, rank), BF16, True),
-    ] + [((rank, rank), BF16, True)] * (chips > 2)
-    fixed, reach, slope, hop_fixed, hop, *hop_slope = kernel_call(
-        chain_kernel, outs, [], [gain, base, block, other], 2 * rank * rank * panel
+    ] + hop_outs * (chips > 2)
+    fixed, reach, slope, *hops = kernel_call(
+        chain_kernel, outs, [], [gain, base, block, other], CHAIN_COST
     )
 
     (top,) = kernel_call(
@@ -308,24 +357,40 @@
         [((rows, top_rows), BF16, True)],
         [],
         [own, cross, held, swap],
-        LEVEL_COST,
+        LEVEL_COST if chips > 2 else LAST_COST,
     )
     slabs = [top] + [flipped(top, mask) for mask in range(1, chain)]
+    wide = pltpu.VMEM((vectors, top_rows), F32)
+    staging = [pltpu.VMEM((vectors, panel), BF16), pltpu.SemaphoreType.DMA((4,))]
+    results = [((vectors, panel), BF16, False), ((rows, top_rows), BF16, False)]
+    if chips <= 2:
+        prior, _ = lax.optimization_barrier((prior, top))
+        prior_maps = kernel_call(
+            prior_kernel, hop_outs[:2], [], [prior, flipped(prior, 1)], PRIOR_COST
+        )
+        solved, top = kernel_call(
+            whole_kernel,
+            results,
+            [wide, *staging, pltpu.SemaphoreType.DMA],
+            [fixed, reach, gain, slope, *prior_maps, *slabs],
+        )
+        return (top, solved)
+
+    hop_fixed, hop, hop_slope = hops
     whole, passed = kernel_call(
         pass_kernel,
         [((vectors, top_rows), BF16, True), ((vectors, rank), BF16, True)],
-        [pltpu.VMEM((vectors, top_rows), F32)],
+        [wide],
         [hop_fixed, hop, *slabs],
     )
     start = passed
     for _ in range(chips - 2):
         here = jnp.where(lax.axis_index("fr") >= 2, turned(passed, 2), 0)
-        passed = (start.astype(F32) + dot(here, hop_slope[0])).astype(BF16)
+        passed = (start.astype(F32) + dot(here, hop_slope)).astype(BF16)
     arrived = turned(passed, 2)
-    staging = [pltpu.VMEM((vectors, panel), BF16), pltpu.SemaphoreType.DMA((4,))]
     ready, solved, top = kernel_call(
         link_kernel,
-        [((vectors, panel), F32, True), ((vectors, panel), BF16, False), ((rows, top_rows), BF16, False)],
+        [((vectors, panel), F32, True), *results],
         [*staging, pltpu.SemaphoreType.DMA],
         [fixed, reach, gain, whole, top],
     )

time: 25.6 us -> 24.6 us (0.961)
  waiting for transfers between devices: 4.96 us -> 4.44 us
  starting transfers between devices: 11.4 us -> 10.9 us
    ppermute x2 -> x1, waiting for transfers between devices: 1.68 us -> 0.01 us  [turned(): lax.ppermute(array, 'fr', [(i, (i + by) % chain) for i in range(chain)])]
    ppermute x3, starting transfers between devices: 7.2 us -> 5.74 us  [swapped(): return lax.ppermute(array, 'bf', [(g, g ^ mask) for g in range(groups)])]
    ppermute x3, waiting for transfers between devices: 1.75 us -> 2.86 us  [swapped(): return lax.ppermute(array, 'bf', [(g, g ^ mask) for g in range(groups)])]
    ppermute x4 -> x6, starting transfers between devices: 1.94 us -> 2.68 us  [flipped(): return lax.ppermute(array, 'fr', [(i, i ^ mask) for i in range(chain)])]
    ppermute x2 -> x1, starting transfers between devices: 2.24 us -> 2.46 us  [turned(): lax.ppermute(array, 'fr', [(i, (i + by) % chain) for i in range(chain)])]
    pallas_call x11 -> x10, Pallas kernels: 8.24 us -> 8.31 us  [kernel_call(): pl.pallas_call(kernel, out_shape=shapes, in_specs=[vmem] * len(placed) +...]
    ppermute x4 -> x6, waiting for transfers between devices: 1.54 us -> 1.57 us  [flipped(): return lax.ppermute(array, 'fr', [(i, i ^ mask) for i in range(chain)])]
  transfers between devices with their start and end apart: 9 -> 10, of which waited for: 4 -> 4; matrix products, arithmetic and copies ran while one was open for 0% -> 0% of each run, Pallas kernels for 28% -> 28%
where the time goes in v7:
time: 24.6 us; the launch traced here: 24.3 us
  starting transfers between devices  10.9 us (44%)
  Pallas kernels  8.31 us (34%)
  waiting for transfers between devices  4.44 us (18%)
  between operations  0.71 us (3%)
    pallas_call x10, Pallas kernels, kernel_call(): pl.pallas_call(kernel, out_shape=shapes, in_specs=[vmem] * len(placed) +...  8.31 us
    ppermute x3, starting transfers between devices, swapped(): return lax.ppermute(array, 'bf', [(g, g ^ mask) for g in range(groups)])  5.74 us
    ppermute x3, waiting for transfers between devices, swapped(): return lax.ppermute(array, 'bf', [(g, g ^ mask) for g in range(groups)])  2.86 us
    ppermute x6, starting transfers between devices, flipped(): return lax.ppermute(array, 'fr', [(i, i ^ mask) for i in range(chain)])  2.68 us
    ppermute x1, starting transfers between devices, turned(): lax.ppermute(array, 'fr', [(i, (i + by) % chain) for i in range(chain)])  2.46 us
    ppermute x6, waiting for transfers between devices, flipped(): return lax.ppermute(array, 'fr', [(i, i ^ mask) for i in range(chain)])  1.57 us
  transfers between devices with their start and end apart: 10, of which 4 were waited for; matrix products, arithmetic and copies ran while one was open for 0% of the time, Pallas kernels for 28%

profile of v7, /device:TPU:0, one launch (start us, length us, event | category | flops | bytes accessed | tf_op | source)
XLA Modules:
  0.0 24.3 jit_solution(6671506676690883650)
XLA Ops:
  0.6 2.5 %collective-permute-start.1 = (bf16[1024,256]{1,0:T(8,128)(2,1)}, bf16[1024,256]{1,0:T(8,128)(2,1)S(1)}, u32[]{:S(2)}, u32[]{:S(2)}) collective-permute-start(bf16[1024,256]{1,0:T(8,128)(2,1)} %param.16), channel_id=1, source_target_pairs={{0,3},{1,0},{2,1},{3,2},{4,7},{5,4},{6,5},{7,6},{8,11},{9,8},{10,9... | collective-permute-start | bytes 1572872 | tf_op jit(solution)/shard_map/ppermute | solution.py:275
  3.1 1.0 %shard_map.104 = (bf16[32,512]{1,0:T(8,128)(2,1)S(1)}, s32[3,1,512]{2,1,0:T(1,128)S(1)}) custom-call(bf16[32,512]{1,0:T(8,128)(2,1)} %source_hbm.2, s32[3,1,512]{2,1,0:T(1,128)} %order_hbm.1), custom_call_target="tpu_custom_call" | custom-call | tf_op jit(solution)/shard_map/pallas_call | solution.py:36
  4.1 1.6 %collective-permute-start = (bf16[32,512]{1,0:T(8,128)(2,1)S(1)}, bf16[32,512]{1,0:T(8,128)(2,1)S(1)}, u32[]{:S(2)}, u32[]{:S(2)}) collective-permute-start(bf16[32,512]{1,0:T(8,128)(2,1)S(1)} %get-tuple-element.26.held_ref), channel_id=1, source_target_pairs={{0,4},{4,0},{8,12},{12,8},{16,20},{20,16},{24,28},{28,24},{1,5},{5... | collective-permute-start | bytes 98312 | tf_op jit(solution)/shard_map/ppermute | solution.py:278
  5.7 1.8 %shard_map.105 = (f32[32,512]{1,0:T(8,128)S(1)}, bf16[512,512]{1,0:T(8,128)(2,1)S(1)}, bf16[3,256,256]{2,1,0:T(8,128)(2,1)S(1)}, bf16[3,256,256]{2,1,0:T(8,128)(2,1)S(1)}, s32[1,256]{1,0:T(1,128)S(1)}) custom-call(s32[3,1,512]{2,1,0:T(1,128)S(1)} %get-tuple-element.25.order_ref, bf16[32,512]{1,0:T(8,128)(2,1)S(1)} %get-tuple-element.26.held_ref, ...), custom_call_target="tpu_custom_call" | custom-call | tf_op jit(solution)/shard_map/pallas_call | solution.py:36
  7.5 0.6 %collective-permute-done.swap_ref = bf16[32,512]{1,0:T(8,128)(2,1)S(1)} collective-permute-done((bf16[32,512]{1,0:T(8,128)(2,1)S(1)}, bf16[32,512]{1,0:T(8,128)(2,1)S(1)}, u32[]{:S(2)}, u32[]{:S(2)}) %collective-permute-start) | collective-permute-done | bytes 32800 | tf_op jit(solution)/shard_map/ppermute | solution.py:278
  8.1 0.2 shard_map.106.held_ref
  8.3 1.6 %collective-permute-start.2 = (bf16[32,512]{1,0:T(8,128)(2,1)S(1)}, bf16[32,512]{1,0:T(8,128)(2,1)S(1)}, u32[]{:S(2)}, u32[]{:S(2)}) collective-permute-start(bf16[32,512]{1,0:T(8,128)(2,1)S(1)} %shard_map.106.held_ref), channel_id=1, source_target_pairs={{0,8},{4,12},{8,0},{12,4},{16,24},{20,28},{24,16},{28,20},{1,9},{5... | collective-permute-start | bytes 98312 | tf_op jit(solution)/shard_map/ppermute | solution.py:278
  9.9 2.5 %shard_map.107 = (f32[32,512]{1,0:T(8,128)S(1)}, bf16[512,512]{1,0:T(8,128)(2,1)S(1)}, bf16[256,1024]{1,0:T(8,128)(2,1)S(1)}, f32[128,1024]{1,0:T(8,128)S(1)}) custom-call(s32[3,1,512]{2,1,0:T(1,128)S(1)} %get-tuple-element.25.order_ref, bf16[32,512]{1,0:T(8,128)(2,1)S(1)} %shard_map.106.held_ref, bf16[3,256,256]{2,1,0:T(8,128)(2,1)S(1)} %get-tuple-element.29.own_ref, ...), custom_call_target="tpu_custom_call" | custom-call | flops 1000000000 | tf_op jit(solution)/shard_map/pallas_call | solution.py:36
  12.4 0.0 collective-permute-done.2.swap_ref
  12.4 0.2 shard_map.108.held_ref
  12.6 0.0 collective-permute-done.1.read_ref
  12.6 0.4 %shard_map.109.block_ref = bf16[416,256]{1,0:T(8,128)(2,1)S(1)} custom-call(bf16[256,1024]{1,0:T(8,128)(2,1)S(1)} %get-tuple-element.31.gain_ref, f32[128,1024]{1,0:T(8,128)S(1)} %get-tuple-element.32.base_ref, bf16[1024,256]{1,0:T(8,128)(2,1)S(1)} %collective-permute-done.1.read_ref, s32[1,256]{1,0:T(1,128)S(1)} %get-tuple-element.36.rows_ref), custom_call_target="tpu_custom_call" | custom-call | flops 201326592 | tf_op jit(solution)/shard_map/pallas_call | solution.py:36
  13.0 0.6 %collective-permute-start.4 = (bf16[416,256]{1,0:T(8,128)(2,1)S(1)}, bf16[416,256]{1,0:T(8,128)(2,1)S(1)}, u32[]{:S(2)}, u32[]{:S(2)}) collective-permute-start(bf16[416,256]{1,0:T(8,128)(2,1)S(1)} %shard_map.109.block_ref), channel_id=1, source_target_pairs={{0,2},{1,3},{2,0},{3,1},{4,6},{5,7},{6,4},{7,5},{8,10},{9,11},{10,... | collective-permute-start | bytes 638984 | tf_op jit(solution)/shard_map/ppermute | solution.py:272
  13.6 0.0 collective-permute-start.3
  13.6 2.6 %collective-permute-start.5 = (bf16[32,512]{1,0:T(8,128)(2,1)S(1)}, bf16[32,512]{1,0:T(8,128)(2,1)S(1)}, u32[]{:S(2)}, u32[]{:S(2)}) collective-permute-start(bf16[32,512]{1,0:T(8,128)(2,1)S(1)} %shard_map.108.held_ref), channel_id=1, source_target_pairs={{0,16},{4,20},{8,24},{12,28},{16,0},{20,4},{24,8},{28,12},{1,17},{... | collective-permute-start | bytes 98312 | tf_op jit(solution)/shard_map/ppermute | solution.py:278
  16.2 2.2 %collective-permute-done.5.swap_ref = bf16[32,512]{1,0:T(8,128)(2,1)S(1)} collective-permute-done((bf16[32,512]{1,0:T(8,128)(2,1)S(1)}, bf16[32,512]{1,0:T(8,128)(2,1)S(1)}, u32[]{:S(2)}, u32[]{:S(2)}) %collective-permute-start.5) | collective-permute-done | bytes 32800 | tf_op jit(solution)/shard_map/ppermute | solution.py:278
  18.5 0.2 shard_map.111.refs_0_
  18.6 0.4 %collective-permute-start.9 = (bf16[32,512]{1,0:T(8,128)(2,1)S(1)}, bf16[32,512]{1,0:T(8,128)(2,1)S(1)}, u32[]{:S(2)}, u32[]{:S(2)}) collective-permute-start(bf16[32,512]{1,0:T(8,128)(2,1)S(1)} %shard_map.111.refs_0_), channel_id=1, source_target_pairs={{0,3},{1,2},{2,1},{3,0},{4,7},{5,6},{6,5},{7,4},{8,11},{9,10},{10,... | collective-permute-start | bytes 98312 | tf_op jit(solution)/shard_map/ppermute | solution.py:272
  19.1 1.1 %collective-permute-start.8 = (bf16[32,512]{1,0:T(8,128)(2,1)S(1)}, bf16[32,512]{1,0:T(8,128)(2,1)S(1)}, u32[]{:S(2)}, u32[]{:S(2)}) collective-permute-start(bf16[32,512]{1,0:T(8,128)(2,1)S(1)} %shard_map.111.refs_0_), channel_id=1, source_target_pairs={{0,2},{1,3},{2,0},{3,1},{4,6},{5,7},{6,4},{7,5},{8,10},{9,11},{10,... | collective-permute-start | bytes 98312 | tf_op jit(solution)/shard_map/ppermute | solution.py:272
  20.2 0.3 %collective-permute-start.7 = (bf16[32,512]{1,0:T(8,128)(2,1)S(1)}, bf16[32,512]{1,0:T(8,128)(2,1)S(1)}, u32[]{:S(2)}, u32[]{:S(2)}) collective-permute-start(bf16[32,512]{1,0:T(8,128)(2,1)S(1)} %shard_map.111.refs_0_), channel_id=1, source_target_pairs={{0,1},{1,0},{2,3},{3,2},{4,5},{5,4},{6,7},{7,6},{8,9},{9,8},{10,11... | collective-permute-start | bytes 98312 | tf_op jit(solution)/shard_map/ppermute | solution.py:272
  20.5 0.0 collective-permute-done.4.block_ref
  20.5 0.2 collective-permute-start.6
  20.7 0.0 collective-permute-done.3.other_ref
  20.7 0.5 %shard_map.110 = (f32[128,1024]{1,0:T(8,128)S(1)}, bf16[512,256]{1,0:T(8,128)(2,1)S(1)}, bf16[256,1024]{1,0:T(8,128)(2,1)S(1)}) custom-call(bf16[256,1024]{1,0:T(8,128)(2,1)S(1)} %get-tuple-element.31.gain_ref, f32[128,1024]{1,0:T(8,128)S(1)} %get-tuple-element.32.base_ref, bf16[416,256]{1,0:T(8,128)(2,1)S(1)} %shard_map.109.block_ref, ...), custom_call_target="tpu_custom_call" | custom-call | flops 3000000000 | tf_op jit(solution)/shard_map/pallas_call | solution.py:36
  21.2 0.8 %collective-permute-done.6.other_ref = bf16[416,256]{1,0:T(8,128)(2,1)S(1)} collective-permute-done((bf16[416,256]{1,0:T(8,128)(2,1)S(1)}, bf16[416,256]{1,0:T(8,128)(2,1)S(1)}, u32[]{:S(2)}, u32[]{:S(2)}) %collective-permute-start.6) | collective-permute-done | bytes 213024 | tf_op jit(solution)/shard_map/ppermute | solution.py:272
  22.0 0.4 %shard_map.112 = (f32[128,256]{1,0:T(8,128)S(1)}, bf16[512,256]{1,0:T(8,128)(2,1)S(1)}) custom-call(bf16[416,256]{1,0:T(8,128)(2,1)S(1)} %collective-permute-done.4.block_ref, bf16[416,256]{1,0:T(8,128)(2,1)S(1)} %collective-permute-done.6.other_ref), custom_call_target="tpu_custom_call" | custom-call | flops 1000000000 | tf_op jit(solution)/shard_map/pallas_call | solution.py:36
  22.4 0.0 collective-permute-done.9.refs_3_
  22.4 0.7 %collective-permute-done.8.refs_2_ = bf16[32,512]{1,0:T(8,128)(2,1)S(1)} collective-permute-done((bf16[32,512]{1,0:T(8,128)(2,1)S(1)}, bf16[32,512]{1,0:T(8,128)(2,1)S(1)}, u32[]{:S(2)}, u32[]{:S(2)}) %collective-permute-start.8) | collective-permute-done | bytes 32800 | tf_op jit(solution)/shard_map/ppermute | solution.py:272
  23.1 0.0 collective-permute-done.7.refs_1_
  23.2 1.2 %shard_map.113 = (bf16[128,1024]{1,0:T(8,128)(2,1)}, bf16[32,512]{1,0:T(8,128)(2,1)}) custom-call(f32[128,1024]{1,0:T(8,128)S(1)} %get-tuple-element.39.fixed_ref, bf16[512,256]{1,0:T(8,128)(2,1)S(1)} %get-tuple-element.40.reach_ref, bf16[256,1024]{1,0:T(8,128)(2,1)S(1)} %get-tuple-element.31.gain_ref, bf16[256,1024]{1,0:T(8,128)(2,1)S(1)} %get-tuple-element.41.slope_ref, ...), custom_call_target="tpu_custom_call" | custom-call | tf_op jit(solution)/shard_map/pallas_call | solution.py:36
Async XLA Ops:
  0.6 12.0 %collective-permute-start.1 = (bf16[1024,256]{1,0:T(8,128)(2,1)}, bf16[1024,256]{1,0:T(8,128)(2,1)S(1)}, u32[]{:S(2)}, u32[]{:S(2)}) collective-permute-start(bf16[1024,256]{1,0:T(8,128)(2,1)} %param.16), channel_id=1, source_target_pairs={{0,3},{1,0},{2,1},{3,2},{4,7},{5,4},{6,5},{7,6},{8,11},{9,8},{10,9... | collective-permute-start | bytes 1572872 | tf_op jit(solution)/shard_map/ppermute | solution.py:275
  4.1 4.0 %collective-permute-start = (bf16[32,512]{1,0:T(8,128)(2,1)S(1)}, bf16[32,512]{1,0:T(8,128)(2,1)S(1)}, u32[]{:S(2)}, u32[]{:S(2)}) collective-permute-start(bf16[32,512]{1,0:T(8,128)(2,1)S(1)} %get-tuple-element.26.held_ref), channel_id=1, source_target_pairs={{0,4},{4,0},{8,12},{12,8},{16,20},{20,16},{24,28},{28,24},{1,5},{5... | collective-permute-start | bytes 98312 | tf_op jit(solution)/shard_map/ppermute | solution.py:278
  8.3 4.1 %collective-permute-start.2 = (bf16[32,512]{1,0:T(8,128)(2,1)S(1)}, bf16[32,512]{1,0:T(8,128)(2,1)S(1)}, u32[]{:S(2)}, u32[]{:S(2)}) collective-permute-start(bf16[32,512]{1,0:T(8,128)(2,1)S(1)} %shard_map.106.held_ref), channel_id=1, source_target_pairs={{0,8},{4,12},{8,0},{12,4},{16,24},{20,28},{24,16},{28,20},{1,9},{5... | collective-permute-start | bytes 98312 | tf_op jit(solution)/shard_map/ppermute | solution.py:278
  13.0 7.5 %collective-permute-start.4 = (bf16[416,256]{1,0:T(8,128)(2,1)S(1)}, bf16[416,256]{1,0:T(8,128)(2,1)S(1)}, u32[]{:S(2)}, u32[]{:S(2)}) collective-permute-start(bf16[416,256]{1,0:T(8,128)(2,1)S(1)} %shard_map.109.block_ref), channel_id=1, source_target_pairs={{0,2},{1,3},{2,0},{3,1},{4,6},{5,7},{6,4},{7,5},{8,10},{9,11},{10,... | collective-permute-start | bytes 638984 | tf_op jit(solution)/shard_map/ppermute | solution.py:272
  13.6 7.0 %collective-permute-start.3 = (bf16[416,256]{1,0:T(8,128)(2,1)S(1)}, bf16[416,256]{1,0:T(8,128)(2,1)S(1)}, u32[]{:S(2)}, u32[]{:S(2)}) collective-permute-start(bf16[416,256]{1,0:T(8,128)(2,1)S(1)} %shard_map.109.block_ref), channel_id=1, source_target_pairs={{0,1},{1,0},{2,3},{3,2},{4,5},{5,4},{6,7},{7,6},{8,9},{9,8},{10,11... | collective-permute-start | bytes 638984 | tf_op jit(solution)/shard_map/ppermute | solution.py:272
  13.6 4.8 %collective-permute-start.5 = (bf16[32,512]{1,0:T(8,128)(2,1)S(1)}, bf16[32,512]{1,0:T(8,128)(2,1)S(1)}, u32[]{:S(2)}, u32[]{:S(2)}) collective-permute-start(bf16[32,512]{1,0:T(8,128)(2,1)S(1)} %shard_map.108.held_ref), channel_id=1, source_target_pairs={{0,16},{4,20},{8,24},{12,28},{16,0},{20,4},{24,8},{28,12},{1,17},{... | collective-permute-start | bytes 98312 | tf_op jit(solution)/shard_map/ppermute | solution.py:278
  18.6 3.8 %collective-permute-start.9 = (bf16[32,512]{1,0:T(8,128)(2,1)S(1)}, bf16[32,512]{1,0:T(8,128)(2,1)S(1)}, u32[]{:S(2)}, u32[]{:S(2)}) collective-permute-start(bf16[32,512]{1,0:T(8,128)(2,1)S(1)} %shard_map.111.refs_0_), channel_id=1, source_target_pairs={{0,3},{1,2},{2,1},{3,0},{4,7},{5,6},{6,5},{7,4},{8,11},{9,10},{10,... | collective-permute-start | bytes 98312 | tf_op jit(solution)/shard_map/ppermute | solution.py:272
  19.1 4.1 %collective-permute-start.8 = (bf16[32,512]{1,0:T(8,128)(2,1)S(1)}, bf16[32,512]{1,0:T(8,128)(2,1)S(1)}, u32[]{:S(2)}, u32[]{:S(2)}) collective-permute-start(bf16[32,512]{1,0:T(8,128)(2,1)S(1)} %shard_map.111.refs_0_), channel_id=1, source_target_pairs={{0,2},{1,3},{2,0},{3,1},{4,6},{5,7},{6,4},{7,5},{8,10},{9,11},{10,... | collective-permute-start | bytes 98312 | tf_op jit(solution)/shard_map/ppermute | solution.py:272
  20.2 3.0 %collective-permute-start.7 = (bf16[32,512]{1,0:T(8,128)(2,1)S(1)}, bf16[32,512]{1,0:T(8,128)(2,1)S(1)}, u32[]{:S(2)}, u32[]{:S(2)}) collective-permute-start(bf16[32,512]{1,0:T(8,128)(2,1)S(1)} %shard_map.111.refs_0_), channel_id=1, source_target_pairs={{0,1},{1,0},{2,3},{3,2},{4,5},{5,4},{6,7},{7,6},{8,9},{9,8},{10,11... | collective-permute-start | bytes 98312 | tf_op jit(solution)/shard_map/ppermute | solution.py:272
  20.5 1.5 %collective-permute-start.6 = (bf16[416,256]{1,0:T(8,128)(2,1)S(1)}, bf16[416,256]{1,0:T(8,128)(2,1)S(1)}, u32[]{:S(2)}, u32[]{:S(2)}) collective-permute-start(bf16[416,256]{1,0:T(8,128)(2,1)S(1)} %collective-permute-done.4.block_ref), channel_id=1, source_target_pairs={{0,1},{1,0},{2,3},{3,2},{4,5},{5,4},{6,7},{7,6},{8,9},{9,8},{10,11... | collective-permute-start | bytes 638984 | tf_op jit(solution)/shard_map/ppermute | solution.py:272

commit v8 on v7

--- a/solution.py
+++ b/solution.py
@@ -14,6 +14,7 @@
 PANEL_COST = 10**9
 CHAIN_COST = 3 * 10**9
 PRIOR_COST = 10**9
+BLOCK_COST = 10**9
 LAST_COST = 10**8
 LEVEL_COST = 2 * 10**9
 
@@ -65,47 +66,42 @@
 
 
 def ready_kernel(
-    order_ref, held_ref, own_hbm, cross_hbm, rows_hbm, part_ref, fold_ref, own_ref, cross_ref, rows_ref, sems
+    order_ref, held_ref, own_hbm, cross_hbm, rows_hbm, write_hbm, source_hbm, inverse_hbm,
+    part_ref, fold_ref, own_ref, cross_ref, rows_ref, left_ref, inverse_ref, sems,
 ):
-    copies = [
-        pltpu.make_async_copy(own_hbm, own_ref, sems.at[0]),
-        pltpu.make_async_copy(cross_hbm, cross_ref, sems.at[1]),
-        pltpu.make_async_copy(rows_hbm, rows_ref, sems.at[2]),
+    rank, size = write_hbm.shape
+    pairs = [
+        (own_hbm, own_ref),
+        (cross_hbm, cross_ref),
+        (rows_hbm, rows_ref),
+        (write_hbm, left_ref.at[:rank]),
+        (source_hbm, left_ref.at[rank:]),
     ]
+    for start in range(0, size, rank):
+        block = (pl.ds(start, rank), pl.ds(0, start + rank))
+        pairs.append((inverse_hbm.at[block], inverse_ref.at[block]))
+    copies = [pltpu.make_async_copy(a, b, sems.at[i]) for i, (a, b) in enumerate(pairs)]
     for copy in copies:
         copy.start()
     pick = picker(order_ref[1], held_ref.shape[1])
-    for copy in copies:
+    for copy in copies[:2]:
         copy.wait()
     part_ref[...] = dot(held_ref[...], fold(own_ref[0], pick))
     fold_ref[...] = fold(cross_ref[0], pick)
+    for copy in copies[2:]:
+        copy.wait()
 
 
 def panel_kernel(
-    level, order_ref, held_ref, own_ref, cross_ref, write_hbm, inverse_hbm, source_hbm,
-    part_ref, fold_ref, gain_ref, base_ref, left, inverse, sems,
+    level, order_ref, held_ref, own_ref, cross_ref, left_ref, inverse_ref, part_ref, fold_ref, gain_ref, base_ref
 ):
     rank, size = gain_ref.shape
-    part = rank
-    copies = [
-        pltpu.make_async_copy(write_hbm, left.at[:rank], sems.at[0]),
-        pltpu.make_async_copy(source_hbm, left.at[rank:], sems.at[1]),
-    ]
-    for start in range(0, size, part):
-        block = (pl.ds(start, part), pl.ds(0, start + part))
-        copies.append(
-            pltpu.make_async_copy(inverse_hbm.at[block], inverse.at[block], sems.at[2 + start // part])
-        )
-    for copy in copies:
-        copy.start()
     pick = picker(order_ref[level + 1], held_ref.shape[1])
     part_ref[...] = dot(held_ref[...], fold(own_ref[level], pick))
     fold_ref[...] = fold(cross_ref[level], pick)
-    for copy in copies:
-        copy.wait()
-    for start in range(0, size, part):
-        cut = slice(start, start + part)
-        product = dot(left[:, start:], inverse[start:, cut])
+    for start in range(0, size, rank):
+        cut = slice(start, start + rank)
+        product = dot(left_ref[:, start:], inverse_ref[start:, cut])
         gain_ref[:, cut] = product[:rank].astype(BF16)
         base_ref[:, cut] = product[rank:]
 
@@ -189,7 +185,7 @@
 def gathered(wide, slabs):
     rows = slabs[0].shape[0]
     place = lax.axis_index("fr")
-    for flip, slab in enumerate(slabs):
+    for flip, slab in enumerate(reversed(slabs)):
         start = pl.multiple_of(jnp.bitwise_xor(place, flip) * rows, rows)
         wide[pl.ds(start, rows), :] = slab[...].astype(F32)
     return wide[...].astype(BF16)
@@ -237,7 +233,7 @@
 
 def whole_kernel(fixed_ref, reach_ref, gain_ref, slope_ref, prior_fixed_ref, prior_ref, *refs):
     *slabs, out_hbm, top_hbm, wide, held, sems, top_sem = refs
-    copy = pltpu.make_async_copy(slabs[0], top_hbm, top_sem)
+    copy = pltpu.make_async_copy(slabs[-1], top_hbm, top_sem)
     copy.start()
     top = gathered(wide, slabs)
     link = dot(top, reach_ref[...]).astype(BF16)
@@ -289,17 +285,21 @@
         coupling_read, order = lax.optimization_barrier((coupling_read, order))
     next_read = turned(coupling_read, -1)
     ready_outs = [((rows, top_rows), F32, True), ((top_rows, top_rows), BF16, True)]
-    part, folded, own, cross, parent_rows = kernel_call(
+    part, folded, own, cross, parent_rows, left, inverse = kernel_call(
         ready_kernel,
         [
             *ready_outs,
             (butterfly_own.shape, BF16, True),
             (butterfly_cross.shape, BF16, True),
             (parent_rows.shape, jnp.int32, True),
+            ((rank + vectors, panel), BF16, True),
+            (panel_inverse.shape, BF16, True),
         ],
-        [pltpu.SemaphoreType.DMA((3,))],
+        [pltpu.SemaphoreType.DMA((5 + panel // rank,))],
         [order, held],
-        remote=[butterfly_own, butterfly_cross, parent_rows],
+        remote=[
+            butterfly_own, butterfly_cross, parent_rows, coupling_write, front_source, panel_inverse
+        ],
     )
 
     def next_level(part, folded, swap):
@@ -312,31 +312,29 @@
     part, folded, gain, base = kernel_call(
         functools.partial(panel_kernel, 1),
         [*ready_outs, ((rank, panel), BF16, True), ((vectors, panel), F32, True)],
-        [
-            pltpu.VMEM((rank + vectors, panel), BF16),
-            pltpu.VMEM((panel, panel), BF16),
-            pltpu.SemaphoreType.DMA((2 + panel // rank,)),
-        ],
-        [order, held, own, cross],
+        [],
+        [order, held, own, cross, left, inverse],
         PANEL_COST,
-        [coupling_write, panel_inverse, front_source],
-    )
+    )
+
+    def products(next_read):
+        return kernel_call(
+            block_kernel,
+            [((vectors + rank + 2 * INDEX_ROWS, rank), BF16, True)],
+            [],
+            [gain, base, next_read, parent_rows],
+            BLOCK_COST,
+        )[0]
+
+    if chips <= 2:
+        block = products(next_read)
+        prior = flipped(block, 2)
+        swap, block = lax.optimization_barrier((swap, block))
     held = next_level(part, folded, swap)
-
+    swap = swapped(held, 4)
     if chips > 2:
-        swap = swapped(held, 4)
-    next_read, held = lax.optimization_barrier((next_read, held))
-    (block,) = kernel_call(
-        block_kernel,
-        [((vectors + rank + 2 * INDEX_ROWS, rank), BF16, True)],
-        [],
-        [gain, base, next_read, parent_rows],
-        2 * (vectors + rank) * panel * rank,
-    )
-    if chips <= 2:
-        block, held = lax.optimization_barrier((block, held))
-        prior = flipped(block, 2)
-        swap = swapped(held, 4)
+        next_read, held = lax.optimization_barrier((next_read, held))
+        block = products(next_read)
     other = flipped(block, 1)
     hop_outs = [
         ((vectors, rank), F32, True),
@@ -359,7 +357,7 @@
         [own, cross, held, swap],
         LEVEL_COST if chips > 2 else LAST_COST,
     )
-    slabs = [top] + [flipped(top, mask) for mask in range(1, chain)]
+    slabs = [flipped(top, mask) for mask in range(chain - 1, 0, -1)] + [top]
     wide = pltpu.VMEM((vectors, top_rows), F32)
     staging = [pltpu.VMEM((vectors, panel), BF16), pltpu.SemaphoreType.DMA((4,))]
     results = [((vectors, panel), BF16, False), ((rows, top_rows), BF16, False)]

time: 24.6 us -> 23.9 us (0.972)
  Pallas kernels: 8.31 us -> 7.07 us
  starting transfers between devices: 10.9 us -> 11.3 us
    pallas_call x10, Pallas kernels: 8.31 us -> 7.07 us  [kernel_call(): pl.pallas_call(kernel, out_shape=shapes, in_specs=[vmem] * len(placed) +...]
    ppermute x3, waiting for transfers between devices: 2.86 us -> 3.26 us  [swapped(): return lax.ppermute(array, 'bf', [(g, g ^ mask) for g in range(groups)])]
    ppermute x6, starting transfers between devices: 2.68 us -> 3.05 us  [flipped(): return lax.ppermute(array, 'fr', [(i, i ^ mask) for i in range(chain)])]
  transfers between devices with their start and end apart: 10 -> 10, of which waited for: 4 -> 5; matrix products, arithmetic and copies ran while one was open for 0% -> 0% of each run, Pallas kernels for 28% -> 25%
where the time goes in v8:
time: 23.9 us; the launch traced here: 23.7 us
  starting transfers between devices  11.3 us (47%)
  Pallas kernels  7.07 us (30%)
  waiting for transfers between devices  4.67 us (20%)
  between operations  0.71 us (3%)
    pallas_call x10, Pallas kernels, kernel_call(): pl.pallas_call(kernel, out_shape=shapes, in_specs=[vmem] * len(placed) +...  7.07 us
    ppermute x3, starting transfers between devices, swapped(): return lax.ppermute(array, 'bf', [(g, g ^ mask) for g in range(groups)])  5.76 us
    ppermute x3, waiting for transfers between devices, swapped(): return lax.ppermute(array, 'bf', [(g, g ^ mask) for g in range(groups)])  3.26 us
    ppermute x6, starting transfers between devices, flipped(): return lax.ppermute(array, 'fr', [(i, i ^ mask) for i in range(chain)])  3.05 us
    ppermute x1, starting transfers between devices, turned(): lax.ppermute(array, 'fr', [(i, (i + by) % chain) for i in range(chain)])  2.46 us
    ppermute x6, waiting for transfers between devices, flipped(): return lax.ppermute(array, 'fr', [(i, i ^ mask) for i in range(chain)])  1.41 us
  transfers between devices with their start and end apart: 10, of which 5 were waited for; matrix products, arithmetic and copies ran while one was open for 0% of the time, Pallas kernels for 25%

profile of v8, /device:TPU:0, one launch (start us, length us, event | category | flops | bytes accessed | tf_op | source)
XLA Modules:
  0.0 23.7 jit_solution(6229671728759377498)
XLA Ops:
  0.6 2.5 %collective-permute-start.2 = (bf16[1024,256]{1,0:T(8,128)(2,1)}, bf16[1024,256]{1,0:T(8,128)(2,1)S(1)}, u32[]{:S(2)}, u32[]{:S(2)}) collective-permute-start(bf16[1024,256]{1,0:T(8,128)(2,1)} %param.16), channel_id=1, source_target_pairs={{0,3},{1,0},{2,1},{3,2},{4,7},{5,4},{6,5},{7,6},{8,11},{9,8},{10,9... | collective-permute-start | bytes 1572872 | tf_op jit(solution)/shard_map/ppermute | solution.py:271
  3.1 1.0 %shard_map.104 = (bf16[32,512]{1,0:T(8,128)(2,1)S(1)}, s32[3,1,512]{2,1,0:T(1,128)S(1)}) custom-call(bf16[32,512]{1,0:T(8,128)(2,1)} %source_hbm.2, s32[3,1,512]{2,1,0:T(1,128)} %order_hbm.1), custom_call_target="tpu_custom_call" | custom-call | tf_op jit(solution)/shard_map/pallas_call | solution.py:37
  4.1 1.6 %collective-permute-start = (bf16[32,512]{1,0:T(8,128)(2,1)S(1)}, bf16[32,512]{1,0:T(8,128)(2,1)S(1)}, u32[]{:S(2)}, u32[]{:S(2)}) collective-permute-start(bf16[32,512]{1,0:T(8,128)(2,1)S(1)} %get-tuple-element.26.held_ref), channel_id=1, source_target_pairs={{0,4},{4,0},{8,12},{12,8},{16,20},{20,16},{24,28},{28,24},{1,5},{5... | collective-permute-start | bytes 98312 | tf_op jit(solution)/shard_map/ppermute | solution.py:274
  5.7 1.9 %shard_map.105 = (f32[32,512]{1,0:T(8,128)S(1)}, bf16[512,512]{1,0:T(8,128)(2,1)S(1)}, bf16[3,256,256]{2,1,0:T(8,128)(2,1)S(1)}, bf16[3,256,256]{2,1,0:T(8,128)(...) custom-call(s32[3,1,512]{2,1,0:T(1,128)S(1)} %get-tuple-element.25.order_ref, ...), custom_call_target="tpu_custom_call" | custom-call | tf_op jit(solution)/shard_map/pallas_call | solution.py:37
  7.5 0.6 %collective-permute-done.swap_ref = bf16[32,512]{1,0:T(8,128)(2,1)S(1)} collective-permute-done((bf16[32,512]{1,0:T(8,128)(2,1)S(1)}, bf16[32,512]{1,0:T(8,128)(2,1)S(1)}, u32[]{:S(2)}, u32[]{:S(2)}) %collective-permute-start) | collective-permute-done | bytes 32800 | tf_op jit(solution)/shard_map/ppermute | solution.py:274
  8.1 0.2 shard_map.106.held_ref
  8.3 1.6 %collective-permute-start.1 = (bf16[32,512]{1,0:T(8,128)(2,1)S(1)}, bf16[32,512]{1,0:T(8,128)(2,1)S(1)}, u32[]{:S(2)}, u32[]{:S(2)}) collective-permute-start(bf16[32,512]{1,0:T(8,128)(2,1)S(1)} %shard_map.106.held_ref), channel_id=1, source_target_pairs={{0,8},{4,12},{8,0},{12,4},{16,24},{20,28},{24,16},{28,20},{1,9},{5... | collective-permute-start | bytes 98312 | tf_op jit(solution)/shard_map/ppermute | solution.py:274
  9.9 1.2 %shard_map.107 = (f32[32,512]{1,0:T(8,128)S(1)}, bf16[512,512]{1,0:T(8,128)(2,1)S(1)}, bf16[256,1024]{1,0:T(8,128)(2,1)S(1)}, f32[128,1024]{1,0:T(8,128)S(1)}) custom-call(s32[3,1,512]{2,1,0:T(1,128)S(1)} %get-tuple-element.25.order_ref, bf16[32,512]{1,0:T(8,128)(2,1)S(1)} %shard_map.106.held_ref, bf16[3,256,256]{2,1,0:T(8,128)(2,1)S(1)} %get-tuple-element.29.own_ref, ...), custom_call_target="tpu_custom_call" | custom-call | flops 1000000000 | tf_op jit(solution)/shard_map/pallas_call | solution.py:37
  11.1 0.0 collective-permute-done.2.read_ref
  11.1 0.4 %shard_map.108.block_ref = bf16[416,256]{1,0:T(8,128)(2,1)S(1)} custom-call(bf16[256,1024]{1,0:T(8,128)(2,1)S(1)} %get-tuple-element.33.gain_ref, f32[128,1024]{1,0:T(8,128)S(1)} %get-tuple-element.34.base_ref, bf16[1024,256]{1,0:T(8,128)(2,1)S(1)} %collective-permute-done.2.read_ref, s32[1,256]{1,0:T(1,128)S(1)} %get-tuple-element.35.rows_ref), custom_call_target="tpu_custom_call" | custom-call | flops 1000000000 | tf_op jit(solution)/shard_map/pallas_call | solution.py:37
  11.5 0.6 %collective-permute-start.4 = (bf16[416,256]{1,0:T(8,128)(2,1)S(1)}, bf16[416,256]{1,0:T(8,128)(2,1)S(1)}, u32[]{:S(2)}, u32[]{:S(2)}) collective-permute-start(bf16[416,256]{1,0:T(8,128)(2,1)S(1)} %shard_map.108.block_ref), channel_id=1, source_target_pairs={{0,2},{1,3},{2,0},{3,1},{4,6},{5,7},{6,4},{7,5},{8,10},{9,11},{10,... | collective-permute-start | bytes 638984 | tf_op jit(solution)/shard_map/ppermute | solution.py:268
  12.1 0.1 collective-permute-done.1.swap_ref
  12.2 0.5 %collective-permute-start.3 = (bf16[416,256]{1,0:T(8,128)(2,1)S(1)}, bf16[416,256]{1,0:T(8,128)(2,1)S(1)}, u32[]{:S(2)}, u32[]{:S(2)}) collective-permute-start(bf16[416,256]{1,0:T(8,128)(2,1)S(1)} %shard_map.108.block_ref), channel_id=1, source_target_pairs={{0,1},{1,0},{2,3},{3,2},{4,5},{5,4},{6,7},{7,6},{8,9},{9,8},{10,11... | collective-permute-start | bytes 638984 | tf_op jit(solution)/shard_map/ppermute | solution.py:268
  12.8 0.2 shard_map.110.held_ref
  13.0 2.6 %collective-permute-start.5 = (bf16[32,512]{1,0:T(8,128)(2,1)S(1)}, bf16[32,512]{1,0:T(8,128)(2,1)S(1)}, u32[]{:S(2)}, u32[]{:S(2)}) collective-permute-start(bf16[32,512]{1,0:T(8,128)(2,1)S(1)} %shard_map.110.held_ref), channel_id=1, source_target_pairs={{0,16},{4,20},{8,24},{12,28},{16,0},{20,4},{24,8},{28,12},{1,17},{... | collective-permute-start | bytes 98312 | tf_op jit(solution)/shard_map/ppermute | solution.py:274
  15.6 2.6 %collective-permute-done.5.swap_ref = bf16[32,512]{1,0:T(8,128)(2,1)S(1)} collective-permute-done((bf16[32,512]{1,0:T(8,128)(2,1)S(1)}, bf16[32,512]{1,0:T(8,128)(2,1)S(1)}, u32[]{:S(2)}, u32[]{:S(2)}) %collective-permute-start.5) | collective-permute-done | bytes 32800 | tf_op jit(solution)/shard_map/ppermute | solution.py:274
  18.1 0.2 shard_map.111.refs_3_
  18.3 0.0 collective-permute-start.7
  18.3 1.1 %collective-permute-start.8 = (bf16[32,512]{1,0:T(8,128)(2,1)S(1)}, bf16[32,512]{1,0:T(8,128)(2,1)S(1)}, u32[]{:S(2)}, u32[]{:S(2)}) collective-permute-start(bf16[32,512]{1,0:T(8,128)(2,1)S(1)} %shard_map.111.refs_3_), channel_id=1, source_target_pairs={{0,2},{1,3},{2,0},{3,1},{4,6},{5,7},{6,4},{7,5},{8,10},{9,11},{10,... | collective-permute-start | bytes 98312 | tf_op jit(solution)/shard_map/ppermute | solution.py:268
  19.4 0.8 %collective-permute-start.9 = (bf16[32,512]{1,0:T(8,128)(2,1)S(1)}, bf16[32,512]{1,0:T(8,128)(2,1)S(1)}, u32[]{:S(2)}, u32[]{:S(2)}) collective-permute-start(bf16[32,512]{1,0:T(8,128)(2,1)S(1)} %shard_map.111.refs_3_), channel_id=1, source_target_pairs={{0,1},{1,0},{2,3},{3,2},{4,5},{5,4},{6,7},{7,6},{8,9},{9,8},{10,11... | collective-permute-start | bytes 98312 | tf_op jit(solution)/shard_map/ppermute | solution.py:268
  20.2 0.0 collective-permute-done.4.block_ref
  20.2 0.0 collective-permute-start.6
  20.2 0.0 collective-permute-done.3.other_ref
  20.2 0.5 %shard_map.109 = (f32[128,1024]{1,0:T(8,128)S(1)}, bf16[512,256]{1,0:T(8,128)(2,1)S(1)}, bf16[256,1024]{1,0:T(8,128)(2,1)S(1)}) custom-call(bf16[256,1024]{1,0:T(8,128)(2,1)S(1)} %get-tuple-element.33.gain_ref, f32[128,1024]{1,0:T(8,128)S(1)} %get-tuple-element.34.base_ref, bf16[416,256]{1,0:T(8,128)(2,1)S(1)} %shard_map.108.block_ref, ...), custom_call_target="tpu_custom_call" | custom-call | flops 3000000000 | tf_op jit(solution)/shard_map/pallas_call | solution.py:37
  20.7 1.0 %collective-permute-done.6.other_ref = bf16[416,256]{1,0:T(8,128)(2,1)S(1)} collective-permute-done((bf16[416,256]{1,0:T(8,128)(2,1)S(1)}, bf16[416,256]{1,0:T(8,128)(2,1)S(1)}, u32[]{:S(2)}, u32[]{:S(2)}) %collective-permute-start.6) | collective-permute-done | bytes 213024 | tf_op jit(solution)/shard_map/ppermute | solution.py:268
  21.7 0.4 %shard_map.112 = (f32[128,256]{1,0:T(8,128)S(1)}, bf16[512,256]{1,0:T(8,128)(2,1)S(1)}) custom-call(bf16[416,256]{1,0:T(8,128)(2,1)S(1)} %collective-permute-done.4.block_ref, bf16[416,256]{1,0:T(8,128)(2,1)S(1)} %collective-permute-done.6.other_ref), custom_call_target="tpu_custom_call" | custom-call | flops 1000000000 | tf_op jit(solution)/shard_map/pallas_call | solution.py:37
  22.1 0.0 collective-permute-done.7.refs_0_
  22.1 0.4 %collective-permute-done.8.refs_1_ = bf16[32,512]{1,0:T(8,128)(2,1)S(1)} collective-permute-done((bf16[32,512]{1,0:T(8,128)(2,1)S(1)}, bf16[32,512]{1,0:T(8,128)(2,1)S(1)}, u32[]{:S(2)}, u32[]{:S(2)}) %collective-permute-start.8) | collective-permute-done | bytes 32800 | tf_op jit(solution)/shard_map/ppermute | solution.py:268
  22.5 0.0 collective-permute-done.9.refs_2_
  22.5 1.2 %shard_map.113 = (bf16[128,1024]{1,0:T(8,128)(2,1)}, bf16[32,512]{1,0:T(8,128)(2,1)}) custom-call(f32[128,1024]{1,0:T(8,128)S(1)} %get-tuple-element.37.fixed_ref, bf16[512,256]{1,0:T(8,128)(2,1)S(1)} %get-tuple-element.38.reach_ref, bf16[256,1024]{1,0:T(8,128)(2,1)S(1)} %get-tuple-element.33.gain_ref, bf16[256,1024]{1,0:T(8,128)(2,1)S(1)} %get-tuple-element.39.slope_ref, ...), custom_call_target="tpu_custom_call" | custom-call | tf_op jit(solution)/shard_map/pallas_call | solution.py:37
Async XLA Ops:
  0.6 10.4 %collective-permute-start.2 = (bf16[1024,256]{1,0:T(8,128)(2,1)}, bf16[1024,256]{1,0:T(8,128)(2,1)S(1)}, u32[]{:S(2)}, u32[]{:S(2)}) collective-permute-start(bf16[1024,256]{1,0:T(8,128)(2,1)} %param.16), channel_id=1, source_target_pairs={{0,3},{1,0},{2,1},{3,2},{4,7},{5,4},{6,5},{7,6},{8,11},{9,8},{10,9... | collective-permute-start | bytes 1572872 | tf_op jit(solution)/shard_map/ppermute | solution.py:271
  4.1 4.0 %collective-permute-start = (bf16[32,512]{1,0:T(8,128)(2,1)S(1)}, bf16[32,512]{1,0:T(8,128)(2,1)S(1)}, u32[]{:S(2)}, u32[]{:S(2)}) collective-permute-start(bf16[32,512]{1,0:T(8,128)(2,1)S(1)} %get-tuple-element.26.held_ref), channel_id=1, source_target_pairs={{0,4},{4,0},{8,12},{12,8},{16,20},{20,16},{24,28},{28,24},{1,5},{5... | collective-permute-start | bytes 98312 | tf_op jit(solution)/shard_map/ppermute | solution.py:274
  8.3 3.9 %collective-permute-start.1 = (bf16[32,512]{1,0:T(8,128)(2,1)S(1)}, bf16[32,512]{1,0:T(8,128)(2,1)S(1)}, u32[]{:S(2)}, u32[]{:S(2)}) collective-permute-start(bf16[32,512]{1,0:T(8,128)(2,1)S(1)} %shard_map.106.held_ref), channel_id=1, source_target_pairs={{0,8},{4,12},{8,0},{12,4},{16,24},{20,28},{24,16},{28,20},{1,9},{5... | collective-permute-start | bytes 98312 | tf_op jit(solution)/shard_map/ppermute | solution.py:274
  11.5 8.7 %collective-permute-start.4 = (bf16[416,256]{1,0:T(8,128)(2,1)S(1)}, bf16[416,256]{1,0:T(8,128)(2,1)S(1)}, u32[]{:S(2)}, u32[]{:S(2)}) collective-permute-start(bf16[416,256]{1,0:T(8,128)(2,1)S(1)} %shard_map.108.block_ref), channel_id=1, source_target_pairs={{0,2},{1,3},{2,0},{3,1},{4,6},{5,7},{6,4},{7,5},{8,10},{9,11},{10,... | collective-permute-start | bytes 638984 | tf_op jit(solution)/shard_map/ppermute | solution.py:268
  12.2 8.0 %collective-permute-start.3 = (bf16[416,256]{1,0:T(8,128)(2,1)S(1)}, bf16[416,256]{1,0:T(8,128)(2,1)S(1)}, u32[]{:S(2)}, u32[]{:S(2)}) collective-permute-start(bf16[416,256]{1,0:T(8,128)(2,1)S(1)} %shard_map.108.block_ref), channel_id=1, source_target_pairs={{0,1},{1,0},{2,3},{3,2},{4,5},{5,4},{6,7},{7,6},{8,9},{9,8},{10,11... | collective-permute-start | bytes 638984 | tf_op jit(solution)/shard_map/ppermute | solution.py:268
  13.0 5.2 %collective-permute-start.5 = (bf16[32,512]{1,0:T(8,128)(2,1)S(1)}, bf16[32,512]{1,0:T(8,128)(2,1)S(1)}, u32[]{:S(2)}, u32[]{:S(2)}) collective-permute-start(bf16[32,512]{1,0:T(8,128)(2,1)S(1)} %shard_map.110.held_ref), channel_id=1, source_target_pairs={{0,16},{4,20},{8,24},{12,28},{16,0},{20,4},{24,8},{28,12},{1,17},{... | collective-permute-start | bytes 98312 | tf_op jit(solution)/shard_map/ppermute | solution.py:274
  18.3 3.8 %collective-permute-start.7 = (bf16[32,512]{1,0:T(8,128)(2,1)S(1)}, bf16[32,512]{1,0:T(8,128)(2,1)S(1)}, u32[]{:S(2)}, u32[]{:S(2)}) collective-permute-start(bf16[32,512]{1,0:T(8,128)(2,1)S(1)} %shard_map.111.refs_3_), channel_id=1, source_target_pairs={{0,3},{1,2},{2,1},{3,0},{4,7},{5,6},{6,5},{7,4},{8,11},{9,10},{10,... | collective-permute-start | bytes 98312 | tf_op jit(solution)/shard_map/ppermute | solution.py:268
  18.3 4.2 %collective-permute-start.8 = (bf16[32,512]{1,0:T(8,128)(2,1)S(1)}, bf16[32,512]{1,0:T(8,128)(2,1)S(1)}, u32[]{:S(2)}, u32[]{:S(2)}) collective-permute-start(bf16[32,512]{1,0:T(8,128)(2,1)S(1)} %shard_map.111.refs_3_), channel_id=1, source_target_pairs={{0,2},{1,3},{2,0},{3,1},{4,6},{5,7},{6,4},{7,5},{8,10},{9,11},{10,... | collective-permute-start | bytes 98312 | tf_op jit(solution)/shard_map/ppermute | solution.py:268
  19.4 3.1 %collective-permute-start.9 = (bf16[32,512]{1,0:T(8,128)(2,1)S(1)}, bf16[32,512]{1,0:T(8,128)(2,1)S(1)}, u32[]{:S(2)}, u32[]{:S(2)}) collective-permute-start(bf16[32,512]{1,0:T(8,128)(2,1)S(1)} %shard_map.111.refs_3_), channel_id=1, source_target_pairs={{0,1},{1,0},{2,3},{3,2},{4,5},{5,4},{6,7},{7,6},{8,9},{9,8},{10,11... | collective-permute-start | bytes 98312 | tf_op jit(solution)/shard_map/ppermute | solution.py:268
  20.2 1.5 %collective-permute-start.6 = (bf16[416,256]{1,0:T(8,128)(2,1)S(1)}, bf16[416,256]{1,0:T(8,128)(2,1)S(1)}, u32[]{:S(2)}, u32[]{:S(2)}) collective-permute-start(bf16[416,256]{1,0:T(8,128)(2,1)S(1)} %collective-permute-done.4.block_ref), channel_id=1, source_target_pairs={{0,1},{1,0},{2,3},{3,2},{4,5},{5,4},{6,7},{7,6},{8,9},{9,8},{10,11... | collective-permute-start | bytes 638984 | tf_op jit(solution)/shard_map/ppermute | solution.py:268

commit v9 on v8

--- a/solution.py
+++ b/solution.py
@@ -67,7 +67,7 @@
 
 def ready_kernel(
     order_ref, held_ref, own_hbm, cross_hbm, rows_hbm, write_hbm, source_hbm, inverse_hbm,
-    part_ref, fold_ref, own_ref, cross_ref, rows_ref, left_ref, inverse_ref, sems,
+    part_ref, fold_ref, next_own_ref, next_fold_ref, own_ref, cross_ref, rows_ref, left_ref, inverse_ref, sems,
 ):
     rank, size = write_hbm.shape
     pairs = [
@@ -88,17 +88,16 @@
         copy.wait()
     part_ref[...] = dot(held_ref[...], fold(own_ref[0], pick))
     fold_ref[...] = fold(cross_ref[0], pick)
+    pick = picker(order_ref[2], held_ref.shape[1])
+    next_own_ref[...] = fold(own_ref[1], pick)
+    next_fold_ref[...] = fold(cross_ref[1], pick)
     for copy in copies[2:]:
         copy.wait()
 
 
-def panel_kernel(
-    level, order_ref, held_ref, own_ref, cross_ref, left_ref, inverse_ref, part_ref, fold_ref, gain_ref, base_ref
-):
+def panel_kernel(held_ref, fold_ref, left_ref, inverse_ref, part_ref, gain_ref, base_ref):
     rank, size = gain_ref.shape
-    pick = picker(order_ref[level + 1], held_ref.shape[1])
-    part_ref[...] = dot(held_ref[...], fold(own_ref[level], pick))
-    fold_ref[...] = fold(cross_ref[level], pick)
+    part_ref[...] = dot(held_ref[...], fold_ref[...])
     for start in range(0, size, rank):
         cut = slice(start, start + rank)
         product = dot(left_ref[:, start:], inverse_ref[start:, cut])
@@ -285,10 +284,12 @@
         coupling_read, order = lax.optimization_barrier((coupling_read, order))
     next_read = turned(coupling_read, -1)
     ready_outs = [((rows, top_rows), F32, True), ((top_rows, top_rows), BF16, True)]
-    part, folded, own, cross, parent_rows, left, inverse = kernel_call(
+    part, folded, next_own, next_folded, own, cross, parent_rows, left, inverse = kernel_call(
         ready_kernel,
         [
             *ready_outs,
+            ready_outs[1],
+            ready_outs[1],
             (butterfly_own.shape, BF16, True),
             (butterfly_cross.shape, BF16, True),
             (parent_rows.shape, jnp.int32, True),
@@ -309,11 +310,11 @@
 
     held = next_level(part, folded, swap)
     swap = swapped(held, 2)
-    part, folded, gain, base = kernel_call(
-        functools.partial(panel_kernel, 1),
-        [*ready_outs, ((rank, panel), BF16, True), ((vectors, panel), F32, True)],
+    part, gain, base = kernel_call(
+        panel_kernel,
+        [ready_outs[0], ((rank, panel), BF16, True), ((vectors, panel), F32, True)],
         [],
-        [order, held, own, cross, left, inverse],
+        [held, next_own, left, inverse],
         PANEL_COST,
     )
 
@@ -328,14 +329,15 @@
 
     if chips <= 2:
         block = products(next_read)
-        prior = flipped(block, 2)
+        prior, other = flipped(block, 2), flipped(block, 1)
         swap, block = lax.optimization_barrier((swap, block))
-    held = next_level(part, folded, swap)
+    held = next_level(part, next_folded, swap)
     swap = swapped(held, 4)
     if chips > 2:
         next_read, held = lax.optimization_barrier((next_read, held))
         block = products(next_read)
-    other = flipped(block, 1)
+    if chips > 2:
+        other = flipped(block, 1)
     hop_outs = [
         ((vectors, rank), F32, True),
         ((top_rows, rank), BF16, True),

time: 23.9 us -> 23.8 us (level)
  waiting for transfers between devices: 4.67 us -> 4.1 us
  starting transfers between devices: 11.3 us -> 11.8 us
    ppermute x6, starting transfers between devices: 3.05 us -> 3.58 us  [flipped(): return lax.ppermute(array, 'fr', [(i, i ^ mask) for i in range(chain)])]
    ppermute x3, waiting for transfers between devices: 3.26 us -> 2.84 us  [swapped(): return lax.ppermute(array, 'bf', [(g, g ^ mask) for g in range(groups)])]
  transfers between devices with their start and end apart: 10 -> 10, of which waited for: 5 -> 4; matrix products, arithmetic and copies ran while one was open for 0% -> 0% of each run, Pallas kernels for 25% -> 24%
where the time goes in v9:
time: 23.8 us; the launch traced here: 23.6 us
  starting transfers between devices  11.8 us (50%)
  Pallas kernels  6.96 us (29%)
  waiting for transfers between devices  4.1 us (17%)
  between operations  0.71 us (3%)
    pallas_call x10, Pallas kernels, kernel_call(): pl.pallas_call(kernel, out_shape=shapes, in_specs=[vmem] * len(placed) +...  6.96 us
    ppermute x3, starting transfers between devices, swapped(): return lax.ppermute(array, 'bf', [(g, g ^ mask) for g in range(groups)])  5.76 us
    ppermute x6, starting transfers between devices, flipped(): return lax.ppermute(array, 'fr', [(i, i ^ mask) for i in range(chain)])  3.58 us
    ppermute x3, waiting for transfers between devices, swapped(): return lax.ppermute(array, 'bf', [(g, g ^ mask) for g in range(groups)])  2.84 us
    ppermute x1, starting transfers between devices, turned(): lax.ppermute(array, 'fr', [(i, (i + by) % chain) for i in range(chain)])  2.46 us
    ppermute x6, waiting for transfers between devices, flipped(): return lax.ppermute(array, 'fr', [(i, i ^ mask) for i in range(chain)])  1.25 us
  transfers between devices with their start and end apart: 10, of which 4 were waited for; matrix products, arithmetic and copies ran while one was open for 0% of the time, Pallas kernels for 24%

profile of v9, /device:TPU:0, one launch (start us, length us, event | category | flops | bytes accessed | tf_op | source)
XLA Modules:
  0.0 23.6 jit_solution(3097289351556312047)
XLA Ops:
  0.6 2.5 %collective-permute-start.2 = (bf16[1024,256]{1,0:T(8,128)(2,1)}, bf16[1024,256]{1,0:T(8,128)(2,1)S(1)}, u32[]{:S(2)}, u32[]{:S(2)}) collective-permute-start(bf16[1024,256]{1,0:T(8,128)(2,1)} %param.16), channel_id=1, source_target_pairs={{0,3},{1,0},{2,1},{3,2},{4,7},{5,4},{6,5},{7,6},{8,11},{9,8},{10,9... | collective-permute-start | bytes 1572872 | tf_op jit(solution)/shard_map/ppermute | solution.py:270
  3.1 1.0 %shard_map.104 = (bf16[32,512]{1,0:T(8,128)(2,1)S(1)}, s32[3,1,512]{2,1,0:T(1,128)S(1)}) custom-call(bf16[32,512]{1,0:T(8,128)(2,1)} %source_hbm.2, s32[3,1,512]{2,1,0:T(1,128)} %order_hbm.1), custom_call_target="tpu_custom_call" | custom-call | tf_op jit(solution)/shard_map/pallas_call | solution.py:37
  4.1 1.6 %collective-permute-start = (bf16[32,512]{1,0:T(8,128)(2,1)S(1)}, bf16[32,512]{1,0:T(8,128)(2,1)S(1)}, u32[]{:S(2)}, u32[]{:S(2)}) collective-permute-start(bf16[32,512]{1,0:T(8,128)(2,1)S(1)} %get-tuple-element.27.held_ref), channel_id=1, source_target_pairs={{0,4},{4,0},{8,12},{12,8},{16,20},{20,16},{24,28},{28,24},{1,5},{5... | collective-permute-start | bytes 98312 | tf_op jit(solution)/shard_map/ppermute | solution.py:273
  5.7 2.2 %shard_map.105 = (f32[32,512]{1,0:T(8,128)S(1)}, bf16[512,512]{1,0:T(8,128)(2,1)S(1)}, bf16[512,512]{1,0:T(8,128)(2,1)S(1)}, bf16[512,512]{1,0:T(8,128)(2,1)S(1)...) custom-call(s32[3,1,512]{2,1,0:T(1,128)S(1)} %get-tuple-element.26.o, ...), custom_call_target="tpu_custom_call" | custom-call | tf_op jit(solution)/shard_map/pallas_call | solution.py:37
  7.9 0.3 %collective-permute-done.swap_ref = bf16[32,512]{1,0:T(8,128)(2,1)S(1)} collective-permute-done((bf16[32,512]{1,0:T(8,128)(2,1)S(1)}, bf16[32,512]{1,0:T(8,128)(2,1)S(1)}, u32[]{:S(2)}, u32[]{:S(2)}) %collective-permute-start) | collective-permute-done | bytes 32800 | tf_op jit(solution)/shard_map/ppermute | solution.py:273
  8.1 0.2 shard_map.106.held_ref
  8.3 1.6 %collective-permute-start.1 = (bf16[32,512]{1,0:T(8,128)(2,1)S(1)}, bf16[32,512]{1,0:T(8,128)(2,1)S(1)}, u32[]{:S(2)}, u32[]{:S(2)}) collective-permute-start(bf16[32,512]{1,0:T(8,128)(2,1)S(1)} %shard_map.106.held_ref), channel_id=1, source_target_pairs={{0,8},{4,12},{8,0},{12,4},{16,24},{20,28},{24,16},{28,20},{1,9},{5... | collective-permute-start | bytes 98312 | tf_op jit(solution)/shard_map/ppermute | solution.py:273
  9.9 0.8 %shard_map.107 = (f32[32,512]{1,0:T(8,128)S(1)}, bf16[256,1024]{1,0:T(8,128)(2,1)S(1)}, f32[128,1024]{1,0:T(8,128)S(1)}) custom-call(bf16[32,512]{1,0:T(8,128)(2,1)S(1)} %shard_map.106.held_ref, bf16[512,512]{1,0:T(8,128)(2,1)S(1)} %get-tuple-element.30.fold_ref, bf16[384,1024]{1,0:T(8,128)(2,1)S(1)} %get-tuple-element.31.left_ref, ...), custom_call_target="tpu_custom_call" | custom-call | flops 1000000000 | tf_op jit(solution)/shard_map/pallas_call | solution.py:37
  10.7 0.0 collective-permute-done.2.read_ref
  10.7 0.4 %shard_map.108.block_ref = bf16[416,256]{1,0:T(8,128)(2,1)S(1)} custom-call(bf16[256,1024]{1,0:T(8,128)(2,1)S(1)} %get-tuple-element.33.gain_ref, f32[128,1024]{1,0:T(8,128)S(1)} %get-tuple-element.34.base_ref, bf16[1024,256]{1,0:T(8,128)(2,1)S(1)} %collective-permute-done.2.read_ref, s32[1,256]{1,0:T(1,128)S(1)} %get-tuple-element.35.rows_ref), custom_call_target="tpu_custom_call" | custom-call | flops 1000000000 | tf_op jit(solution)/shard_map/pallas_call | solution.py:37
  11.1 0.6 %collective-permute-start.4 = (bf16[416,256]{1,0:T(8,128)(2,1)S(1)}, bf16[416,256]{1,0:T(8,128)(2,1)S(1)}, u32[]{:S(2)}, u32[]{:S(2)}) collective-permute-start(bf16[416,256]{1,0:T(8,128)(2,1)S(1)} %shard_map.108.block_ref), channel_id=1, source_target_pairs={{0,2},{1,3},{2,0},{3,1},{4,6},{5,7},{6,4},{7,5},{8,10},{9,11},{10,... | collective-permute-start | bytes 638984 | tf_op jit(solution)/shard_map/ppermute | solution.py:267
  11.7 1.1 %collective-permute-start.3 = (bf16[416,256]{1,0:T(8,128)(2,1)S(1)}, bf16[416,256]{1,0:T(8,128)(2,1)S(1)}, u32[]{:S(2)}, u32[]{:S(2)}) collective-permute-start(bf16[416,256]{1,0:T(8,128)(2,1)S(1)} %shard_map.108.block_ref), channel_id=1, source_target_pairs={{0,1},{1,0},{2,3},{3,2},{4,5},{5,4},{6,7},{7,6},{8,9},{9,8},{10,11... | collective-permute-start | bytes 638984 | tf_op jit(solution)/shard_map/ppermute | solution.py:267
  12.8 0.0 collective-permute-done.1.swap_ref
  12.8 0.2 shard_map.110.held_ref
  13.0 2.6 %collective-permute-start.5 = (bf16[32,512]{1,0:T(8,128)(2,1)S(1)}, bf16[32,512]{1,0:T(8,128)(2,1)S(1)}, u32[]{:S(2)}, u32[]{:S(2)}) collective-permute-start(bf16[32,512]{1,0:T(8,128)(2,1)S(1)} %shard_map.110.held_ref), channel_id=1, source_target_pairs={{0,16},{4,20},{8,24},{12,28},{16,0},{20,4},{24,8},{28,12},{1,17},{... | collective-permute-start | bytes 98312 | tf_op jit(solution)/shard_map/ppermute | solution.py:273
  15.6 2.6 %collective-permute-done.5.swap_ref = bf16[32,512]{1,0:T(8,128)(2,1)S(1)} collective-permute-done((bf16[32,512]{1,0:T(8,128)(2,1)S(1)}, bf16[32,512]{1,0:T(8,128)(2,1)S(1)}, u32[]{:S(2)}, u32[]{:S(2)}) %collective-permute-start.5) | collective-permute-done | bytes 32800 | tf_op jit(solution)/shard_map/ppermute | solution.py:273
  18.1 0.2 shard_map.111.refs_3_
  18.3 0.0 collective-permute-start.7
  18.3 0.5 %collective-permute-start.8 = (bf16[32,512]{1,0:T(8,128)(2,1)S(1)}, bf16[32,512]{1,0:T(8,128)(2,1)S(1)}, u32[]{:S(2)}, u32[]{:S(2)}) collective-permute-start(bf16[32,512]{1,0:T(8,128)(2,1)S(1)} %shard_map.111.refs_3_), channel_id=1, source_target_pairs={{0,2},{1,3},{2,0},{3,1},{4,6},{5,7},{6,4},{7,5},{8,10},{9,11},{10,... | collective-permute-start | bytes 98312 | tf_op jit(solution)/shard_map/ppermute | solution.py:267
  18.8 1.4 %collective-permute-start.9 = (bf16[32,512]{1,0:T(8,128)(2,1)S(1)}, bf16[32,512]{1,0:T(8,128)(2,1)S(1)}, u32[]{:S(2)}, u32[]{:S(2)}) collective-permute-start(bf16[32,512]{1,0:T(8,128)(2,1)S(1)} %shard_map.111.refs_3_), channel_id=1, source_target_pairs={{0,1},{1,0},{2,3},{3,2},{4,5},{5,4},{6,7},{7,6},{8,9},{9,8},{10,11... | collective-permute-start | bytes 98312 | tf_op jit(solution)/shard_map/ppermute | solution.py:267
  20.2 0.0 collective-permute-done.4.block_ref
  20.2 0.0 collective-permute-start.6
  20.2 0.0 collective-permute-done.3.other_ref
  20.2 0.5 %shard_map.109 = (f32[128,1024]{1,0:T(8,128)S(1)}, bf16[512,256]{1,0:T(8,128)(2,1)S(1)}, bf16[256,1024]{1,0:T(8,128)(2,1)S(1)}) custom-call(bf16[256,1024]{1,0:T(8,128)(2,1)S(1)} %get-tuple-element.33.gain_ref, f32[128,1024]{1,0:T(8,128)S(1)} %get-tuple-element.34.base_ref, bf16[416,256]{1,0:T(8,128)(2,1)S(1)} %shard_map.108.block_ref, ...), custom_call_target="tpu_custom_call" | custom-call | flops 3000000000 | tf_op jit(solution)/shard_map/pallas_call | solution.py:37
  20.7 1.0 %collective-permute-done.6.other_ref = bf16[416,256]{1,0:T(8,128)(2,1)S(1)} collective-permute-done((bf16[416,256]{1,0:T(8,128)(2,1)S(1)}, bf16[416,256]{1,0:T(8,128)(2,1)S(1)}, u32[]{:S(2)}, u32[]{:S(2)}) %collective-permute-start.6) | collective-permute-done | bytes 213024 | tf_op jit(solution)/shard_map/ppermute | solution.py:267
  21.7 0.4 %shard_map.112 = (f32[128,256]{1,0:T(8,128)S(1)}, bf16[512,256]{1,0:T(8,128)(2,1)S(1)}) custom-call(bf16[416,256]{1,0:T(8,128)(2,1)S(1)} %collective-permute-done.4.block_ref, bf16[416,256]{1,0:T(8,128)(2,1)S(1)} %collective-permute-done.6.other_ref), custom_call_target="tpu_custom_call" | custom-call | flops 1000000000 | tf_op jit(solution)/shard_map/pallas_call | solution.py:37
  22.1 0.0 collective-permute-done.7.refs_0_
  22.1 0.3 %collective-permute-done.8.refs_1_ = bf16[32,512]{1,0:T(8,128)(2,1)S(1)} collective-permute-done((bf16[32,512]{1,0:T(8,128)(2,1)S(1)}, bf16[32,512]{1,0:T(8,128)(2,1)S(1)}, u32[]{:S(2)}, u32[]{:S(2)}) %collective-permute-start.8) | collective-permute-done | bytes 32800 | tf_op jit(solution)/shard_map/ppermute | solution.py:267
  22.4 0.0 collective-permute-done.9.refs_2_
  22.4 1.2 %shard_map.113 = (bf16[128,1024]{1,0:T(8,128)(2,1)}, bf16[32,512]{1,0:T(8,128)(2,1)}) custom-call(f32[128,1024]{1,0:T(8,128)S(1)} %get-tuple-element.37.fixed_ref, bf16[512,256]{1,0:T(8,128)(2,1)S(1)} %get-tuple-element.38.reach_ref, bf16[256,1024]{1,0:T(8,128)(2,1)S(1)} %get-tuple-element.33.gain_ref, bf16[256,1024]{1,0:T(8,128)(2,1)S(1)} %get-tuple-element.39.slope_ref, ...), custom_call_target="tpu_custom_call" | custom-call | tf_op jit(solution)/shard_map/pallas_call | solution.py:37
Async XLA Ops:
  0.6 10.0 %collective-permute-start.2 = (bf16[1024,256]{1,0:T(8,128)(2,1)}, bf16[1024,256]{1,0:T(8,128)(2,1)S(1)}, u32[]{:S(2)}, u32[]{:S(2)}) collective-permute-start(bf16[1024,256]{1,0:T(8,128)(2,1)} %param.16), channel_id=1, source_target_pairs={{0,3},{1,0},{2,1},{3,2},{4,7},{5,4},{6,5},{7,6},{8,11},{9,8},{10,9... | collective-permute-start | bytes 1572872 | tf_op jit(solution)/shard_map/ppermute | solution.py:270
  4.1 4.0 %collective-permute-start = (bf16[32,512]{1,0:T(8,128)(2,1)S(1)}, bf16[32,512]{1,0:T(8,128)(2,1)S(1)}, u32[]{:S(2)}, u32[]{:S(2)}) collective-permute-start(bf16[32,512]{1,0:T(8,128)(2,1)S(1)} %get-tuple-element.27.held_ref), channel_id=1, source_target_pairs={{0,4},{4,0},{8,12},{12,8},{16,20},{20,16},{24,28},{28,24},{1,5},{5... | collective-permute-start | bytes 98312 | tf_op jit(solution)/shard_map/ppermute | solution.py:273
  8.3 4.5 %collective-permute-start.1 = (bf16[32,512]{1,0:T(8,128)(2,1)S(1)}, bf16[32,512]{1,0:T(8,128)(2,1)S(1)}, u32[]{:S(2)}, u32[]{:S(2)}) collective-permute-start(bf16[32,512]{1,0:T(8,128)(2,1)S(1)} %shard_map.106.held_ref), channel_id=1, source_target_pairs={{0,8},{4,12},{8,0},{12,4},{16,24},{20,28},{24,16},{28,20},{1,9},{5... | collective-permute-start | bytes 98312 | tf_op jit(solution)/shard_map/ppermute | solution.py:273
  11.1 9.1 %collective-permute-start.4 = (bf16[416,256]{1,0:T(8,128)(2,1)S(1)}, bf16[416,256]{1,0:T(8,128)(2,1)S(1)}, u32[]{:S(2)}, u32[]{:S(2)}) collective-permute-start(bf16[416,256]{1,0:T(8,128)(2,1)S(1)} %shard_map.108.block_ref), channel_id=1, source_target_pairs={{0,2},{1,3},{2,0},{3,1},{4,6},{5,7},{6,4},{7,5},{8,10},{9,11},{10,... | collective-permute-start | bytes 638984 | tf_op jit(solution)/shard_map/ppermute | solution.py:267
  11.7 8.5 %collective-permute-start.3 = (bf16[416,256]{1,0:T(8,128)(2,1)S(1)}, bf16[416,256]{1,0:T(8,128)(2,1)S(1)}, u32[]{:S(2)}, u32[]{:S(2)}) collective-permute-start(bf16[416,256]{1,0:T(8,128)(2,1)S(1)} %shard_map.108.block_ref), channel_id=1, source_target_pairs={{0,1},{1,0},{2,3},{3,2},{4,5},{5,4},{6,7},{7,6},{8,9},{9,8},{10,11... | collective-permute-start | bytes 638984 | tf_op jit(solution)/shard_map/ppermute | solution.py:267
  13.0 5.2 %collective-permute-start.5 = (bf16[32,512]{1,0:T(8,128)(2,1)S(1)}, bf16[32,512]{1,0:T(8,128)(2,1)S(1)}, u32[]{:S(2)}, u32[]{:S(2)}) collective-permute-start(bf16[32,512]{1,0:T(8,128)(2,1)S(1)} %shard_map.110.held_ref), channel_id=1, source_target_pairs={{0,16},{4,20},{8,24},{12,28},{16,0},{20,4},{24,8},{28,12},{1,17},{... | collective-permute-start | bytes 98312 | tf_op jit(solution)/shard_map/ppermute | solution.py:273
  18.3 3.8 %collective-permute-start.7 = (bf16[32,512]{1,0:T(8,128)(2,1)S(1)}, bf16[32,512]{1,0:T(8,128)(2,1)S(1)}, u32[]{:S(2)}, u32[]{:S(2)}) collective-permute-start(bf16[32,512]{1,0:T(8,128)(2,1)S(1)} %shard_map.111.refs_3_), channel_id=1, source_target_pairs={{0,3},{1,2},{2,1},{3,0},{4,7},{5,6},{6,5},{7,4},{8,11},{9,10},{10,... | collective-permute-start | bytes 98312 | tf_op jit(solution)/shard_map/ppermute | solution.py:267
  18.3 4.0 %collective-permute-start.8 = (bf16[32,512]{1,0:T(8,128)(2,1)S(1)}, bf16[32,512]{1,0:T(8,128)(2,1)S(1)}, u32[]{:S(2)}, u32[]{:S(2)}) collective-permute-start(bf16[32,512]{1,0:T(8,128)(2,1)S(1)} %shard_map.111.refs_3_), channel_id=1, source_target_pairs={{0,2},{1,3},{2,0},{3,1},{4,6},{5,7},{6,4},{7,5},{8,10},{9,11},{10,... | collective-permute-start | bytes 98312 | tf_op jit(solution)/shard_map/ppermute | solution.py:267
  18.8 3.6 %collective-permute-start.9 = (bf16[32,512]{1,0:T(8,128)(2,1)S(1)}, bf16[32,512]{1,0:T(8,128)(2,1)S(1)}, u32[]{:S(2)}, u32[]{:S(2)}) collective-permute-start(bf16[32,512]{1,0:T(8,128)(2,1)S(1)} %shard_map.111.refs_3_), channel_id=1, source_target_pairs={{0,1},{1,0},{2,3},{3,2},{4,5},{5,4},{6,7},{7,6},{8,9},{9,8},{10,11... | collective-permute-start | bytes 98312 | tf_op jit(solution)/shard_map/ppermute | solution.py:267
  20.2 1.5 %collective-permute-start.6 = (bf16[416,256]{1,0:T(8,128)(2,1)S(1)}, bf16[416,256]{1,0:T(8,128)(2,1)S(1)}, u32[]{:S(2)}, u32[]{:S(2)}) collective-permute-start(bf16[416,256]{1,0:T(8,128)(2,1)S(1)} %collective-permute-done.4.block_ref), channel_id=1, source_target_pairs={{0,1},{1,0},{2,3},{3,2},{4,5},{5,4},{6,7},{7,6},{8,9},{9,8},{10,11... | collective-permute-start | bytes 638984 | tf_op jit(solution)/shard_map/ppermute | solution.py:267
